TPU v7x, 128 devices: a whole 4x4x4 slice. The times are simulated.
128 devices in a mesh: seq: 16 (over y, z_lo, core), fsdp: 8 (over x, z_hi).
Axes of the slice: x: 4, y: 4, z: 4 (z_hi: 2, z_lo: 2; z = z_hi * 2 + z_lo), core: 2. Of those that a mesh axis runs over, the one named last changes fastest.
Arguments:
- queries: bfloat16 [8, 3456, 2048], P('fsdp', 'seq'), may hold values from -5 to 5
- key_vectors: bfloat16 [8, 3456, 2048], P('fsdp', 'seq'), may hold values from -5 to 5
- values: bfloat16 [8, 3456, 2048], P('fsdp', 'seq'), may hold values from -5 to 5
- out_weight: bfloat16 [2048, 2048], P(('seq', 'fsdp')), may hold values from -0.125 to 0.125
- cotangent: bfloat16 [8, 3456, 2048], P('fsdp', 'seq'), may hold values from -0.59765625 to 0.59765625
- neighbours: int32 [18, 9], replicated, may hold values from 0 to 17, as said below
- tile_order: int32 [3456], replicated, may hold values from 0 to 3455, as said below
Outputs:
- projected: bfloat16 [8, 3456, 2048], P('fsdp', 'seq')
- grad_queries: bfloat16 [8, 3456, 2048], P('fsdp', 'seq')
- grad_keys: bfloat16 [8, 3456, 2048], P('fsdp', 'seq')
- grad_values: bfloat16 [8, 3456, 2048], P('fsdp', 'seq')
- grad_weight: bfloat16 [2048, 2048], P(('seq', 'fsdp'))
Inputs may be any that keep to these rules, and one draw needn't show every extreme that they name: `neighbours`: each row names 9 different tiles, the row's own tile among them. `tile_order`: a permutation of the 3456 token indices.
All inputs are finite; a program needn't handle non-finite values.
Results may differ from a plain program's by a relative error of at most 0.014.
Values may be sent and summed in bfloat16 or wider, within the bound.
No kernel may reach another device: no remote copies, remote signals or barrier semaphores. Data moves between devices by JAX's collectives and lax.ppermute only.
A program may use at most 128 MiB of HBM per device.

v0:
```python
import math

import jax
import jax.numpy as jnp
from jax import lax
from jax.sharding import PartitionSpec as P

HD = 128
HEADS = 16
TILE = 192
NB = 9


def pick_tiles(tile_rows, chosen):
    gathered = tile_rows[chosen]
    return gathered.reshape(
        chosen.shape[0], chosen.shape[1] * tile_rows.shape[1], tile_rows.shape[2]
    )


def head_forward(query_rows, key_rows, value_rows, tile_order, neighbours):
    count_tiles = neighbours.shape[0]
    head_width = query_rows.shape[1]
    score_scale = 1.0 / math.sqrt(head_width)
    query_tiles = query_rows[tile_order].reshape(count_tiles // 3, 3, TILE, head_width)
    key_tiles = key_rows[tile_order].reshape(count_tiles, TILE, head_width)
    value_tiles = value_rows[tile_order].reshape(count_tiles, TILE, head_width)
    chosen = neighbours.reshape(count_tiles // 3, 3, NB)

    def one_group(operands):
        query_block, pick_list = operands
        key_block = pick_tiles(key_tiles, pick_list)
        value_block = pick_tiles(value_tiles, pick_list)
        scores = (
            jnp.einsum("gqd,gkd->gqk", query_block, key_block, preferred_element_type=jnp.float32)
            * score_scale
        )
        row_max = jnp.max(scores, axis=-1, keepdims=True)
        row_sum = jnp.sum(jnp.exp(scores - row_max), axis=-1, keepdims=True)
        log_total = row_max + jnp.log(row_sum)
        low_prob = jnp.exp(scores - log_total).astype(jnp.bfloat16)
        result = jnp.einsum(
            "gqk,gkd->gqd", low_prob, value_block, preferred_element_type=jnp.float32
        ).astype(jnp.bfloat16)
        return (result, log_total[..., 0])

    results, log_total = lax.map(one_group, (query_tiles, chosen))
    restored = (
        jnp.zeros(query_rows.shape, jnp.bfloat16)
        .at[tile_order]
        .set(results.reshape(-1, head_width))
    )
    return (restored, log_total.reshape(-1))


def head_backward(query_rows, key_rows, value_rows, grad_rows, log_total, tile_order, neighbours):
    count_tiles = neighbours.shape[0]
    head_width = query_rows.shape[1]
    score_scale = 1.0 / math.sqrt(head_width)
    query_tiles = query_rows[tile_order].reshape(count_tiles // 3, 3, TILE, head_width)
    grad_tiles = grad_rows[tile_order].reshape(count_tiles // 3, 3, TILE, head_width)
    key_tiles = key_rows[tile_order].reshape(count_tiles, TILE, head_width)
    value_tiles = value_rows[tile_order].reshape(count_tiles, TILE, head_width)
    log_blocks = log_total.reshape(count_tiles // 3, 3, TILE)
    chosen = neighbours.reshape(count_tiles // 3, 3, NB)

    def one_group(partial_value, operands):
        key_acc, value_acc = partial_value
        query_block, grad_block, log_block, pick_list = operands
        key_block = pick_tiles(key_tiles, pick_list)
        value_block = pick_tiles(value_tiles, pick_list)
        scores = (
            jnp.einsum("gqd,gkd->gqk", query_block, key_block, preferred_element_type=jnp.float32)
            * score_scale
        )
        probability = jnp.exp(scores - log_block[..., None])
        low_prob = probability.astype(jnp.bfloat16)
        grad_prob = jnp.einsum(
            "gqd,gkd->gqk", grad_block, value_block, preferred_element_type=jnp.float32
        )
        row_dot = jnp.sum(probability * grad_prob, axis=-1, keepdims=True)
        grad_score = (probability * (grad_prob - row_dot)).astype(jnp.bfloat16)
        grad_query = (
            jnp.einsum("gqk,gkd->gqd", grad_score, key_block, preferred_element_type=jnp.float32)
            * score_scale
        ).astype(jnp.bfloat16)
        grad_key = (
            jnp.einsum("gqk,gqd->gkd", grad_score, query_block, preferred_element_type=jnp.float32)
            * score_scale
        )
        grad_value = jnp.einsum(
            "gqk,gqd->gkd", low_prob, grad_block, preferred_element_type=jnp.float32
        )
        flat_ids = pick_list.reshape(-1)
        key_acc = key_acc.at[flat_ids].add(grad_key.reshape(-1, TILE, head_width))
        value_acc = value_acc.at[flat_ids].add(grad_value.reshape(-1, TILE, head_width))
        return ((key_acc, value_acc), grad_query)

    empty_acc = jnp.zeros((count_tiles, TILE, head_width), jnp.float32)
    (key_acc, value_acc), grad_query = lax.scan(
        one_group, (empty_acc, empty_acc), (query_tiles, grad_tiles, log_blocks, chosen)
    )

    def restore(tile_rows):
        return (
            jnp.zeros(query_rows.shape, jnp.bfloat16)
            .at[tile_order]
            .set(tile_rows.reshape(-1, head_width).astype(jnp.bfloat16))
        )

    return (restore(grad_query), restore(key_acc), restore(value_acc))


def local(queries, key_vectors, values, out_weight, cotangent, neighbours, tile_order):
    video_count, local_rows, all_width = queries.shape

    def as_heads(tensor):
        return tensor.reshape(video_count, local_rows, HEADS, HD)

    query_heads, key_heads, value_heads = (
        lax.all_to_all(as_heads(queries), "seq", split_axis=2, concat_axis=1, tiled=True),
        lax.all_to_all(as_heads(key_vectors), "seq", split_axis=2, concat_axis=1, tiled=True),
        lax.all_to_all(as_heads(values), "seq", split_axis=2, concat_axis=1, tiled=True),
    )

    def forward_one(query_rows, key_rows, value_rows):
        return head_forward(query_rows, key_rows, value_rows, tile_order, neighbours)

    forward_heads = jax.vmap(
        jax.vmap(forward_one, in_axes=1, out_axes=(1, 0)), in_axes=0, out_axes=(0, 0)
    )
    attended_heads, log_total = forward_heads(query_heads, key_heads, value_heads)
    full_weight = lax.all_gather(out_weight, ("seq", "fsdp"), axis=0, tiled=True)
    attended_local = lax.all_to_all(
        attended_heads, "seq", split_axis=1, concat_axis=2, tiled=True
    ).reshape(video_count * local_rows, all_width)
    cot_rows = cotangent.reshape(video_count * local_rows, -1)
    projected = (
        jnp.dot(attended_local, full_weight, preferred_element_type=jnp.float32)
        .astype(jnp.bfloat16)
        .reshape(video_count, local_rows, -1)
    )
    contract_last = (((1,), (1,)), ((), ()))
    contract_first = (((0,), (0,)), ((), ()))
    grad_local = lax.dot_general(
        cot_rows, full_weight, contract_last, preferred_element_type=jnp.float32
    ).astype(jnp.bfloat16)
    grad_heads = lax.all_to_all(
        grad_local.reshape(video_count, local_rows, HEADS, HD),
        "seq",
        split_axis=2,
        concat_axis=1,
        tiled=True,
    )
    grad_weight = lax.psum_scatter(
        lax.dot_general(
            attended_local, cot_rows, contract_first, preferred_element_type=jnp.float32
        ),
        ("seq", "fsdp"),
        scatter_dimension=0,
        tiled=True,
    ).astype(jnp.bfloat16)

    def backward_one(query_rows, key_rows, value_rows, grad_rows, log_rows):
        return head_backward(
            query_rows, key_rows, value_rows, grad_rows, log_rows, tile_order, neighbours
        )

    backward_heads = jax.vmap(
        jax.vmap(backward_one, in_axes=(1, 1, 1, 1, 0), out_axes=1), in_axes=0, out_axes=0
    )
    grad_query, grad_key, grad_value = backward_heads(
        query_heads, key_heads, value_heads, grad_heads, log_total
    )
    grad_query, grad_key, grad_value = (
        lax.all_to_all(grad_query, "seq", split_axis=1, concat_axis=2, tiled=True),
        lax.all_to_all(grad_key, "seq", split_axis=1, concat_axis=2, tiled=True),
        lax.all_to_all(grad_value, "seq", split_axis=1, concat_axis=2, tiled=True),
    )
    shape_out = (video_count, local_rows, all_width)
    return (
        projected,
        grad_query.reshape(shape_out),
        grad_key.reshape(shape_out),
        grad_value.reshape(shape_out),
        grad_weight,
    )


def solution(mesh):
    placed = (
        P("fsdp", "seq", None),
        P("fsdp", "seq", None),
        P("fsdp", "seq", None),
        P(("seq", "fsdp"), None),
        P("fsdp", "seq", None),
        P(),
        P(),
    )
    return jax.shard_map(
        local,
        mesh=mesh,
        in_specs=placed,
        out_specs=(
            P("fsdp", "seq", None),
            P("fsdp", "seq", None),
            P("fsdp", "seq", None),
            P("fsdp", "seq", None),
            P(("seq", "fsdp"), None),
        ),
        check_vma=False,
    )
```

profile of v0, /device:TPU:0, one launch (start us, length us, event | category | flops | bytes accessed | tf_op | source)
XLA Modules:
  0.0 1044.5 jit_solution(1663358205235776297)
XLA Ops:
  10.2 6.0 all-to-all-start
  17.3 13.2 %all-to-all-done = bf16[1,216,16,128]{3,1,0,2:T(8,128)(2,1)S(1)} async-done(((bf16[1,216,16,128]{3,1,0,2:T(8,128)(2,1)}), bf16[1,216,16,128]{3,1,0,2:T(8,128)(2,1)S(1)}, u32[]{:S(2)}, u32[]{:S(2)}) %all-to-all-start) | async-done | bytes 884768 | tf_op jit(solution)/shard_map/all_to_all | solution.py:121
  30.5 3.8 all-to-all-start.1
  35.4 12.9 %all-to-all-done.1 = bf16[1,216,16,128]{3,1,0,2:T(8,128)(2,1)S(1)} async-done(((bf16[1,216,16,128]{3,1,0,2:T(8,128)(2,1)}), bf16[1,216,16,128]{3,1,0,2:T(8,128)(2,1)S(1)}, u32[]{:S(2)}, u32[]{:S(2)}) %all-to-all-start.1) | async-done | bytes 884768 | tf_op jit(solution)/shard_map/all_to_all | solution.py:122
  48.3 4.8 all-to-all-start.2
  54.6 8.1 gather_fusion.4
  62.8 7.1 gather_fusion.5
  69.9 8.7 gather_fusion.6
  79.7 56.7 %while.26 = (s32[]{:T(128)}, bf16[6,1,1,3,192,128]{5,4,3,2,1,0:T(8,128)(2,1)}, f32[6,1,1,3,192]{4,3,2,1,0:T(4,128)}, bf16[6,1,1,3,192,128]{5,4,3,2,1,0:T(8,128)(...) while((s32[]{:T(128)}, ...), condition=%wide.region_3.4_spmd, body=%wide.region_0.3_spmd.sunk | while | flops 517644800 | bytes 25535100 | solution.py:47
  136.4 14.8 %scatter_custom_fusion.2 = bf16[3456,128]{1,0:T(8,128)(2,1)} fusion(s32[3456]{0:T(1024)} %copy-done.10, bf16[3456,128]{1,0:T(8,128)(2,1)} %bitcast.274, bf16[]{:T(256)} %constant.33.clone.1), kind=kCustom, calls=%fused_computation.84 | custom fusion | bytes 885248 | tf_op jit(solution)/shard_map/vmap(vmap())/scatter | solution.py:51
  151.2 8.3 copy.103
  160.0 19.9 %reduce.12 = bf16[3456,128]{1,0:T(8,128)(2,1)} reduce(bf16[3456,1,1,128]{3,2,1,0:T(2,128)(2,1)S(1)} %bitcast.253, bf16[]{:T(256)} %broadcast.167), dimensions={1,2}, to_apply=%bitcast.168.reduce_sub_computation | reduce | bytes 1769474
  182.2 20.7 %all_to_all.120 = bf16[16,2,13824]{2,1,0:T(2,128)(2,1)} all-to-all(bf16[16,2,13824]{2,1,0:T(2,128)(2,1)S(1)} %reshape.548), channel_id=1, replica_groups=mesh['seq'=16,'fsdp'=8] {'seq'}, dimensions={0} | all-to-all | bytes 1769472 | tf_op jit(solution)/shard_map/all_to_all | solution.py:134
  202.8 4.1 reshape.549
  207.2 8.1 fusion.35
  215.3 118.4 %all-gather.2.cloned.1.call-done = bf16[2048,2048]{1,0:T(8,128)(2,1)} async-done(((bf16[16,2048]{1,0:T(8,128)(2,1)}), bf16[2048,2048]{1,0:T(8,128)(2,1)}) %all-gather.2.cloned.1.call-update) | async-done | bytes 8388624 | tf_op jit(solution)/shard_map/all_gather | solution.py:133
  333.7 6.1 fusion.34
  340.2 20.6 %all_to_all.121 = bf16[1,216,16,128]{3,1,0,2:T(8,128)(2,1)S(1)} all-to-all(bf16[1,216,16,128]{3,1,0,2:T(8,128)(2,1)S(1)} %copy.66), channel_id=1, replica_groups=mesh['seq'=16,'fsdp'=8] {'seq'}, dimensions={2} | all-to-all | bytes 1769472 | tf_op jit(solution)/shard_map/all_to_all | solution.py:148
  360.8 8.1 gather_fusion.7
  372.9 183.7 %while.27 = (s32[]{:T(128)}, f32[1,1,18,192,128]{4,3,2,1,0:T(8,128)}, f32[1,1,18,192,128]{4,3,2,1,0:T(8,128)}, bf16[6,1,1,3,192,128]{5,4,3,2,1,0:T(8,128)(2,1)},...) while((s32[]{:T(128)}, ...), condition=%wide.region_9.10_spmd, body=%wide.region_5.9_spmd.sunk | while | flops 1284121216 | bytes 79791168 | solution.py:100
  386.5 7.2 scatter_fusion.1
  396.3 7.1 scatter_fusion
  417.1 7.2 scatter_fusion.1
  427.0 7.1 scatter_fusion
  447.7 7.2 scatter_fusion.1
  457.6 7.1 scatter_fusion
  478.3 7.2 scatter_fusion.1
  488.2 7.1 scatter_fusion
  508.9 7.2 scatter_fusion.1
  518.8 7.1 scatter_fusion
  539.5 7.2 scatter_fusion.1
  549.4 7.2 scatter_fusion
  556.5 14.3 %scatter_custom_fusion.3 = bf16[3456,128]{1,0:T(8,128)(2,1)S(1)} fusion(s32[3456]{0:T(1024)} %copy-done.10, bf16[3456,128]{1,0:T(8,128)(2,1)} %bitcast.273, bf16[]{:T(256)} %constant.33.clone.1), kind=kCustom, calls=%fused_computation.82 | custom fusion | bytes 885248 | tf_op jit(solution)/shard_map/vmap(vmap())/scatter | solution.py:108
  570.9 14.1 %copy.102 = bf16[1,3456,1,128]{3,2,0,1:T(2,128)(2,1)S(1)} copy(bf16[1,3456,1,128]{3,1,2,0:T(8,128)(2,1)S(1)} %bitcast.266) | data formatting | bytes 1769472 | tf_op jit(solution)/shard_map/vmap(vmap())/transpose | solution.py:172
  585.0 19.0 %reduce.13 = bf16[3456,128]{1,0:T(8,128)(2,1)S(1)} reduce(bf16[3456,1,1,128]{3,2,1,0:T(2,128)(2,1)S(1)} %bitcast.256, bf16[]{:T(256)} %broadcast.167), dimensions={1,2}, to_apply=%bitcast.167.reduce_sub_computation | reduce | bytes 1769474
  605.1 4.0 all-to-all-start.5
  610.8 14.3 %scatter_custom_fusion.4 = bf16[3456,128]{1,0:T(8,128)(2,1)S(1)} fusion(s32[3456]{0:T(1024)} %copy-done.10, bf16[3456,128]{1,0:T(8,128)(2,1)S(1)} %bitcast.276, bf16[]{:T(256)} %constant.33.clone.1), kind=kCustom, calls=%fused_computation.80 | custom fusion | bytes 885248 | tf_op jit(solution)/shard_map/vmap(vmap())/scatter | solution.py:108
  625.0 14.1 %copy.101 = bf16[1,3456,1,128]{3,2,0,1:T(2,128)(2,1)S(1)} copy(bf16[1,3456,1,128]{3,1,2,0:T(8,128)(2,1)S(1)} %bitcast.267) | data formatting | bytes 1769472 | tf_op jit(solution)/shard_map/vmap(vmap())/transpose | solution.py:172
  639.2 19.0 %reduce.14 = bf16[3456,128]{1,0:T(8,128)(2,1)S(1)} reduce(bf16[3456,1,1,128]{3,2,1,0:T(2,128)(2,1)S(1)} %bitcast.257, bf16[]{:T(256)} %broadcast.167), dimensions={1,2}, to_apply=%bitcast.166.reduce_sub_computation | reduce | bytes 1769474
  659.3 5.8 all-to-all-start.6
  666.7 14.3 %scatter_custom_fusion.5 = bf16[3456,128]{1,0:T(8,128)(2,1)S(1)} fusion(s32[3456]{0:T(1024)} %copy-done.10, bf16[3456,128]{1,0:T(8,128)(2,1)S(1)} %bitcast.275, bf16[]{:T(256)} %constant.33.clone.1), kind=kCustom, calls=%fused_computation.78 | custom fusion | bytes 885248 | tf_op jit(solution)/shard_map/vmap(vmap())/scatter | solution.py:108
  681.0 14.1 %copy.100 = bf16[1,3456,1,128]{3,2,0,1:T(2,128)(2,1)S(1)} copy(bf16[1,3456,1,128]{3,1,2,0:T(8,128)(2,1)S(1)} %bitcast.263) | data formatting | bytes 1769472 | tf_op jit(solution)/shard_map/vmap(vmap())/transpose | solution.py:172
  695.1 19.0 %reduce.15 = bf16[3456,128]{1,0:T(8,128)(2,1)S(1)} reduce(bf16[3456,1,1,128]{3,2,1,0:T(2,128)(2,1)S(1)} %bitcast.254, bf16[]{:T(256)} %broadcast.167), dimensions={1,2}, to_apply=%bitcast.165.reduce_sub_computation | reduce | bytes 1769474
  715.3 5.7 all-to-all-start.7
  721.0 6.3 fusion.33
  729.6 4.1 reshape.553
  737.1 4.1 reshape.555
  742.7 293.1 %reduce-scatter.2.cloned.1.call-done = f32[16,2048]{1,0:T(8,128)} async-done(((f32[2048,2048]{1,0:T(8,128)}), f32[16,2048]{1,0:T(8,128)}) %reduce-scatter.2.cloned.1.call-update) | async-done | bytes 131088 | tf_op jit(solution)/shard_map/reduce_scatter | solution.py:155
  (251 shorter events, 184.2 us)
Async XLA Ops:
  7.2 200.0 %copy-start = (bf16[1,216,2048]{2,1,0:T(8,128)(2,1)S(1)}, bf16[1,216,2048]{2,1,0:T(8,128)(2,1)}, u32[]{:S(2)}) copy-start(bf16[1,216,2048]{2,1,0:T(8,128)(2,1)} %param.15) | copy-start | bytes 2654212
  7.2 9.0 copy-start.8
  7.2 326.5 %all-gather.2.cloned.1.call-start = ((), (), s32[]{:S(2)}) async-start(), calls=%async_computation.9 | async-start | bytes 8454144 | tf_op jit(solution)/shard_map/all_gather | solution.py:133
  10.2 20.4 %all-to-all-start = ((bf16[1,216,16,128]{3,1,0,2:T(8,128)(2,1)}), bf16[1,216,16,128]{3,1,0,2:T(8,128)(2,1)S(1)}, u32[]{:S(2)}, u32[]{:S(2)}) async-start(bf16[1,216,16,128]{3,1,0,2:T(8,128)(2,1)} %copy_bitcast_fusion.2), calls=%async_computation | async-start | bytes 1769472 | tf_op jit(solution)/shard_map/all_to_all | solution.py:121
  16.2 18.1 %copy-start.9 = (bf16[1,216,2048]{2,1,0:T(8,128)(2,1)S(1)}, bf16[1,216,2048]{2,1,0:T(8,128)(2,1)}, u32[]{:S(2)}) copy-start(bf16[1,216,2048]{2,1,0:T(8,128)(2,1)} %param.13) | copy-start | bytes 2654212
  30.5 17.8 %all-to-all-start.1 = ((bf16[1,216,16,128]{3,1,0,2:T(8,128)(2,1)}), bf16[1,216,16,128]{3,1,0,2:T(8,128)(2,1)S(1)}, u32[]{:S(2)}, u32[]{:S(2)}) async-start(bf16[1,216,16,128]{3,1,0,2:T(8,128)(2,1)} %copy_bitcast_fusion.1), calls=%async_computation.1 | async-start | bytes 1769472 | tf_op jit(solution)/shard_map/all_to_all | solution.py:122
  34.3 20.3 %copy-start.11 = (s32[3456]{0:T(1024)S(1)}, s32[3456]{0:T(1024)}, u32[]{:S(2)}) copy-start(s32[3456]{0:T(1024)} %param.17) | copy-start | bytes 41476
  48.3 21.6 %all-to-all-start.2 = ((bf16[1,216,16,128]{3,1,0,2:T(8,128)(2,1)}), bf16[1,216,16,128]{3,1,0,2:T(8,128)(2,1)}, u32[]{:S(2)}, u32[]{:S(2)}) async-start(bf16[1,216,16,128]{3,1,0,2:T(8,128)(2,1)} %copy_bitcast_fusion), calls=%async_computation.2 | async-start | bytes 1769472 | tf_op jit(solution)/shard_map/all_to_all | solution.py:123
  53.2 982.7 %reduce-scatter.2.cloned.1.call-start = ((), (), s32[]{:S(2)}) async-start(), calls=%async_computation.10 | async-start | bytes 16908288 | tf_op jit(solution)/shard_map/reduce_scatter | solution.py:155
  54.6 8.1 copy-start.10
  86.0 1.5 copy-start.5
  95.5 1.5 copy-start.5
  104.9 1.5 copy-start.5
  114.4 1.5 copy-start.5
  123.8 1.5 copy-start.5
  133.3 1.5 copy-start.5
  207.2 8.2 copy-start.6
  376.0 4.1 copy-start.3
  382.8 2.3 copy-start.2
  382.8 2.3 copy-start.4
  406.6 4.1 copy-start.3
  413.4 2.3 copy-start.2
  413.4 2.3 copy-start.4
  437.2 4.1 copy-start.3
  444.0 2.3 copy-start.2
  444.0 2.3 copy-start.4
  467.8 4.1 copy-start.3
  474.6 2.3 copy-start.2
  474.6 2.3 copy-start.4
  498.4 4.1 copy-start.3
  505.2 2.3 copy-start.2
  505.2 2.3 copy-start.4
  529.0 4.1 copy-start.3
  535.8 2.3 copy-start.2
  535.8 2.3 copy-start.4
  605.1 54.1 %all-to-all-start.5 = ((bf16[16,2,13824]{2,1,0:T(2,128)(2,1)}), bf16[16,2,13824]{2,1,0:T(2,128)(2,1)S(1)}, u32[]{:S(2)}, u32[]{:S(2)}) async-start(bf16[16,2,13824]{2,1,0:T(2,128)(2,1)} %reshape.550), calls=%async_computation.5 | async-start | bytes 1769472 | tf_op jit(solution)/shard_map/all_to_all | solution.py:176
  659.3 56.0 %all-to-all-start.6 = ((bf16[16,2,13824]{2,1,0:T(2,128)(2,1)}), bf16[16,2,13824]{2,1,0:T(2,128)(2,1)}, u32[]{:S(2)}, u32[]{:S(2)}) async-start(bf16[16,2,13824]{2,1,0:T(2,128)(2,1)} %reshape.552), calls=%async_computation.6 | async-start | bytes 1769472 | tf_op jit(solution)/shard_map/all_to_all | solution.py:177
  714.1 6.9 copy-start.7
  715.3 21.8 %all-to-all-start.7 = ((bf16[16,2,13824]{2,1,0:T(2,128)(2,1)}), bf16[16,2,13824]{2,1,0:T(2,128)(2,1)}, u32[]{:S(2)}, u32[]{:S(2)}) async-start(bf16[16,2,13824]{2,1,0:T(2,128)(2,1)} %reshape.554), calls=%async_computation.7 | async-start | bytes 1769472 | tf_op jit(solution)/shard_map/all_to_all | solution.py:178
  741.2 296.2 %copy-start.1 = (bf16[1,216,2048]{2,1,0:T(8,128)(2,1)S(1)}, bf16[1,216,2048]{2,1,0:T(8,128)(2,1)}, u32[]{:S(2)}) copy-start(bf16[1,216,2048]{2,1,0:T(8,128)(2,1)} %param.15) | copy-start | bytes 2654212
Sparse Core Ops, SparseCore 0:
  9.7 323.9 all-gather.1
  336.1 699.6 reduce-scatter.1
where the time goes:
time: 1060 us; the launch traced here: 1040 us
  waiting for transfers between devices  440 us (42%)
  local copies, waits for them, and re-layouts  228 us (22%)
  other arithmetic  188 us (18%)
  matrix products  102 us (10%)
  blocking collectives  41.3 us (4%)
  starting transfers between devices  30.1 us (3%)
  between operations  14.7 us (1%)
    reduce_scatter x1, waiting for transfers between devices, local(): lax.psum_scatter(lax.dot_general(attended_local, cot_rows, contract_first...  293 us
    all_gather x1, waiting for transfers between devices, local(): lax.all_gather(out_weight, ('seq', 'fsdp'), axis=0, tiled=True)  118 us
    unnamed x4, other arithmetic  76.8 us
    scatter-add x6, other arithmetic, one_group(): value_acc.at[flat_ids].add(grad_value.reshape(-1, TILE, head_width))  43.1 us
    scatter x3, local copies, waits for them, and re-layouts, restore(): return jnp.zeros(query_rows.shape, jnp.bfloat16).at[tile_order].set(tile_...  42.9 us
    scatter-add x6, other arithmetic, one_group(): key_acc = key_acc.at[flat_ids].add(grad_key.reshape(-1, TILE, head_width))  42.8 us
    transpose x3, local copies, waits for them, and re-layouts, local(): backward_heads(query_heads, key_heads, value_heads, grad_heads, log_total)  42.4 us
    gather x24, local copies, waits for them, and re-layouts, pick_tiles(): gathered = tile_rows[chosen]  42.3 us
  transfers between devices with their start and end apart: 8, of which 5 were waited for; matrix products, arithmetic and copies ran while one was open for 49% of the time, Pallas kernels for 0%

commit v1 on v0

v1 whole, which is shorter than its diff:
```python
import math

import jax
import jax.numpy as jnp
import numpy as np
from jax import lax
from jax.experimental import pallas as pl
from jax.experimental.pallas import tpu as pltpu
from jax.sharding import Mesh, PartitionSpec as P

T=192; NT=18; NB=9; N=T*NT; KC=T*NB; HD=128
bf=jnp.bfloat16; f32=jnp.float32
SC=1.0/math.sqrt(HD); LOG2E=math.log2(math.e)
PITCH=4

def permute_rows(order_ref, src, dst, width, scatter, unroll=16):
    def body(i, c):
        for u in range(unroll):
            p=i*unroll+u
            t=order_ref[p]
            a,b=(t,p) if scatter else (p,t)
            dst[pl.ds(a*width,width),:]=src[pl.ds(b*width,width),:]
        return c
    lax.fori_loop(0,N//unroll,body,0)

def k1(order_ref, neigh_ref, qkv_ref, att_ref, qp_ref, kp_ref, vp_ref, o_ref, rinv_ref, e_ref, tok, per, kc, vc, s_ref):
    t=pl.program_id(0)
    @pl.when(t==0)
    def _():
        for j in range(3):
            for s in range(16):
                tok[pl.ds(s*216*PITCH+j,216,stride=PITCH),:]=qkv_ref[s,j].astype(f32)
        permute_rows(order_ref,tok,per,PITCH,False)
        for j,r in enumerate((qp_ref,kp_ref,vp_ref)):
            for u in range(NT):
                r[pl.ds(u*T,T),:]=per[pl.ds(u*T*PITCH+j,T,stride=PITCH),:].astype(bf)
    for j in range(NB):
        n=neigh_ref[t*NB+j]
        off=pl.multiple_of(n*T,T)
        kc[pl.ds(j*T,T),:]=kp_ref[pl.ds(off,T),:]
        vc[pl.ds(j*T,T),:]=vp_ref[pl.ds(off,T),:]
    q=qp_ref[pl.ds(pl.multiple_of(t*T,T),T),:]
    s=lax.dot_general(q,kc[...],(((1,),(1,)),((),())),preferred_element_type=f32)
    m=jnp.max(s,axis=-1,keepdims=True)
    e=jnp.exp2(s*(SC*LOG2E)-m*(SC*LOG2E))
    l=jnp.sum(e,axis=-1,keepdims=True)
    eb=e.astype(bf)
    e_ref[0]=eb
    rinv=1.0/l
    o=jnp.dot(eb,vc[...],preferred_element_type=f32)*rinv
    rinv_ref[...]=jnp.broadcast_to(rinv,(T,HD))
    o_ref[pl.ds(pl.multiple_of(t*T,T),T),:]=o
    @pl.when(t==NT-1)
    def _():
        permute_rows(order_ref,o_ref,tok,1,True)
        for s in range(16):
            att_ref[s]=tok[pl.ds(s*216,216),:].astype(bf)

def run_k1(order, neigh, qkv):
    full=lambda shape: pl.BlockSpec(shape,lambda t,*_:(0,)*len(shape))
    return pl.pallas_call(k1,
      grid_spec=pltpu.PrefetchScalarGridSpec(num_scalar_prefetch=2,grid=(NT,),
        in_specs=[full((16,3,216,HD))],
        out_specs=[full((16,216,HD)),full((N,HD)),full((N,HD)),full((N,HD)),full((N,HD)),
                   pl.BlockSpec((T,HD),lambda t,*_:(t,0)),pl.BlockSpec((1,T,KC),lambda t,*_:(t,0,0))],
        scratch_shapes=[pltpu.VMEM((N*PITCH,HD),f32),pltpu.VMEM((N*PITCH,HD),f32),pltpu.VMEM((KC,HD),bf),pltpu.VMEM((KC,HD),bf),pltpu.VMEM((T,KC),f32)]),
      out_shape=[jax.ShapeDtypeStruct((16,216,HD),bf)]+[jax.ShapeDtypeStruct((N,HD),bf)]*3+[jax.ShapeDtypeStruct((N,HD),f32),jax.ShapeDtypeStruct((N,HD),f32),jax.ShapeDtypeStruct((NT,T,KC),bf)],
      compiler_params=pltpu.CompilerParams(vmem_limit_bytes=60*1024*1024),
      name="attend")(order,neigh,qkv)

def k2(order_ref, neigh_ref, g_ref, qp_ref, kp_ref, vp_ref, o_ref, rinv_ref, e_ref, out_ref, tok, gp, acc, kc, vc):
    t=pl.program_id(0)
    @pl.when(t==0)
    def _():
        for s in range(16):
            tok[pl.ds(s*216,216),:]=g_ref[s].astype(f32)
        permute_rows(order_ref,tok,gp,1,False)
        for u in range(NT*PITCH):
            acc[pl.ds(u*T,T),:]=jnp.zeros((T,HD),f32)
    ns=[]
    for j in range(NB):
        n=neigh_ref[t*NB+j]
        off=pl.multiple_of(n*T,T); ns.append(n)
        kc[pl.ds(j*T,T),:]=kp_ref[pl.ds(off,T),:]
        vc[pl.ds(j*T,T),:]=vp_ref[pl.ds(off,T),:]
    ts=pl.ds(pl.multiple_of(t*T,T),T)
    q=qp_ref[ts,:]
    gs=(gp[ts,:]*rinv_ref[...]).astype(bf)
    d=jnp.sum(gs.astype(f32)*o_ref[ts,:],axis=-1,keepdims=True)
    dp=lax.dot_general(gs,vc[...],(((1,),(1,)),((),())),preferred_element_type=f32)
    eb=e_ref[0]
    ds=(eb.astype(f32)*(dp-d)).astype(bf)
    dq=jnp.dot(ds,kc[...],preferred_element_type=f32)*SC
    acc[pl.ds(t*T*PITCH,T,stride=PITCH),:]=dq
    dk=lax.dot_general(ds,q,(((0,),(0,)),((),())),preferred_element_type=f32)*SC
    dv=lax.dot_general(eb,gs,(((0,),(0,)),((),())),preferred_element_type=f32)
    for j in range(NB):
        base=ns[j]*(T*PITCH)
        i1=pl.ds(base+1,T,stride=PITCH); i2=pl.ds(base+2,T,stride=PITCH)
        acc[i1,:]=acc[i1,:]+dk[j*T:(j+1)*T]
        acc[i2,:]=acc[i2,:]+dv[j*T:(j+1)*T]
    @pl.when(t==NT-1)
    def _():
        permute_rows(order_ref,acc,tok,PITCH,True)
        for s in range(16):
            for j in range(3):
                out_ref[s,j]=tok[pl.ds(s*216*PITCH+j,216,stride=PITCH),:].astype(bf)

def run_k2(order, neigh, g, qp,kp,vp,o,rinv,e):
    full=lambda shape: pl.BlockSpec(shape,lambda t,*_:(0,)*len(shape))
    return pl.pallas_call(k2,
      grid_spec=pltpu.PrefetchScalarGridSpec(num_scalar_prefetch=2,grid=(NT,),
        in_specs=[full((16,216,HD)),full((N,HD)),full((N,HD)),full((N,HD)),full((N,HD)),
                   pl.BlockSpec((T,HD),lambda t,*_:(t,0)),pl.BlockSpec((1,T,KC),lambda t,*_:(t,0,0))],
        out_specs=full((16,3,216,HD)),
        scratch_shapes=[pltpu.VMEM((N*PITCH,HD),f32),pltpu.VMEM((N,HD),f32),pltpu.VMEM((N*PITCH,HD),f32),pltpu.VMEM((KC,HD),bf),pltpu.VMEM((KC,HD),bf)]),
      out_shape=jax.ShapeDtypeStruct((16,3,216,HD),bf),
      compiler_params=pltpu.CompilerParams(vmem_limit_bytes=60*1024*1024),
      name="attend_grad")(order,neigh,g,qp,kp,vp,o,rinv,e)


CHIPS = ("y", "zl")
SEQ = ("y", "zl", "c")
VIDEOS = ("x", "zh")


def shift(value, axis, size, step):
    return lax.ppermute(value, axis, [(i, (i + step) % size) for i in range(size)])


def gather_ring(value, axis, size):
    me = lax.axis_index(axis)
    parts = [value] + [shift(value, axis, size, d) for d in range(1, size)]
    out = jnp.zeros((size,) + value.shape, value.dtype)
    for d, part in enumerate(parts):
        out = lax.dynamic_update_index_in_dim(out, part, (me - d) % size, 0)
    return out


def gather_weight(own):
    w = gather_ring(own, "y", 4)
    w = gather_ring(w, "zl", 2)
    w = gather_ring(w, "zh", 2)
    w = gather_ring(w, "x", 4)
    return w.transpose(3, 2, 0, 1, 4, 5).reshape(1024, 2048)


def scatter_weight(part):
    x, zh = lax.axis_index("x"), lax.axis_index("zh")

    def piece(d):
        return lax.dynamic_index_in_dim(part, (x + d) % 4, 1, keepdims=False)

    far = piece(2).astype(bf)
    up, down = piece(1), piece(3)
    a = shift(far[..., :1024], "x", 4, 1)
    b = shift(far[..., 1024:], "x", 4, -1)
    up_low = shift(up[..., 1024:].astype(bf), "x", 4, 1)
    down_low = shift(down[..., :1024].astype(bf), "x", 4, -1)
    up_high = shift((up[..., :1024] + a.astype(f32)).astype(bf), "x", 4, 1)
    down_high = shift((down[..., 1024:] + b.astype(f32)).astype(bf), "x", 4, -1)
    got = jnp.concatenate(
        [up_high.astype(f32) + down_low.astype(f32), up_low.astype(f32) + down_high.astype(f32)],
        axis=-1,
    )
    rows = piece(0) + got
    mine = lax.dynamic_index_in_dim(rows, zh, 1, keepdims=False)
    other = lax.dynamic_index_in_dim(rows, 1 - zh, 1, keepdims=False)
    rows = mine + shift(other.astype(bf), "zh", 2, 1).astype(f32)
    rows = lax.all_to_all(rows.astype(bf), CHIPS, split_axis=0, concat_axis=0, tiled=True)
    return jnp.sum(rows.astype(f32), axis=0).astype(bf)


def local(queries, key_vectors, values, out_weight, cotangent, neighbours, tile_order):
    core = lax.axis_index("c")
    neigh = neighbours.reshape(-1)

    def by_head(tensor):
        return tensor.reshape(216, 16, HD).transpose(1, 0, 2)

    qkv = jnp.stack([by_head(queries[0]), by_head(key_vectors[0]), by_head(values[0])], axis=1)
    qkv = lax.all_to_all(qkv, SEQ, split_axis=0, concat_axis=0, tiled=True)

    cot = cotangent[0]
    cot_other = shift(cot, "c", 2, 1)
    first = core == 0
    cot_chip = jnp.concatenate(
        [jnp.where(first, cot, cot_other), jnp.where(first, cot_other, cot)], axis=0
    )
    weight = gather_weight(out_weight)
    grad = lax.dot_general(
        cot_chip, weight, (((1,), (1,)), ((), ())), preferred_element_type=f32
    ).astype(bf)
    grad = grad.reshape(432, 8, HD).transpose(1, 0, 2)
    grad = lax.all_to_all(grad, CHIPS, split_axis=0, concat_axis=0, tiled=True)

    att, *saved = run_k1(tile_order, neigh, qkv)
    att = lax.all_to_all(att.reshape(8, 432, HD), CHIPS, split_axis=0, concat_axis=0, tiled=True)
    att = att.transpose(1, 0, 2).reshape(432, 1024)
    grads = run_k2(tile_order, neigh, grad.reshape(16, 216, HD), *saved)
    grads = lax.all_to_all(grads, SEQ, split_axis=0, concat_axis=0, tiled=True)

    partial = jnp.dot(att, weight, preferred_element_type=f32)
    mine = lax.dynamic_slice_in_dim(partial, core * 216, 216, 0)
    other = lax.dynamic_slice_in_dim(partial, (1 - core) * 216, 216, 0)
    projected = (mine + shift(other.astype(bf), "c", 2, 1).astype(f32)).astype(bf)

    weight_part = lax.dot_general(
        att, cot_chip, (((0,), (0,)), ((), ())), preferred_element_type=f32
    )
    grad_weight = scatter_weight(weight_part.reshape(8, 4, 2, 16, 2048))

    def by_token(tensor):
        return tensor.transpose(1, 0, 2).reshape(1, 216, 2048)

    return (
        projected[None],
        by_token(grads[:, 0]),
        by_token(grads[:, 1]),
        by_token(grads[:, 2]),
        grad_weight,
    )


def solution(mesh):
    fine = Mesh(np.asarray(mesh.devices).reshape(4, 2, 2, 4, 2), ("y", "zl", "c", "x", "zh"))
    rows = P(VIDEOS, SEQ, None)
    weight = P(SEQ + VIDEOS, None)
    return jax.shard_map(
        local,
        mesh=fine,
        in_specs=(rows, rows, rows, weight, rows, P(), P()),
        out_specs=(rows, rows, rows, rows, weight),
        check_vma=False,
    )
```

time: 1060 us -> 274 us (0.26); the launches traced: 1040 us -> 272 us
  waiting for transfers between devices: 440 us -> 84.2 us
  local copies, waits for them, and re-layouts: 228 us -> 46.8 us
  other arithmetic: 188 us -> 14.8 us
  matrix products: 102 us -> 12.8 us
  Pallas kernels: 0 us -> 67.2 us
  blocking collectives: 41.3 us -> 0 us
  starting transfers between devices: 30.1 us -> 45.6 us
  between operations: 14.7 us -> 1.09 us
    reduce_scatter x1 -> x0, waiting for transfers between devices: 293 us -> none  [local(): lax.psum_scatter(lax.dot_general(attended_local, cot_rows, contract_first...]
    all_gather x1 -> x0, waiting for transfers between devices: 118 us -> none  [local(): lax.all_gather(out_weight, ('seq', 'fsdp'), axis=0, tiled=True)]
    dot_general x45 -> x3, matrix products: 102 us -> 12.8 us  [the longest x1 4.76 us: local(): lax.dot_general(cot_chip, weight, (((1,), (1,)), ((), ())), preferred_ele...]
    scatter-add x12 -> x0, other arithmetic: 85.9 us -> none  [the longest x6 43.1 us: one_group(): value_acc.at[flat_ids].add(grad_value.reshape(-1, TILE, head_width))]
    unnamed x4 -> x0, other arithmetic: 76.8 us -> none
    ppermute x0 -> x17, waiting for transfers between devices: none -> 76.1 us  [shift(): lax.ppermute(value, axis, [(i, (i + step) % size) for i in range(size)])]
    gather x28 -> x0, local copies, waits for them, and re-layouts: 74.3 us -> none  [the longest x24 42.3 us: pick_tiles(): gathered = tile_rows[chosen]]
    pallas_call x0 -> x2, Pallas kernels: none -> 67.2 us  [the longest x1 34.1 us: run_k2(): pl.pallas_call(k2, grid_spec=pltpu.PrefetchScalarGridSpec(num_scalar_pref...]
  transfers between devices with their start and end apart: 8 -> 22, of which waited for: 5 -> 12; matrix products, arithmetic and copies ran while one was open for 49% -> 23% of each run, Pallas kernels for 0% -> 25%
where the time goes in v1:
time: 274 us; the launch traced here: 272 us
  waiting for transfers between devices  84.2 us (31%)
  Pallas kernels  67.2 us (25%)
  local copies, waits for them, and re-layouts  46.8 us (17%)
  starting transfers between devices  45.6 us (17%)
  other arithmetic  14.8 us (5%)
  matrix products  12.8 us (5%)
    ppermute x17, waiting for transfers between devices, shift(): lax.ppermute(value, axis, [(i, (i + step) % size) for i in range(size)])  76.1 us
    pallas_call x1, Pallas kernels, run_k2(): pl.pallas_call(k2, grid_spec=pltpu.PrefetchScalarGridSpec(num_scalar_pref...  34.1 us
    pallas_call x1, Pallas kernels, run_k1(): pl.pallas_call(k1, grid_spec=pltpu.PrefetchScalarGridSpec(num_scalar_pref...  33.1 us
    ppermute x17, starting transfers between devices, shift(): lax.ppermute(value, axis, [(i, (i + step) % size) for i in range(size)])  23.3 us
    dynamic_update_slice x12, local copies, waits for them, and re-layouts, gather_ring(): out = lax.dynamic_update_index_in_dim(out, part, (me - d) % size, 0)  15.8 us
    unnamed x26, local copies, waits for them, and re-layouts  12.4 us
    all_to_all x1, starting transfers between devices, local(): lax.all_to_all(att.reshape(8, 432, HD), CHIPS, split_axis=0, concat_axis=...  5.54 us
  transfers between devices with their start and end apart: 22, of which 12 were waited for; matrix products, arithmetic and copies ran while one was open for 23% of the time, Pallas kernels for 25%

profile of v1, /device:TPU:0, one launch (start us, length us, event | category | flops | bytes accessed | tf_op | source)
XLA Modules:
  0.0 272.4 jit_solution(3872698439203372091)
XLA Ops:
  0.6 1.7 collective-permute-start
  2.4 2.9 %collective-permute-start.1 = (bf16[16,2048]{1,0:T(8,128)(2,1)}, bf16[16,2048]{1,0:T(8,128)(2,1)}, u32[]{:S(2)}, u32[]{:S(2)}) collective-permute-start(bf16[16,2048]{1,0:T(8,128)(2,1)} %param.10), channel_id=1, source_target_pairs={{0,64},{32,96},{64,0},{96,32},{1,65},{33,97},{65,1},{97,33},{2,66}... | collective-permute-start | bytes 196616 | tf_op jit(solution)/shard_map/ppermute | solution.py:128
  5.3 1.3 collective-permute-start.2
  8.0 1.3 copy.47
  10.6 1.3 copy.46
  14.8 1.9 collective-permute-start.3
  18.3 3.9 %collective-permute-done.3 = bf16[4,16,2048]{2,1,0:T(8,128)(2,1)S(1)} collective-permute-done((bf16[4,16,2048]{2,1,0:T(8,128)(2,1)S(1)}, bf16[4,16,2048]{2,1,0:T(8,128)(2,1)S(1)}, u32[]{:S(2)}, u32[]{:S(2)}) %collective-permute-start.3) | collective-permute-done | bytes 262176 | tf_op jit(solution)/shard_map/ppermute | solution.py:128
  22.9 3.7 %collective-permute-start.4 = (bf16[2,4,16,2048]{3,2,0,1:T(8,128)(2,1)}, bf16[2,4,16,2048]{3,2,0,1:T(8,128)(2,1)}, u32[]{:S(2)}, u32[]{:S(2)}) collective-permute-start(bf16[2,4,16,2048]{3,2,0,1:T(8,128)(2,1)} %bitcast_dynamic-update-slice_fusion.7), channel_id=1, source_target_pairs={{0,1},{1,0},{2,3},{3,2},{4,5},{5,4},{6,7},{7,6},{8,9},{9,8},{10,11... | collective-permute-start | bytes 1572872 | tf_op jit(solution)/shard_map/ppermute | solution.py:128
  26.6 1.8 pad_maximum_fusion
  28.4 3.9 %all-to-all-start = ((bf16[16,3,216,128]{3,2,1,0:T(8,128)(2,1)}), bf16[16,3,216,128]{3,2,1,0:T(8,128)(2,1)S(1)}, u32[]{:S(2)}, u32[]{:S(2)}) async-start(bf16[16,3,216,128]{3,2,1,0:T(8,128)(2,1)} %pad_maximum_fusion), calls=%async_computation | async-start | bytes 5308416 | tf_op jit(solution)/shard_map/all_to_all | solution.py:182
  33.7 1.9 bitcast_dynamic-update-slice_fusion.4
  35.6 7.3 %collective-permute-done.4 = bf16[2,4,16,2048]{3,2,0,1:T(8,128)(2,1)} collective-permute-done((bf16[2,4,16,2048]{3,2,0,1:T(8,128)(2,1)}, bf16[2,4,16,2048]{3,2,0,1:T(8,128)(2,1)}, u32[]{:S(2)}, u32[]{:S(2)}) %collective-permute-start.4) | collective-permute-done | bytes 524320 | tf_op jit(solution)/shard_map/ppermute | solution.py:128
  42.9 1.9 bitcast_dynamic-update-slice_fusion.5
  44.8 1.5 collective-permute-start.5
  47.8 2.7 %collective-permute-start.6 = (bf16[2,2,4,16,2048]{4,3,0,1,2:T(8,128)(2,1)}, bf16[2,2,4,16,2048]{4,3,0,1,2:T(8,128)(2,1)S(1)}, u32[]{:S(2)}, u32[]{:S(2)}) collective-permute-start(bf16[2,2,4,16,2048]{4,3,0,1,2:T(8,128)(2,1)} %bitcast_dynamic-update-slice_fusion.5), channel_id=1, source_target_pairs={{0,4},{2,6},{4,0},{6,2},{1,5},{3,7},{5,1},{7,3},{8,12},{10,14},{12... | collective-permute-start | bytes 3145736 | tf_op jit(solution)/shard_map/ppermute | solution.py:128
  50.5 1.4 collective-permute-start.7
  51.9 2.6 broadcast_in_dim.55
  54.5 2.3 bitcast_dynamic-update-slice_fusion.2
  56.8 2.5 broadcast_select_fusion.1
  59.3 12.2 %collective-permute-done.5 = bf16[2,2,4,16,2048]{4,3,0,1,2:T(8,128)(2,1)} collective-permute-done((bf16[2,2,4,16,2048]{4,3,0,1,2:T(8,128)(2,1)}, bf16[2,2,4,16,2048]{4,3,0,1,2:T(8,128)(2,1)}, u32[]{:S(2)}, u32[]{:S(2)}) %collective-permute-start.5) | collective-permute-done | bytes 1048608 | tf_op jit(solution)/shard_map/ppermute | solution.py:128
  71.5 2.3 bitcast_dynamic-update-slice_fusion.1
  73.8 13.9 %collective-permute-done.6 = bf16[2,2,4,16,2048]{4,3,0,1,2:T(8,128)(2,1)S(1)} collective-permute-done((bf16[2,2,4,16,2048]{4,3,0,1,2:T(8,128)(2,1)}, bf16[2,2,4,16,2048]{4,3,0,1,2:T(8,128)(2,1)S(1)}, u32[]{:S(2)}, u32[]{:S(2)}) %collective-permute-start.6) | collective-permute-done | bytes 1048608 | tf_op jit(solution)/shard_map/ppermute | solution.py:128
  88.7 1.5 copy-done
  90.2 33.1 %attend.1 = (bf16[16,216,128]{2,1,0:T(8,128)(2,1)}, bf16[3456,128]{1,0:T(8,128)(2,1)}, bf16[3456,128]{1,0:T(8,128)(2,1)}, bf16[3456,128]{1,0:T(8,128)(2,1)}, f32...) custom-call(s32[3456]{0:T(1024)} %order_ref.3, s32[162]{0:T(256)} %reshape.41.neigh_ref, ...), custom_call_target="tpu_custom_call" | custom-call | tf_op jit(solution)/shard_map/attend/pallas_call | solution.py:61
  123.3 5.5 %all-to-all-start.1 = ((bf16[8,432,128]{2,1,0:T(8,128)(2,1)}), bf16[8,432,128]{2,1,0:T(8,128)(2,1)S(1)}, u32[]{:S(2)}, u32[]{:S(2)}) async-start(bf16[8,432,128]{2,1,0:T(8,128)(2,1)} %bitcast.131), calls=%async_computation.1 | async-start | bytes 1769472 | tf_op jit(solution)/shard_map/all_to_all | solution.py:198
  128.9 2.3 bitcast_dynamic-update-slice_fusion.3
  131.2 4.8 %fusion.2 = bf16[54,8,8,128]{3,2,1,0:T(8,128)(2,1)S(1)} fusion(bf16[1024,2048]{1,0:T(8,128)(2,1)} %bitcast.26, bf16[216,2048]{1,0:T(8,128)(2,1)} %get-tuple-element.25, bf16[216,2048]{1,0:T(8,128)(2,1)} %get-tuple-element.24), kind=kOutput, calls=%fused_computation.11 | convolution fusion | flops 1815920640 | bytes 6848512 | tf_op jit(solution)/shard_map/dot_general | solution.py:191
  137.1 5.1 %all-to-all-done.1 = bf16[8,432,128]{2,1,0:T(8,128)(2,1)S(1)} async-done(((bf16[8,432,128]{2,1,0:T(8,128)(2,1)}), bf16[8,432,128]{2,1,0:T(8,128)(2,1)S(1)}, u32[]{:S(2)}, u32[]{:S(2)}) %all-to-all-start.1) | async-done | bytes 884768 | tf_op jit(solution)/shard_map/all_to_all | solution.py:198
  142.2 3.9 %all-to-all-start.2 = ((bf16[8,432,128]{2,1,0:T(8,128)(2,1)}), bf16[8,432,128]{2,1,0:T(8,128)(2,1)S(1)}, u32[]{:S(2)}, u32[]{:S(2)}) async-start(bf16[8,432,128]{2,1,0:T(8,128)(2,1)} %bitcast.120), calls=%async_computation.2 | async-start | bytes 1769472 | tf_op jit(solution)/shard_map/all_to_all | solution.py:195
  146.2 1.3 copy.42
  147.5 3.8 %fusion = f32[8,4,2,16,2048]{4,3,2,1,0:T(8,128)S(1)} fusion(bf16[8,4,2,16,432]{4,3,2,1,0:T(8,128)(2,1)} %bitcast.127, bf16[216,2048]{1,0:T(8,128)(2,1)} %get-tuple-element.25, bf16[216,2048]{1,0:T(8,128)(2,1)S(1)} %copy-done.9), kind=kOutput, calls=%fused_computation.6 | convolution fusion | flops 1815478272 | bytes 11042816 | tf_op jit(solution)/shard_map/dot_general | solution.py:208
  151.3 3.2 %copy-done.1 = f32[8,4,2,16,2048]{4,3,2,1,0:T(8,128)} copy-done((f32[8,4,2,16,2048]{4,3,2,1,0:T(8,128)}, f32[8,4,2,16,2048]{4,3,2,1,0:T(8,128)S(1)}, u32[]{:S(2)}) %copy-start.1) | copy-done | bytes 8388632
  155.8 2.8 %all-to-all-done.2 = bf16[8,432,128]{2,1,0:T(8,128)(2,1)S(1)} async-done(((bf16[8,432,128]{2,1,0:T(8,128)(2,1)}), bf16[8,432,128]{2,1,0:T(8,128)(2,1)S(1)}, u32[]{:S(2)}, u32[]{:S(2)}) %all-to-all-start.2) | async-done | bytes 884768 | tf_op jit(solution)/shard_map/all_to_all | solution.py:195
  159.5 34.1 %attend_grad.1 = bf16[16,3,216,128]{3,2,1,0:T(8,128)(2,1)} custom-call(s32[3456]{0:T(1024)} %order_ref.3, s32[162]{0:T(256)} %reshape.41.neigh_ref, bf16[16,216,128]{2,1,0:T(8,128)(2,1)} %bitcast.125, bf16[3456,128]{1,0:T(8,128)(2,1)} %get-tuple-element.13.qp_ref, bf16[3456,128]{1,0:T(8,128)(2,1)} %get-tuple-element.14.kp_ref, ...), custom_call_target="tpu_custom_call" | custom-call | tf_op jit(solution)/shard_map/attend_grad/pallas_call | solution.py:111
  193.6 3.7 %all-to-all-start.3 = ((bf16[16,3,216,128]{3,2,1,0:T(8,128)(2,1)}), bf16[16,3,216,128]{3,2,1,0:T(8,128)(2,1)S(1)}, u32[]{:S(2)}, u32[]{:S(2)}) async-start(bf16[16,3,216,128]{3,2,1,0:T(8,128)(2,1)} %attend_grad.1), calls=%async_computation.3 | async-start | bytes 5308416 | tf_op jit(solution)/shard_map/all_to_all | solution.py:201
  198.5 2.5 dynamic-slice_bitcast_fusion.1
  201.2 3.3 %collective-permute-start.12 = (bf16[8,2,16,1024]{3,2,1,0:T(8,128)(2,1)S(1)}, bf16[8,2,16,1024]{3,2,1,0:T(8,128)(2,1)S(1)}, u32[]{:S(2)}, u32[]{:S(2)}) collective-permute-start(bf16[8,2,16,1024]{3,2,1,0:T(8,128)(2,1)S(1)} %slice.59), channel_id=1, source_target_pairs={{0,6},{2,0},{4,2},{6,4},{1,7},{3,1},{5,3},{7,5},{8,14},{10,8},{12,... | collective-permute-start | bytes 1572872 | tf_op jit(solution)/shard_map/ppermute | solution.py:128
  206.7 6.8 %collective-permute-done.10 = bf16[8,2,16,1024]{3,2,1,0:T(8,128)(2,1)S(1)} collective-permute-done((bf16[8,2,16,1024]{3,2,1,0:T(8,128)(2,1)}, bf16[8,2,16,1024]{3,2,1,0:T(8,128)(2,1)S(1)}, u32[]{:S(2)}, u32[]{:S(2)}) %collective-permute-start.10) | collective-permute-done | bytes 524320 | tf_op jit(solution)/shard_map/ppermute | solution.py:128
  213.8 4.2 %fusion.8 = f32[432,2048]{1,0:T(8,128)S(1)} fusion(bf16[1024,2048]{1,0:T(8,128)(2,1)} %bitcast.26, bf16[8,432,128]{2,1,0:T(8,128)(2,1)S(1)} %all-to-all-done.1), kind=kOutput, calls=%fused_computation.30 | convolution fusion | flops 1811939328 | bytes 8617984 | tf_op jit(solution)/shard_map/dot_general | solution.py:203
  218.0 6.8 %collective-permute-done.13 = bf16[8,2,16,1024]{3,2,1,0:T(8,128)(2,1)S(1)} collective-permute-done((bf16[8,2,16,1024]{3,2,1,0:T(8,128)(2,1)S(1)}, bf16[8,2,16,1024]{3,2,1,0:T(8,128)(2,1)S(1)}, u32[]{:S(2)}, u32[]{:S(2)}) %collective-permute-start.13) | collective-permute-done | bytes 524320 | tf_op jit(solution)/shard_map/ppermute | solution.py:128
  224.8 2.0 collective-permute-done.15
  227.1 8.3 %collective-permute-done.11 = bf16[8,2,16,1024]{3,2,1,0:T(8,128)(2,1)S(1)} collective-permute-done((bf16[8,2,16,1024]{3,2,1,0:T(8,128)(2,1)S(1)}, bf16[8,2,16,1024]{3,2,1,0:T(8,128)(2,1)S(1)}, u32[]{:S(2)}, u32[]{:S(2)}) %collective-permute-start.11) | collective-permute-done | bytes 524320 | tf_op jit(solution)/shard_map/ppermute | solution.py:128
  235.5 1.9 maximum_add_fusion
  239.9 14.8 %collective-permute-done.16 = bf16[8,16,2048]{2,1,0:T(8,128)(2,1)} collective-permute-done((bf16[8,16,2048]{2,1,0:T(8,128)(2,1)}, bf16[8,16,2048]{2,1,0:T(8,128)(2,1)}, u32[]{:S(2)}, u32[]{:S(2)}) %collective-permute-start.16) | collective-permute-done | bytes 524320 | tf_op jit(solution)/shard_map/ppermute | solution.py:128
  254.7 2.3 fusion.6
  257.0 5.3 %all-to-all-start.4 = ((bf16[8,16,2048]{2,1,0:T(8,128)(2,1)}), bf16[8,16,2048]{2,1,0:T(8,128)(2,1)}, u32[]{:S(2)}, u32[]{:S(2)}) async-start(bf16[8,16,2048]{2,1,0:T(8,128)(2,1)} %fusion.6), calls=%async_computation.4 | async-start | bytes 1048576 | tf_op jit(solution)/shard_map/all_to_all | solution.py:170
  262.3 2.9 %fusion.7 = bf16[1,216,2048]{2,1,0:T(8,128)(2,1)} fusion(bf16[216,2048]{1,0:T(8,128)(2,1)} %collective-permute-done.8, f32[432,2048]{1,0:T(8,128)} %copy-done.5, s32[]{:T(128)S(6)} %select_n.165), kind=kLoop, calls=%fused_computation.28 | loop fusion | flops 1327104 | bytes 3538948 | tf_op jit(solution)/shard_map/broadcast_in_dim | solution.py:217
  270.7 1.8 reduce_sum.12
  (73 shorter events, 26.9 us)
Async XLA Ops:
  0.6 8.7 %copy-start.10 = (bf16[16,2048]{1,0:T(8,128)(2,1)S(1)}, bf16[16,2048]{1,0:T(8,128)(2,1)}, u32[]{:S(2)}) copy-start(bf16[16,2048]{1,0:T(8,128)(2,1)} %param.10) | copy-start | bytes 196612
  0.6 11.6 %collective-permute-start = (bf16[16,2048]{1,0:T(8,128)(2,1)}, bf16[16,2048]{1,0:T(8,128)(2,1)}, u32[]{:S(2)}, u32[]{:S(2)}) collective-permute-start(bf16[16,2048]{1,0:T(8,128)(2,1)} %param.10), channel_id=1, source_target_pairs={{0,32},{32,64},{64,96},{96,0},{1,33},{33,65},{65,97},{97,1},{2,34}... | collective-permute-start | bytes 196616 | tf_op jit(solution)/shard_map/ppermute | solution.py:128
  2.4 10.7 %collective-permute-start.1 = (bf16[16,2048]{1,0:T(8,128)(2,1)}, bf16[16,2048]{1,0:T(8,128)(2,1)}, u32[]{:S(2)}, u32[]{:S(2)}) collective-permute-start(bf16[16,2048]{1,0:T(8,128)(2,1)} %param.10), channel_id=1, source_target_pairs={{0,64},{32,96},{64,0},{96,32},{1,65},{33,97},{65,1},{97,33},{2,66}... | collective-permute-start | bytes 196616 | tf_op jit(solution)/shard_map/ppermute | solution.py:128
  5.3 8.7 %collective-permute-start.2 = (bf16[16,2048]{1,0:T(8,128)(2,1)}, bf16[16,2048]{1,0:T(8,128)(2,1)}, u32[]{:S(2)}, u32[]{:S(2)}) collective-permute-start(bf16[16,2048]{1,0:T(8,128)(2,1)} %param.10), channel_id=1, source_target_pairs={{0,96},{32,0},{64,32},{96,64},{1,97},{33,1},{65,33},{97,65},{2,98}... | collective-permute-start | bytes 196616 | tf_op jit(solution)/shard_map/ppermute | solution.py:128
  9.4 0.7 copy-start.6
  10.5 1.7 copy-start.7
  14.8 7.4 %collective-permute-start.3 = (bf16[4,16,2048]{2,1,0:T(8,128)(2,1)S(1)}, bf16[4,16,2048]{2,1,0:T(8,128)(2,1)S(1)}, u32[]{:S(2)}, u32[]{:S(2)}) collective-permute-start(bf16[4,16,2048]{2,1,0:T(8,128)(2,1)S(1)} %bitcast_dynamic-update-slice_fusion.8), channel_id=1, source_target_pairs={{0,16},{16,0},{1,17},{17,1},{2,18},{18,2},{3,19},{19,3},{4,20},{20... | collective-permute-start | bytes 786440 | tf_op jit(solution)/shard_map/ppermute | solution.py:128
  22.9 20.0 %collective-permute-start.4 = (bf16[2,4,16,2048]{3,2,0,1:T(8,128)(2,1)}, bf16[2,4,16,2048]{3,2,0,1:T(8,128)(2,1)}, u32[]{:S(2)}, u32[]{:S(2)}) collective-permute-start(bf16[2,4,16,2048]{3,2,0,1:T(8,128)(2,1)} %bitcast_dynamic-update-slice_fusion.7), channel_id=1, source_target_pairs={{0,1},{1,0},{2,3},{3,2},{4,5},{5,4},{6,7},{7,6},{8,9},{9,8},{10,11... | collective-permute-start | bytes 1572872 | tf_op jit(solution)/shard_map/ppermute | solution.py:128
  28.4 3.9 %copy-start.8 = (bf16[1,216,2048]{2,1,0:T(8,128)(2,1)S(1)}, bf16[1,216,2048]{2,1,0:T(8,128)(2,1)}, u32[]{:S(2)}) copy-start(bf16[1,216,2048]{2,1,0:T(8,128)(2,1)} %param.11) | copy-start | bytes 2654212
  28.4 60.4 %all-to-all-start = ((bf16[16,3,216,128]{3,2,1,0:T(8,128)(2,1)}), bf16[16,3,216,128]{3,2,1,0:T(8,128)(2,1)S(1)}, u32[]{:S(2)}, u32[]{:S(2)}) async-start(bf16[16,3,216,128]{3,2,1,0:T(8,128)(2,1)} %pad_maximum_fusion), calls=%async_computation | async-start | bytes 5308416 | tf_op jit(solution)/shard_map/all_to_all | solution.py:182
  32.3 24.5 %collective-permute-start.9 = (bf16[216,2048]{1,0:T(8,128)(2,1)S(1)}, bf16[216,2048]{1,0:T(8,128)(2,1)}, u32[]{:S(2)}, u32[]{:S(2)}) collective-permute-start(bf16[216,2048]{1,0:T(8,128)(2,1)S(1)} %bitcast.132), channel_id=1, source_target_pairs={{0,8},{8,0},{1,9},{9,1},{2,10},{10,2},{3,11},{11,3},{4,12},{12,4},... | collective-permute-start | bytes 2654216 | tf_op jit(solution)/shard_map/ppermute | solution.py:128
  44.8 26.6 %collective-permute-start.5 = (bf16[2,2,4,16,2048]{4,3,0,1,2:T(8,128)(2,1)}, bf16[2,2,4,16,2048]{4,3,0,1,2:T(8,128)(2,1)}, u32[]{:S(2)}, u32[]{:S(2)}) collective-permute-start(bf16[2,2,4,16,2048]{4,3,0,1,2:T(8,128)(2,1)} %bitcast_dynamic-update-slice_fusion.5), channel_id=1, source_target_pairs={{0,2},{2,4},{4,6},{6,0},{1,3},{3,5},{5,7},{7,1},{8,10},{10,12},{12... | collective-permute-start | bytes 3145736 | tf_op jit(solution)/shard_map/ppermute | solution.py:128
  47.8 39.9 %collective-permute-start.6 = (bf16[2,2,4,16,2048]{4,3,0,1,2:T(8,128)(2,1)}, bf16[2,2,4,16,2048]{4,3,0,1,2:T(8,128)(2,1)S(1)}, u32[]{:S(2)}, u32[]{:S(2)}) collective-permute-start(bf16[2,2,4,16,2048]{4,3,0,1,2:T(8,128)(2,1)} %bitcast_dynamic-update-slice_fusion.5), channel_id=1, source_target_pairs={{0,4},{2,6},{4,0},{6,2},{1,5},{3,7},{5,1},{7,3},{8,12},{10,14},{12... | collective-permute-start | bytes 3145736 | tf_op jit(solution)/shard_map/ppermute | solution.py:128
  50.5 78.4 %collective-permute-start.7 = (bf16[2,2,4,16,2048]{4,3,0,1,2:T(8,128)(2,1)}, bf16[2,2,4,16,2048]{4,3,0,1,2:T(8,128)(2,1)}, u32[]{:S(2)}, u32[]{:S(2)}) collective-permute-start(bf16[2,2,4,16,2048]{4,3,0,1,2:T(8,128)(2,1)} %bitcast_dynamic-update-slice_fusion.5), channel_id=1, source_target_pairs={{0,6},{2,0},{4,2},{6,4},{1,7},{3,1},{5,3},{7,5},{8,14},{10,8},{12,... | collective-permute-start | bytes 3145736 | tf_op jit(solution)/shard_map/ppermute | solution.py:128
  88.7 1.5 copy-start
  123.3 18.8 %all-to-all-start.1 = ((bf16[8,432,128]{2,1,0:T(8,128)(2,1)}), bf16[8,432,128]{2,1,0:T(8,128)(2,1)S(1)}, u32[]{:S(2)}, u32[]{:S(2)}) async-start(bf16[8,432,128]{2,1,0:T(8,128)(2,1)} %bitcast.131), calls=%async_computation.1 | async-start | bytes 1769472 | tf_op jit(solution)/shard_map/all_to_all | solution.py:198
  142.2 5.3 %copy-start.9 = (bf16[216,2048]{1,0:T(8,128)(2,1)S(1)}, bf16[216,2048]{1,0:T(8,128)(2,1)}, u32[]{:S(2)}) copy-start(bf16[216,2048]{1,0:T(8,128)(2,1)} %get-tuple-element.24) | copy-start | bytes 2654212
  142.2 16.4 %all-to-all-start.2 = ((bf16[8,432,128]{2,1,0:T(8,128)(2,1)}), bf16[8,432,128]{2,1,0:T(8,128)(2,1)S(1)}, u32[]{:S(2)}, u32[]{:S(2)}) async-start(bf16[8,432,128]{2,1,0:T(8,128)(2,1)} %bitcast.120), calls=%async_computation.2 | async-start | bytes 1769472 | tf_op jit(solution)/shard_map/all_to_all | solution.py:195
  151.3 3.2 %copy-start.1 = (f32[8,4,2,16,2048]{4,3,2,1,0:T(8,128)}, f32[8,4,2,16,2048]{4,3,2,1,0:T(8,128)S(1)}, u32[]{:S(2)}) copy-start(f32[8,4,2,16,2048]{4,3,2,1,0:T(8,128)S(1)} %fusion) | copy-start | bytes 25165828
  155.8 48.7 %collective-permute-start.14 = (bf16[8,2,16,1024]{3,2,1,0:T(8,128)(2,1)}, bf16[8,2,16,1024]{3,2,1,0:T(8,128)(2,1)}, u32[]{:S(2)}, u32[]{:S(2)}) collective-permute-start(bf16[8,2,16,1024]{3,2,1,0:T(8,128)(2,1)} %get-tuple-element.27), channel_id=1, source_target_pairs={{0,6},{2,0},{4,2},{6,4},{1,7},{3,1},{5,3},{7,5},{8,14},{10,8},{12,... | collective-permute-start | bytes 1572872 | tf_op jit(solution)/shard_map/ppermute | solution.py:128
  158.6 0.9 copy-start.3
  193.6 63.4 %all-to-all-start.3 = ((bf16[16,3,216,128]{3,2,1,0:T(8,128)(2,1)}), bf16[16,3,216,128]{3,2,1,0:T(8,128)(2,1)S(1)}, u32[]{:S(2)}, u32[]{:S(2)}) async-start(bf16[16,3,216,128]{3,2,1,0:T(8,128)(2,1)} %attend_grad.1), calls=%async_computation.3 | async-start | bytes 5308416 | tf_op jit(solution)/shard_map/all_to_all | solution.py:201
  197.3 16.2 %collective-permute-start.10 = (bf16[8,2,16,1024]{3,2,1,0:T(8,128)(2,1)}, bf16[8,2,16,1024]{3,2,1,0:T(8,128)(2,1)S(1)}, u32[]{:S(2)}, u32[]{:S(2)}) collective-permute-start(bf16[8,2,16,1024]{3,2,1,0:T(8,128)(2,1)} %get-tuple-element.26), channel_id=1, source_target_pairs={{0,2},{2,4},{4,6},{6,0},{1,3},{3,5},{5,7},{7,1},{8,10},{10,12},{12... | collective-permute-start | bytes 1572872 | tf_op jit(solution)/shard_map/ppermute | solution.py:128
  201.0 23.8 %collective-permute-start.13 = (bf16[8,2,16,1024]{3,2,1,0:T(8,128)(2,1)S(1)}, bf16[8,2,16,1024]{3,2,1,0:T(8,128)(2,1)S(1)}, u32[]{:S(2)}, u32[]{:S(2)}) collective-permute-start(bf16[8,2,16,1024]{3,2,1,0:T(8,128)(2,1)S(1)} %slice.58), channel_id=1, source_target_pairs={{0,2},{2,4},{4,6},{6,0},{1,3},{3,5},{5,7},{7,1},{8,10},{10,12},{12... | collective-permute-start | bytes 1572872 | tf_op jit(solution)/shard_map/ppermute | solution.py:128
  201.2 25.8 %collective-permute-start.12 = (bf16[8,2,16,1024]{3,2,1,0:T(8,128)(2,1)S(1)}, bf16[8,2,16,1024]{3,2,1,0:T(8,128)(2,1)S(1)}, u32[]{:S(2)}, u32[]{:S(2)}) collective-permute-start(bf16[8,2,16,1024]{3,2,1,0:T(8,128)(2,1)S(1)} %slice.59), channel_id=1, source_target_pairs={{0,6},{2,0},{4,2},{6,4},{1,7},{3,1},{5,3},{7,5},{8,14},{10,8},{12,... | collective-permute-start | bytes 1572872 | tf_op jit(solution)/shard_map/ppermute | solution.py:128
  205.7 21.2 %collective-permute-start.15 = (bf16[8,2,16,1024]{3,2,1,0:T(8,128)(2,1)S(1)}, bf16[8,2,16,1024]{3,2,1,0:T(8,128)(2,1)S(1)}, u32[]{:S(2)}, u32[]{:S(2)}) collective-permute-start(bf16[8,2,16,1024]{3,2,1,0:T(8,128)(2,1)S(1)} %fusion.4), channel_id=1, source_target_pairs={{0,6},{2,0},{4,2},{6,4},{1,7},{3,1},{5,3},{7,5},{8,14},{10,8},{12,... | collective-permute-start | bytes 1572872 | tf_op jit(solution)/shard_map/ppermute | solution.py:128
  213.7 21.6 %collective-permute-start.11 = (bf16[8,2,16,1024]{3,2,1,0:T(8,128)(2,1)S(1)}, bf16[8,2,16,1024]{3,2,1,0:T(8,128)(2,1)S(1)}, u32[]{:S(2)}, u32[]{:S(2)}) collective-permute-start(bf16[8,2,16,1024]{3,2,1,0:T(8,128)(2,1)S(1)} %fusion.5), channel_id=1, source_target_pairs={{0,2},{2,4},{4,6},{6,0},{1,3},{3,5},{5,7},{7,1},{8,10},{10,12},{12... | collective-permute-start | bytes 1572872 | tf_op jit(solution)/shard_map/ppermute | solution.py:128
  218.0 21.7 %copy-start.5 = (f32[432,2048]{1,0:T(8,128)}, f32[432,2048]{1,0:T(8,128)S(1)}, u32[]{:S(2)}) copy-start(f32[432,2048]{1,0:T(8,128)S(1)} %fusion.8) | copy-start | bytes 10616836
  237.5 1.3 copy-start.2
  239.7 15.1 %collective-permute-start.16 = (bf16[8,16,2048]{2,1,0:T(8,128)(2,1)}, bf16[8,16,2048]{2,1,0:T(8,128)(2,1)}, u32[]{:S(2)}, u32[]{:S(2)}) collective-permute-start(bf16[8,16,2048]{2,1,0:T(8,128)(2,1)} %fusion.11), channel_id=1, source_target_pairs={{0,1},{1,0},{2,3},{3,2},{4,5},{5,4},{6,7},{7,6},{8,9},{9,8},{10,11... | collective-permute-start | bytes 1572872 | tf_op jit(solution)/shard_map/ppermute | solution.py:128
  239.8 22.5 %collective-permute-start.8 = (bf16[216,2048]{1,0:T(8,128)(2,1)S(1)}, bf16[216,2048]{1,0:T(8,128)(2,1)}, u32[]{:S(2)}, u32[]{:S(2)}) collective-permute-start(bf16[216,2048]{1,0:T(8,128)(2,1)S(1)} %dynamic-slice_convert_fusion.1), channel_id=1, source_target_pairs={{0,8},{8,0},{1,9},{9,1},{2,10},{10,2},{3,11},{11,3},{4,12},{12,4},... | collective-permute-start | bytes 2654216 | tf_op jit(solution)/shard_map/ppermute | solution.py:128
  257.0 13.7 %all-to-all-start.4 = ((bf16[8,16,2048]{2,1,0:T(8,128)(2,1)}), bf16[8,16,2048]{2,1,0:T(8,128)(2,1)}, u32[]{:S(2)}, u32[]{:S(2)}) async-start(bf16[8,16,2048]{2,1,0:T(8,128)(2,1)} %fusion.6), calls=%async_computation.4 | async-start | bytes 1048576 | tf_op jit(solution)/shard_map/all_to_all | solution.py:170
  266.3 1.4 copy-start.4

commit v2 on v1

--- a/solution.py
+++ b/solution.py
@@ -12,6 +12,7 @@
 bf=jnp.bfloat16; f32=jnp.float32
 SC=1.0/math.sqrt(HD); LOG2E=math.log2(math.e)
 PITCH=4
+COST=pl.CostEstimate(flops=30*10**9,bytes_accessed=20*10**6,transcendentals=0)
 
 def permute_rows(order_ref, src, dst, width, scatter, unroll=16):
     def body(i, c):
@@ -23,7 +24,7 @@
         return c
     lax.fori_loop(0,N//unroll,body,0)
 
-def k1(order_ref, neigh_ref, qkv_ref, att_ref, qp_ref, kp_ref, vp_ref, o_ref, rinv_ref, e_ref, tok, per, kc, vc, s_ref):
+def k1(order_ref, neigh_ref, turn_ref, qkv_ref, att_ref, qp_ref, kp_ref, vp_ref, o_ref, rinv_ref, e_ref, tok, per, kc, vc, s_ref):
     t=pl.program_id(0)
     @pl.when(t==0)
     def _():
@@ -54,26 +55,26 @@
     def _():
         permute_rows(order_ref,o_ref,tok,1,True)
         for s in range(16):
-            att_ref[s]=tok[pl.ds(s*216,216),:].astype(bf)
-
-def run_k1(order, neigh, qkv):
+            att_ref[s]=pltpu.roll(tok[pl.ds(s*216,216),:],lax.rem(HD-turn_ref[0],HD),1).astype(bf)
+
+def run_k1(order, neigh, turn, qkv):
     full=lambda shape: pl.BlockSpec(shape,lambda t,*_:(0,)*len(shape))
     return pl.pallas_call(k1,
-      grid_spec=pltpu.PrefetchScalarGridSpec(num_scalar_prefetch=2,grid=(NT,),
+      grid_spec=pltpu.PrefetchScalarGridSpec(num_scalar_prefetch=3,grid=(NT,),
         in_specs=[full((16,3,216,HD))],
         out_specs=[full((16,216,HD)),full((N,HD)),full((N,HD)),full((N,HD)),full((N,HD)),
                    pl.BlockSpec((T,HD),lambda t,*_:(t,0)),pl.BlockSpec((1,T,KC),lambda t,*_:(t,0,0))],
         scratch_shapes=[pltpu.VMEM((N*PITCH,HD),f32),pltpu.VMEM((N*PITCH,HD),f32),pltpu.VMEM((KC,HD),bf),pltpu.VMEM((KC,HD),bf),pltpu.VMEM((T,KC),f32)]),
       out_shape=[jax.ShapeDtypeStruct((16,216,HD),bf)]+[jax.ShapeDtypeStruct((N,HD),bf)]*3+[jax.ShapeDtypeStruct((N,HD),f32),jax.ShapeDtypeStruct((N,HD),f32),jax.ShapeDtypeStruct((NT,T,KC),bf)],
       compiler_params=pltpu.CompilerParams(vmem_limit_bytes=60*1024*1024),
-      name="attend")(order,neigh,qkv)
-
-def k2(order_ref, neigh_ref, g_ref, qp_ref, kp_ref, vp_ref, o_ref, rinv_ref, e_ref, out_ref, tok, gp, acc, kc, vc):
+      cost_estimate=COST,name="attend")(order,neigh,turn,qkv)
+
+def k2(order_ref, neigh_ref, turn_ref, g_ref, qp_ref, kp_ref, vp_ref, o_ref, rinv_ref, e_ref, out_ref, tok, gp, acc, kc, vc):
     t=pl.program_id(0)
     @pl.when(t==0)
     def _():
         for s in range(16):
-            tok[pl.ds(s*216,216),:]=g_ref[s].astype(f32)
+            tok[pl.ds(s*216,216),:]=pltpu.roll(g_ref[s].astype(f32),turn_ref[0],1)
         permute_rows(order_ref,tok,gp,1,False)
         for u in range(NT*PITCH):
             acc[pl.ds(u*T,T),:]=jnp.zeros((T,HD),f32)
@@ -106,17 +107,17 @@
             for j in range(3):
                 out_ref[s,j]=tok[pl.ds(s*216*PITCH+j,216,stride=PITCH),:].astype(bf)
 
-def run_k2(order, neigh, g, qp,kp,vp,o,rinv,e):
+def run_k2(order, neigh, turn, g, qp,kp,vp,o,rinv,e):
     full=lambda shape: pl.BlockSpec(shape,lambda t,*_:(0,)*len(shape))
     return pl.pallas_call(k2,
-      grid_spec=pltpu.PrefetchScalarGridSpec(num_scalar_prefetch=2,grid=(NT,),
+      grid_spec=pltpu.PrefetchScalarGridSpec(num_scalar_prefetch=3,grid=(NT,),
         in_specs=[full((16,216,HD)),full((N,HD)),full((N,HD)),full((N,HD)),full((N,HD)),
                    pl.BlockSpec((T,HD),lambda t,*_:(t,0)),pl.BlockSpec((1,T,KC),lambda t,*_:(t,0,0))],
         out_specs=full((16,3,216,HD)),
         scratch_shapes=[pltpu.VMEM((N*PITCH,HD),f32),pltpu.VMEM((N,HD),f32),pltpu.VMEM((N*PITCH,HD),f32),pltpu.VMEM((KC,HD),bf),pltpu.VMEM((KC,HD),bf)]),
       out_shape=jax.ShapeDtypeStruct((16,3,216,HD),bf),
       compiler_params=pltpu.CompilerParams(vmem_limit_bytes=60*1024*1024),
-      name="attend_grad")(order,neigh,g,qp,kp,vp,o,rinv,e)
+      cost_estimate=COST,name="attend_grad")(order,neigh,turn,g,qp,kp,vp,o,rinv,e)
 
 
 CHIPS = ("y", "zl")
@@ -128,57 +129,63 @@
     return lax.ppermute(value, axis, [(i, (i + step) % size) for i in range(size)])
 
 
-def gather_ring(value, axis, size):
-    me = lax.axis_index(axis)
-    parts = [value] + [shift(value, axis, size, d) for d in range(1, size)]
-    out = jnp.zeros((size,) + value.shape, value.dtype)
-    for d, part in enumerate(parts):
-        out = lax.dynamic_update_index_in_dim(out, part, (me - d) % size, 0)
-    return out
-
-
-def gather_weight(own):
-    w = gather_ring(own, "y", 4)
-    w = gather_ring(w, "zl", 2)
-    w = gather_ring(w, "zh", 2)
-    w = gather_ring(w, "x", 4)
-    return w.transpose(3, 2, 0, 1, 4, 5).reshape(1024, 2048)
-
-
-def scatter_weight(part):
-    x, zh = lax.axis_index("x"), lax.axis_index("zh")
-
-    def piece(d):
-        return lax.dynamic_index_in_dim(part, (x + d) % 4, 1, keepdims=False)
-
-    far = piece(2).astype(bf)
-    up, down = piece(1), piece(3)
-    a = shift(far[..., :1024], "x", 4, 1)
-    b = shift(far[..., 1024:], "x", 4, -1)
-    up_low = shift(up[..., 1024:].astype(bf), "x", 4, 1)
-    down_low = shift(down[..., :1024].astype(bf), "x", 4, -1)
-    up_high = shift((up[..., :1024] + a.astype(f32)).astype(bf), "x", 4, 1)
-    down_high = shift((down[..., 1024:] + b.astype(f32)).astype(bf), "x", 4, -1)
+def in_place(axis, own, other):
+    low = lax.axis_index(axis) == 0
+    return jnp.concatenate([jnp.where(low, own, other), jnp.where(low, other, own)], axis=0)
+
+
+def around(value, axis):
+    half = value.shape[0] // 2
+    after, before = shift(value, axis, 4, -1), shift(value, axis, 4, 1)
+    far = [shift(after[:half], axis, 4, -1), shift(before[half:], axis, 4, 1)]
+    return [after, jnp.concatenate(far, axis=0), before]
+
+
+def gather_weight(own, qkv):
+    w = in_place("zh", own, shift(own, "zh", 2, 1))
+    w = in_place("zl", w[None], shift(w, "zl", 2, 1)[None])
+    y = lax.axis_index("y")
+    ring = jnp.stack([w] + around(w, "y"))
+    ring = jnp.concatenate([ring, ring], axis=0)
+    w = lax.dynamic_slice_in_dim(ring, 4 - y, 4, 0).reshape(8, 32, 2048)
+    w, qkv = lax.optimization_barrier((w, qkv))
+    return jnp.concatenate([w] + around(w, "x"), axis=1), qkv
+
+
+def scatter_weight(part, after_this):
+    def low(value):
+        return value.astype(bf)
+
+    own, after, far, before = (part[:, d] for d in range(4))
+    far_up = shift(low(far[:4]), "x", 4, 1)
+    far_down = shift(low(far[4:]), "x", 4, -1)
+    up_plain = shift(low(after[4:]), "x", 4, 1)
+    down_plain = shift(low(before[:4]), "x", 4, -1)
+    up_sum = shift(low(after[:4] + far_up.astype(f32)), "x", 4, 1)
+    down_sum = shift(low(before[4:] + far_down.astype(f32)), "x", 4, -1)
     got = jnp.concatenate(
-        [up_high.astype(f32) + down_low.astype(f32), up_low.astype(f32) + down_high.astype(f32)],
-        axis=-1,
-    )
-    rows = piece(0) + got
-    mine = lax.dynamic_index_in_dim(rows, zh, 1, keepdims=False)
-    other = lax.dynamic_index_in_dim(rows, 1 - zh, 1, keepdims=False)
-    rows = mine + shift(other.astype(bf), "zh", 2, 1).astype(f32)
-    rows = lax.all_to_all(rows.astype(bf), CHIPS, split_axis=0, concat_axis=0, tiled=True)
-    return jnp.sum(rows.astype(f32), axis=0).astype(bf)
+        [
+            up_sum.astype(f32) + down_plain.astype(f32),
+            up_plain.astype(f32) + down_sum.astype(f32),
+        ],
+        axis=0,
+    )
+    rows, after_this = lax.optimization_barrier((low(own + got).reshape(16, 16, 2048), after_this))
+    rows = lax.all_to_all(rows, ("y", "zl", "zh"), split_axis=0, concat_axis=0, tiled=True)
+    return low(jnp.sum(rows.astype(f32), axis=0)), after_this
 
 
 def local(queries, key_vectors, values, out_weight, cotangent, neighbours, tile_order):
     core = lax.axis_index("c")
+    turn = (lax.axis_index("x") * 32).astype(jnp.int32).reshape(1)
     neigh = neighbours.reshape(-1)
 
     def by_head(tensor):
         return tensor.reshape(216, 16, HD).transpose(1, 0, 2)
 
     qkv = jnp.stack([by_head(queries[0]), by_head(key_vectors[0]), by_head(values[0])], axis=1)
+    weight, qkv = gather_weight(out_weight, qkv)
+    weight = weight.reshape(1024, 2048)
     qkv = lax.all_to_all(qkv, SEQ, split_axis=0, concat_axis=0, tiled=True)
 
     cot = cotangent[0]
@@ -187,17 +194,19 @@
     cot_chip = jnp.concatenate(
         [jnp.where(first, cot, cot_other), jnp.where(first, cot_other, cot)], axis=0
     )
-    weight = gather_weight(out_weight)
     grad = lax.dot_general(
         cot_chip, weight, (((1,), (1,)), ((), ())), preferred_element_type=f32
     ).astype(bf)
     grad = grad.reshape(432, 8, HD).transpose(1, 0, 2)
+    grad, qkv = lax.optimization_barrier((grad, qkv))
     grad = lax.all_to_all(grad, CHIPS, split_axis=0, concat_axis=0, tiled=True)
 
-    att, *saved = run_k1(tile_order, neigh, qkv)
+    att, *saved = run_k1(tile_order, neigh, turn, qkv)
+    att, grad = lax.optimization_barrier((att, grad))
     att = lax.all_to_all(att.reshape(8, 432, HD), CHIPS, split_axis=0, concat_axis=0, tiled=True)
     att = att.transpose(1, 0, 2).reshape(432, 1024)
-    grads = run_k2(tile_order, neigh, grad.reshape(16, 216, HD), *saved)
+    grads = run_k2(tile_order, neigh, turn, grad.reshape(16, 216, HD), *saved)
+    att, grads = lax.optimization_barrier((att, grads))
     grads = lax.all_to_all(grads, SEQ, split_axis=0, concat_axis=0, tiled=True)
 
     partial = jnp.dot(att, weight, preferred_element_type=f32)
@@ -208,7 +217,7 @@
     weight_part = lax.dot_general(
         att, cot_chip, (((0,), (0,)), ((), ())), preferred_element_type=f32
     )
-    grad_weight = scatter_weight(weight_part.reshape(8, 4, 2, 16, 2048))
+    grad_weight, grads = scatter_weight(weight_part.reshape(8, 4, 32, 2048), grads)
 
     def by_token(tensor):
         return tensor.transpose(1, 0, 2).reshape(1, 216, 2048)

time: 274 us -> 237 us (0.86)
  local copies, waits for them, and re-layouts: 46.8 us -> 17.7 us
  waiting for transfers between devices: 84.2 us -> 65.6 us
  starting transfers between devices: 45.6 us -> 58.2 us
  matrix products: 12.8 us -> 8.23 us
    ppermute x17 -> x18, waiting for transfers between devices: 76.1 us -> 42.8 us  [shift(): lax.ppermute(value, axis, [(i, (i + step) % size) for i in range(size)])]
    dynamic_update_slice x12 -> x0, local copies, waits for them, and re-layouts: 15.8 us -> none  [gather_ring(): out = lax.dynamic_update_index_in_dim(out, part, (me - d) % size, 0)]
    all_to_all x1, waiting for transfers between devices: 0.13 us -> 10.8 us  [scatter_weight(): lax.all_to_all(rows, ('y', 'zl', 'zh'), split_axis=0, concat_axis=0, tile...]
    all_to_all x1, waiting for transfers between devices: 0.01 us -> 8.23 us  [local(): grads = lax.all_to_all(grads, SEQ, split_axis=0, concat_axis=0, tiled=True)]
    unnamed x26 -> x39, local copies, waits for them, and re-layouts: 12.4 us -> 4.89 us
    all_to_all x1, waiting for transfers between devices: 5.13 us -> 0.01 us  [local(): lax.all_to_all(att.reshape(8, 432, HD), CHIPS, split_axis=0, concat_axis=...]
    ppermute x17 -> x18, starting transfers between devices: 23.3 us -> 27.9 us  [shift(): lax.ppermute(value, axis, [(i, (i + step) % size) for i in range(size)])]
    broadcast_in_dim x4 -> x0, local copies, waits for them, and re-layouts: 4.54 us -> none  [gather_ring(): out = jnp.zeros((size,) + value.shape, value.dtype)]
  transfers between devices with their start and end apart: 22 -> 23, of which waited for: 12 -> 13; matrix products, arithmetic and copies ran while one was open for 23% -> 15% of each run, Pallas kernels for 25% -> 29%
where the time goes in v2:
time: 237 us; the launch traced here: 236 us
  Pallas kernels  67.8 us (29%)
  waiting for transfers between devices  65.6 us (28%)
  starting transfers between devices  58.2 us (25%)
  local copies, waits for them, and re-layouts  17.7 us (7%)
  other arithmetic  17 us (7%)
  matrix products  8.23 us (3%)
    ppermute x18, waiting for transfers between devices, shift(): lax.ppermute(value, axis, [(i, (i + step) % size) for i in range(size)])  42.8 us
    pallas_call x1, Pallas kernels, run_k2(): pl.pallas_call(k2, grid_spec=pltpu.PrefetchScalarGridSpec(num_scalar_pref...  34.4 us
    pallas_call x1, Pallas kernels, run_k1(): pl.pallas_call(k1, grid_spec=pltpu.PrefetchScalarGridSpec(num_scalar_pref...  33.5 us
    ppermute x18, starting transfers between devices, shift(): lax.ppermute(value, axis, [(i, (i + step) % size) for i in range(size)])  27.9 us
    all_to_all x1, waiting for transfers between devices, scatter_weight(): lax.all_to_all(rows, ('y', 'zl', 'zh'), split_axis=0, concat_axis=0, tile...  10.8 us
    all_to_all x1, starting transfers between devices, scatter_weight(): lax.all_to_all(rows, ('y', 'zl', 'zh'), split_axis=0, concat_axis=0, tile...  8.32 us
    all_to_all x1, waiting for transfers between devices, local(): grads = lax.all_to_all(grads, SEQ, split_axis=0, concat_axis=0, tiled=True)  8.23 us
    all_to_all x1, starting transfers between devices, local(): grad = lax.all_to_all(grad, CHIPS, split_axis=0, concat_axis=0, tiled=True)  6.03 us
  transfers between devices with their start and end apart: 23, of which 13 were waited for; matrix products, arithmetic and copies ran while one was open for 15% of the time, Pallas kernels for 29%

profile of v2, /device:TPU:0, one launch (start us, length us, event | category | flops | bytes accessed | tf_op | source)
XLA Modules:
  0.0 235.7 jit_solution(2320489656672728699)
XLA Ops:
  0.6 4.0 %collective-permute-start.1 = (bf16[16,2048]{1,0:T(8,128)(2,1)}, bf16[16,2048]{1,0:T(8,128)(2,1)S(1)}, u32[]{:S(2)}, u32[]{:S(2)}) collective-permute-start(bf16[16,2048]{1,0:T(8,128)(2,1)} %param.10), channel_id=1, source_target_pairs={{0,1},{1,0},{2,3},{3,2},{4,5},{5,4},{6,7},{7,6},{8,9},{9,8},{10,11... | collective-permute-start | bytes 196616 | tf_op jit(solution)/shard_map/ppermute | solution.py:129
  4.7 1.3 copy.40
  6.0 1.3 copy.41
  8.1 1.3 collective-permute-start.2
  9.9 1.4 copy.39
  11.5 1.9 collective-permute-done.2
  14.4 3.1 %collective-permute-start.3 = (bf16[2,32,2048]{2,1,0:T(8,128)(2,1)S(1)}, bf16[2,32,2048]{2,1,0:T(8,128)(2,1)S(1)}, u32[]{:S(2)}, u32[]{:S(2)}) collective-permute-start(bf16[2,32,2048]{2,1,0:T(8,128)(2,1)S(1)} %pad_maximum_fusion.6), channel_id=1, source_target_pairs={{0,96},{32,0},{64,32},{96,64},{1,97},{33,1},{65,33},{97,65},{2,98}... | collective-permute-start | bytes 786440 | tf_op jit(solution)/shard_map/ppermute | solution.py:129
  17.5 1.8 pad_maximum_fusion.1
  19.3 2.3 collective-permute-done.3
  21.6 3.8 %collective-permute-start.4 = (bf16[1,32,2048]{2,1,0:T(8,128)(2,1)S(1)}, bf16[1,32,2048]{2,1,0:T(8,128)(2,1)S(1)}, u32[]{:S(2)}, u32[]{:S(2)}) collective-permute-start(bf16[1,32,2048]{2,1,0:T(8,128)(2,1)S(1)} %slice.81), channel_id=1, source_target_pairs={{0,96},{32,0},{64,32},{96,64},{1,97},{33,1},{65,33},{97,65},{2,98}... | collective-permute-start | bytes 393224 | tf_op jit(solution)/shard_map/ppermute | solution.py:129
  25.5 2.4 %collective-permute-done.4 = bf16[1,32,2048]{2,1,0:T(8,128)(2,1)S(1)} collective-permute-done((bf16[1,32,2048]{2,1,0:T(8,128)(2,1)S(1)}, bf16[1,32,2048]{2,1,0:T(8,128)(2,1)S(1)}, u32[]{:S(2)}, u32[]{:S(2)}) %collective-permute-start.4) | collective-permute-done | bytes 131104 | tf_op jit(solution)/shard_map/ppermute | solution.py:129
  27.9 3.7 %collective-permute-done.6 = bf16[1,32,2048]{2,1,0:T(8,128)(2,1)S(1)} collective-permute-done((bf16[1,32,2048]{2,1,0:T(8,128)(2,1)S(1)}, bf16[1,32,2048]{2,1,0:T(8,128)(2,1)S(1)}, u32[]{:S(2)}, u32[]{:S(2)}) %collective-permute-start.6) | collective-permute-done | bytes 131104 | tf_op jit(solution)/shard_map/ppermute | solution.py:129
  31.9 1.6 collective-permute-start.9
  33.5 1.7 collective-permute-start.7
  35.2 4.5 %all-to-all-start = ((bf16[16,3,216,128]{3,2,1,0:T(8,128)(2,1)}), bf16[16,3,216,128]{3,2,1,0:T(8,128)(2,1)}, u32[]{:S(2)}, u32[]{:S(2)}) async-start(bf16[16,3,216,128]{3,2,1,0:T(8,128)(2,1)} %pad_maximum_fusion.1), calls=%async_computation | async-start | bytes 5308416 | tf_op jit(solution)/shard_map/all_to_all | solution.py:189
  40.7 14.4 %collective-permute-done.9 = bf16[8,32,2048]{2,1,0:T(8,128)(2,1)S(1)} collective-permute-done((bf16[8,32,2048]{2,1,0:T(8,128)(2,1)S(1)}, bf16[8,32,2048]{2,1,0:T(8,128)(2,1)S(1)}, u32[]{:S(2)}, u32[]{:S(2)}) %collective-permute-start.9) | collective-permute-done | bytes 1048608 | tf_op jit(solution)/shard_map/ppermute | solution.py:129
  55.2 1.6 collective-permute-start.10
  56.8 1.8 collective-permute-start.8
  58.6 1.4 broadcast_select_fusion.1
  60.0 5.6 %collective-permute-done.10 = bf16[4,32,2048]{2,1,0:T(8,128)(2,1)S(1)} collective-permute-done((bf16[4,32,2048]{2,1,0:T(8,128)(2,1)S(1)}, bf16[4,32,2048]{2,1,0:T(8,128)(2,1)S(1)}, u32[]{:S(2)}, u32[]{:S(2)}) %collective-permute-start.10) | collective-permute-done | bytes 524320 | tf_op jit(solution)/shard_map/ppermute | solution.py:129
  66.6 2.0 fusion
  69.8 3.7 %all-to-all-done.qkv_ref = bf16[16,3,216,128]{3,2,1,0:T(8,128)(2,1)} async-done(((bf16[16,3,216,128]{3,2,1,0:T(8,128)(2,1)}), bf16[16,3,216,128]{3,2,1,0:T(8,128)(2,1)}, u32[]{:S(2)}, u32[]{:S(2)}) %all-to-all-start) | async-done | bytes 2654240 | tf_op jit(solution)/shard_map/all_to_all | solution.py:189
  73.5 6.0 %all-to-all-start.1 = ((bf16[8,432,128]{2,1,0:T(8,128)(2,1)}), bf16[8,432,128]{2,1,0:T(8,128)(2,1)S(1)}, u32[]{:S(2)}, u32[]{:S(2)}) async-start(bf16[8,432,128]{2,1,0:T(8,128)(2,1)} %bitcast.102), calls=%async_computation.1 | async-start | bytes 1769472 | tf_op jit(solution)/shard_map/all_to_all | solution.py:202
  79.5 33.5 %attend.1 = (bf16[16,216,128]{2,1,0:T(8,128)(2,1)}, bf16[3456,128]{1,0:T(8,128)(2,1)}, bf16[3456,128]{1,0:T(8,128)(2,1)}, bf16[3456,128]{1,0:T(8,128)(2,1)}, f32...) custom-call(s32[3456]{0:T(1024)} %order_ref.3, s32[162]{0:T(256)} %reshape.61.neigh_ref, ...), custom_call_target="tpu_custom_call" | custom-call | flops 30000001024 | bytes 20000000 | tf_op jit(solution)/shard_map/attend/pallas_call | solution.py:62
  113.0 5.7 %all-to-all-start.2 = ((bf16[8,432,128]{2,1,0:T(8,128)(2,1)}), bf16[8,432,128]{2,1,0:T(8,128)(2,1)S(1)}, u32[]{:S(2)}, u32[]{:S(2)}) async-start(bf16[8,432,128]{2,1,0:T(8,128)(2,1)} %bitcast.123), calls=%async_computation.2 | async-start | bytes 1769472 | tf_op jit(solution)/shard_map/all_to_all | solution.py:206
  118.7 34.4 %attend_grad.1 = bf16[16,3,216,128]{3,2,1,0:T(8,128)(2,1)} custom-call(s32[3456]{0:T(1024)} %order_ref.3, s32[162]{0:T(256)} %reshape.61.neigh_ref, s32[1]{0:T(128)} %bitcast.turn_ref, bf16[16,216,128]{2,1,0:T(8,128)(2,1)} %bitcast.122, bf16[3456,128]{1,0:T(8,128)(2,1)} %get-tuple-element.29.qp_ref, bf16[3456,128]{1,0:T(8,128)(2,1)} %get-tuple-element.30.kp_ref, ...), custom_call_target="tpu_custom_call" | custom-call | flops 30000001024 | bytes 20000000 | tf_op jit(solution)/shard_map/attend_grad/pallas_call | solution.py:112
  153.2 2.4 %fusion.1 = f32[1024,2048]{1,0:T(8,128)S(1)} fusion(bf16[432,1024]{1,0:T(8,128)(2,1)S(1)} %copy_bitcast_fusion, bf16[216,2048]{1,0:T(8,128)(2,1)S(1)} %copy-done.9, bf16[216,2048]{1,0:T(8,128)(2,1)S(1)} %copy-done.7), kind=kOutput, calls=%fused_computation.9 | convolution fusion | flops 1815478272 | bytes 11042816 | tf_op jit(solution)/shard_map/dot_general | solution.py:217
  155.7 1.4 slice_bitcast_fusion.8
  157.4 3.0 %collective-permute-start.16 = (bf16[4,32,2048]{2,1,0:T(8,128)(2,1)}, bf16[4,32,2048]{2,1,0:T(8,128)(2,1)S(1)}, u32[]{:S(2)}, u32[]{:S(2)}) collective-permute-start(bf16[4,32,2048]{2,1,0:T(8,128)(2,1)} %get-tuple-element.40), channel_id=1, source_target_pairs={{0,6},{2,0},{4,2},{6,4},{1,7},{3,1},{5,3},{7,5},{8,14},{10,8},{12,... | collective-permute-start | bytes 1572872 | tf_op jit(solution)/shard_map/ppermute | solution.py:129
  160.9 3.8 %fusion.11 = f32[432,2048]{1,0:T(8,128)} fusion(bf16[432,1024]{1,0:T(8,128)(2,1)S(1)} %copy_bitcast_fusion, bf16[1024,2048]{1,0:T(8,128)(2,1)S(1)} %bitcast.111), kind=kOutput, calls=%fused_computation.52 | convolution fusion | flops 1811939328 | bytes 8617984 | tf_op jit(solution)/shard_map/dot_general | solution.py:212
  164.7 1.5 collective-permute-start.14
  166.8 5.8 %all-to-all-start.3 = ((bf16[16,3,216,128]{3,2,1,0:T(8,128)(2,1)}), bf16[16,3,216,128]{3,2,1,0:T(8,128)(2,1)S(1)}, u32[]{:S(2)}, u32[]{:S(2)}) async-start(bf16[16,3,216,128]{3,2,1,0:T(8,128)(2,1)} %attend_grad.1), calls=%async_computation.3 | async-start | bytes 5308416 | tf_op jit(solution)/shard_map/all_to_all | solution.py:210
  173.5 1.5 fusion.5
  175.1 1.3 fusion.3
  176.4 3.3 %collective-permute-start.17 = (bf16[4,32,2048]{2,1,0:T(8,128)(2,1)S(1)}, bf16[4,32,2048]{2,1,0:T(8,128)(2,1)S(1)}, u32[]{:S(2)}, u32[]{:S(2)}) collective-permute-start(bf16[4,32,2048]{2,1,0:T(8,128)(2,1)S(1)} %fusion.3), channel_id=1, source_target_pairs={{0,6},{2,0},{4,2},{6,4},{1,7},{3,1},{5,3},{7,5},{8,14},{10,8},{12,... | collective-permute-start | bytes 1572872 | tf_op jit(solution)/shard_map/ppermute | solution.py:129
  179.7 1.6 dynamic-slice_convert_fusion
  181.3 1.7 slice.85
  184.2 10.0 %collective-permute-done.13 = bf16[4,32,2048]{2,1,0:T(8,128)(2,1)S(1)} collective-permute-done((bf16[4,32,2048]{2,1,0:T(8,128)(2,1)S(1)}, bf16[4,32,2048]{2,1,0:T(8,128)(2,1)S(1)}, u32[]{:S(2)}, u32[]{:S(2)}) %collective-permute-start.13) | collective-permute-done | bytes 524320 | tf_op jit(solution)/shard_map/ppermute | solution.py:129
  194.3 1.2 convert_add_fusion.1
  196.8 1.3 add_convert_fusion
  198.1 8.2 %all-to-all-done.3 = bf16[16,3,216,128]{3,2,1,0:T(8,128)(2,1)S(1)} async-done(((bf16[16,3,216,128]{3,2,1,0:T(8,128)(2,1)}), bf16[16,3,216,128]{3,2,1,0:T(8,128)(2,1)S(1)}, u32[]{:S(2)}, u32[]{:S(2)}) %all-to-all-start.3) | async-done | bytes 2654240 | tf_op jit(solution)/shard_map/all_to_all | solution.py:210
  206.3 8.3 %all-to-all-start.4 = ((bf16[16,16,2048]{2,1,0:T(8,128)(2,1)}), bf16[16,16,2048]{2,1,0:T(8,128)(2,1)}, u32[]{:S(2)}, u32[]{:S(2)}) async-start(bf16[16,16,2048]{2,1,0:T(8,128)(2,1)} %add_convert_fusion), calls=%async_computation.4 | async-start | bytes 2097152 | tf_op jit(solution)/shard_map/all_to_all | solution.py:174
  214.7 2.9 %fusion.6 = bf16[1,216,2048]{2,1,0:T(8,128)(2,1)} fusion(bf16[216,2048]{1,0:T(8,128)(2,1)} %collective-permute-done.11, f32[432,2048]{1,0:T(8,128)} %fusion.11, s32[]{:T(128)S(6)} %select_n.63), kind=kLoop, calls=%fused_computation.18 | loop fusion | flops 1327104 | bytes 3538948 | tf_op jit(solution)/shard_map/broadcast_in_dim | solution.py:226
  218.8 1.3 reshape.70
  220.2 1.3 reshape.71
  221.6 1.3 reshape.72
  222.9 10.8 %all-to-all-done.4 = bf16[16,16,2048]{2,1,0:T(8,128)(2,1)} async-done(((bf16[16,16,2048]{2,1,0:T(8,128)(2,1)}), bf16[16,16,2048]{2,1,0:T(8,128)(2,1)}, u32[]{:S(2)}, u32[]{:S(2)}) %all-to-all-start.4) | async-done | bytes 1048608 | tf_op jit(solution)/shard_map/all_to_all | solution.py:174
  233.7 2.0 reduce_sum.12
  (82 shorter events, 12.4 us)
Async XLA Ops:
  0.6 6.8 %copy-start.14 = (bf16[16,2048]{1,0:T(8,128)(2,1)S(1)}, bf16[16,2048]{1,0:T(8,128)(2,1)}, u32[]{:S(2)}) copy-start(bf16[16,2048]{1,0:T(8,128)(2,1)} %param.10) | copy-start | bytes 196612
  0.6 6.7 %collective-permute-start.1 = (bf16[16,2048]{1,0:T(8,128)(2,1)}, bf16[16,2048]{1,0:T(8,128)(2,1)S(1)}, u32[]{:S(2)}, u32[]{:S(2)}) collective-permute-start(bf16[16,2048]{1,0:T(8,128)(2,1)} %param.10), channel_id=1, source_target_pairs={{0,1},{1,0},{2,3},{3,2},{4,5},{5,4},{6,7},{7,6},{8,9},{9,8},{10,11... | collective-permute-start | bytes 196616 | tf_op jit(solution)/shard_map/ppermute | solution.py:129
  7.4 2.0 copy-start.10
  7.4 2.0 copy-start.12
  8.1 5.3 %collective-permute-start.2 = (bf16[32,2048]{1,0:T(8,128)(2,1)}, bf16[32,2048]{1,0:T(8,128)(2,1)}, u32[]{:S(2)}, u32[]{:S(2)}) collective-permute-start(bf16[32,2048]{1,0:T(8,128)(2,1)} %pad_maximum_fusion.7), channel_id=1, source_target_pairs={{0,16},{16,0},{1,17},{17,1},{2,18},{18,2},{3,19},{19,3},{4,20},{20... | collective-permute-start | bytes 393224 | tf_op jit(solution)/shard_map/ppermute | solution.py:129
  9.9 3.5 %copy-start.11 = (bf16[16,2048]{1,0:T(8,128)(2,1)S(1)}, bf16[16,2048]{1,0:T(8,128)(2,1)}, u32[]{:S(2)}) copy-start(bf16[16,2048]{1,0:T(8,128)(2,1)} %copy-done.10) | copy-start | bytes 196612
  9.9 3.5 %copy-start.13 = (bf16[16,2048]{1,0:T(8,128)(2,1)S(1)}, bf16[16,2048]{1,0:T(8,128)(2,1)}, u32[]{:S(2)}) copy-start(bf16[16,2048]{1,0:T(8,128)(2,1)} %copy-done.12) | copy-start | bytes 196612
  14.4 7.2 %collective-permute-start.3 = (bf16[2,32,2048]{2,1,0:T(8,128)(2,1)S(1)}, bf16[2,32,2048]{2,1,0:T(8,128)(2,1)S(1)}, u32[]{:S(2)}, u32[]{:S(2)}) collective-permute-start(bf16[2,32,2048]{2,1,0:T(8,128)(2,1)S(1)} %pad_maximum_fusion.6), channel_id=1, source_target_pairs={{0,96},{32,0},{64,32},{96,64},{1,97},{33,1},{65,33},{97,65},{2,98}... | collective-permute-start | bytes 786440 | tf_op jit(solution)/shard_map/ppermute | solution.py:129
  17.5 7.9 %collective-permute-start.5 = (bf16[2,32,2048]{2,1,0:T(8,128)(2,1)S(1)}, bf16[2,32,2048]{2,1,0:T(8,128)(2,1)S(1)}, u32[]{:S(2)}, u32[]{:S(2)}) collective-permute-start(bf16[2,32,2048]{2,1,0:T(8,128)(2,1)S(1)} %pad_maximum_fusion.6), channel_id=1, source_target_pairs={{0,32},{32,64},{64,96},{96,0},{1,33},{33,65},{65,97},{97,1},{2,34}... | collective-permute-start | bytes 786440 | tf_op jit(solution)/shard_map/ppermute | solution.py:129
  21.6 6.3 %collective-permute-start.4 = (bf16[1,32,2048]{2,1,0:T(8,128)(2,1)S(1)}, bf16[1,32,2048]{2,1,0:T(8,128)(2,1)S(1)}, u32[]{:S(2)}, u32[]{:S(2)}) collective-permute-start(bf16[1,32,2048]{2,1,0:T(8,128)(2,1)S(1)} %slice.81), channel_id=1, source_target_pairs={{0,96},{32,0},{64,32},{96,64},{1,97},{33,1},{65,33},{97,65},{2,98}... | collective-permute-start | bytes 393224 | tf_op jit(solution)/shard_map/ppermute | solution.py:129
  25.4 6.2 %collective-permute-start.6 = (bf16[1,32,2048]{2,1,0:T(8,128)(2,1)S(1)}, bf16[1,32,2048]{2,1,0:T(8,128)(2,1)S(1)}, u32[]{:S(2)}, u32[]{:S(2)}) collective-permute-start(bf16[1,32,2048]{2,1,0:T(8,128)(2,1)S(1)} %slice.82), channel_id=1, source_target_pairs={{0,32},{32,64},{64,96},{96,0},{1,33},{33,65},{65,97},{97,1},{2,34}... | collective-permute-start | bytes 393224 | tf_op jit(solution)/shard_map/ppermute | solution.py:129
  31.9 8.0 %copy-start.15 = (s32[18,9]{0,1:T(8,128)S(1)}, s32[18,9]{0,1:T(8,128)}, u32[]{:S(2)}) copy-start(s32[18,9]{0,1:T(8,128)} %param.12) | copy-start | bytes 1948
  31.9 23.2 %collective-permute-start.9 = (bf16[8,32,2048]{2,1,0:T(8,128)(2,1)S(1)}, bf16[8,32,2048]{2,1,0:T(8,128)(2,1)S(1)}, u32[]{:S(2)}, u32[]{:S(2)}) collective-permute-start(bf16[8,32,2048]{2,1,0:T(8,128)(2,1)S(1)} %bitcast.112), channel_id=1, source_target_pairs={{0,2},{2,4},{4,6},{6,0},{1,3},{3,5},{5,7},{7,1},{8,10},{10,12},{12... | collective-permute-start | bytes 3145736 | tf_op jit(solution)/shard_map/ppermute | solution.py:129
  33.5 23.2 %collective-permute-start.7 = (bf16[8,32,2048]{2,1,0:T(8,128)(2,1)S(1)}, bf16[8,32,2048]{2,1,0:T(8,128)(2,1)S(1)}, u32[]{:S(2)}, u32[]{:S(2)}) collective-permute-start(bf16[8,32,2048]{2,1,0:T(8,128)(2,1)S(1)} %bitcast.113), channel_id=1, source_target_pairs={{0,6},{2,0},{4,2},{6,4},{1,7},{3,1},{5,3},{7,5},{8,14},{10,8},{12,... | collective-permute-start | bytes 3145736 | tf_op jit(solution)/shard_map/ppermute | solution.py:129
  35.2 38.3 %all-to-all-start = ((bf16[16,3,216,128]{3,2,1,0:T(8,128)(2,1)}), bf16[16,3,216,128]{3,2,1,0:T(8,128)(2,1)}, u32[]{:S(2)}, u32[]{:S(2)}) async-start(bf16[16,3,216,128]{3,2,1,0:T(8,128)(2,1)} %pad_maximum_fusion.1), calls=%async_computation | async-start | bytes 5308416 | tf_op jit(solution)/shard_map/all_to_all | solution.py:189
  39.7 18.9 %collective-permute-start = (bf16[216,2048]{1,0:T(8,128)(2,1)}, bf16[216,2048]{1,0:T(8,128)(2,1)}, u32[]{:S(2)}, u32[]{:S(2)}) collective-permute-start(bf16[216,2048]{1,0:T(8,128)(2,1)} %bitcast.124), channel_id=1, source_target_pairs={{0,8},{8,0},{1,9},{9,1},{2,10},{10,2},{3,11},{11,3},{4,12},{12,4},... | collective-permute-start | bytes 2654216 | tf_op jit(solution)/shard_map/ppermute | solution.py:129
  40.7 17.9 %copy-start.5 = (bf16[1,216,2048]{2,1,0:T(8,128)(2,1)S(1)}, bf16[1,216,2048]{2,1,0:T(8,128)(2,1)}, u32[]{:S(2)}) copy-start(bf16[1,216,2048]{2,1,0:T(8,128)(2,1)} %param.11) | copy-start | bytes 2654212
  55.2 10.5 %collective-permute-start.10 = (bf16[4,32,2048]{2,1,0:T(8,128)(2,1)S(1)}, bf16[4,32,2048]{2,1,0:T(8,128)(2,1)S(1)}, u32[]{:S(2)}, u32[]{:S(2)}) collective-permute-start(bf16[4,32,2048]{2,1,0:T(8,128)(2,1)S(1)} %slice.84), channel_id=1, source_target_pairs={{0,2},{2,4},{4,6},{6,0},{1,3},{3,5},{5,7},{7,1},{8,10},{10,12},{12... | collective-permute-start | bytes 1572872 | tf_op jit(solution)/shard_map/ppermute | solution.py:129
  56.8 9.2 %collective-permute-start.8 = (bf16[4,32,2048]{2,1,0:T(8,128)(2,1)S(1)}, bf16[4,32,2048]{2,1,0:T(8,128)(2,1)S(1)}, u32[]{:S(2)}, u32[]{:S(2)}) collective-permute-start(bf16[4,32,2048]{2,1,0:T(8,128)(2,1)S(1)} %slice.83), channel_id=1, source_target_pairs={{0,6},{2,0},{4,2},{6,4},{1,7},{3,1},{5,3},{7,5},{8,14},{10,8},{12,... | collective-permute-start | bytes 1572872 | tf_op jit(solution)/shard_map/ppermute | solution.py:129
  60.0 6.6 %copy-start.6 = (bf16[216,2048]{1,0:T(8,128)(2,1)}, bf16[216,2048]{1,0:T(8,128)(2,1)S(1)}, u32[]{:S(2)}) copy-start(bf16[216,2048]{1,0:T(8,128)(2,1)S(1)} %get-tuple-element.46) | copy-start | bytes 2654212
  60.0 6.6 %copy-start.8 = (bf16[216,2048]{1,0:T(8,128)(2,1)}, bf16[216,2048]{1,0:T(8,128)(2,1)S(1)}, u32[]{:S(2)}) copy-start(bf16[216,2048]{1,0:T(8,128)(2,1)S(1)} %get-tuple-element.47) | copy-start | bytes 2654212
  66.6 2.1 copy-start.1
  73.5 39.5 %all-to-all-start.1 = ((bf16[8,432,128]{2,1,0:T(8,128)(2,1)}), bf16[8,432,128]{2,1,0:T(8,128)(2,1)S(1)}, u32[]{:S(2)}, u32[]{:S(2)}) async-start(bf16[8,432,128]{2,1,0:T(8,128)(2,1)} %bitcast.102), calls=%async_computation.1 | async-start | bytes 1769472 | tf_op jit(solution)/shard_map/all_to_all | solution.py:202
  113.0 5.7 %copy-start.4 = (bf16[8,432,128]{2,1,0:T(8,128)(2,1)}, bf16[8,432,128]{2,1,0:T(8,128)(2,1)S(1)}, u32[]{:S(2)}) copy-start(bf16[8,432,128]{2,1,0:T(8,128)(2,1)S(1)} %all-to-all-done.1) | copy-start | bytes 2654212
  113.0 40.1 %all-to-all-start.2 = ((bf16[8,432,128]{2,1,0:T(8,128)(2,1)}), bf16[8,432,128]{2,1,0:T(8,128)(2,1)S(1)}, u32[]{:S(2)}, u32[]{:S(2)}) async-start(bf16[8,432,128]{2,1,0:T(8,128)(2,1)} %bitcast.123), calls=%async_computation.2 | async-start | bytes 1769472 | tf_op jit(solution)/shard_map/all_to_all | solution.py:206
  118.7 34.5 %copy-start.7 = (bf16[216,2048]{1,0:T(8,128)(2,1)S(1)}, bf16[216,2048]{1,0:T(8,128)(2,1)}, u32[]{:S(2)}) copy-start(bf16[216,2048]{1,0:T(8,128)(2,1)} %copy-done.6) | copy-start | bytes 2654212
  118.7 34.5 %copy-start.9 = (bf16[216,2048]{1,0:T(8,128)(2,1)S(1)}, bf16[216,2048]{1,0:T(8,128)(2,1)}, u32[]{:S(2)}) copy-start(bf16[216,2048]{1,0:T(8,128)(2,1)} %copy-done.8) | copy-start | bytes 2654212
  155.7 9.1 %copy-start = (f32[1024,2048]{1,0:T(8,128)}, f32[1024,2048]{1,0:T(8,128)S(1)}, u32[]{:S(2)}) copy-start(f32[1024,2048]{1,0:T(8,128)S(1)} %fusion.1) | copy-start | bytes 25165828
  155.7 5.3 %copy-start.2 = (bf16[8,128,2048]{2,1,0:T(8,128)(2,1)S(1)}, bf16[8,128,2048]{2,1,0:T(8,128)(2,1)}, u32[]{:S(2)}) copy-start(bf16[8,128,2048]{2,1,0:T(8,128)(2,1)} %copy-done.1) | copy-start | bytes 12582916
  157.1 16.4 %collective-permute-start.12 = (bf16[4,32,2048]{2,1,0:T(8,128)(2,1)}, bf16[4,32,2048]{2,1,0:T(8,128)(2,1)}, u32[]{:S(2)}, u32[]{:S(2)}) collective-permute-start(bf16[4,32,2048]{2,1,0:T(8,128)(2,1)} %get-tuple-element.39), channel_id=1, source_target_pairs={{0,2},{2,4},{4,6},{6,0},{1,3},{3,5},{5,7},{7,1},{8,10},{10,12},{12... | collective-permute-start | bytes 1572872 | tf_op jit(solution)/shard_map/ppermute | solution.py:129
  157.4 17.7 %collective-permute-start.16 = (bf16[4,32,2048]{2,1,0:T(8,128)(2,1)}, bf16[4,32,2048]{2,1,0:T(8,128)(2,1)S(1)}, u32[]{:S(2)}, u32[]{:S(2)}) collective-permute-start(bf16[4,32,2048]{2,1,0:T(8,128)(2,1)} %get-tuple-element.40), channel_id=1, source_target_pairs={{0,6},{2,0},{4,2},{6,4},{1,7},{3,1},{5,3},{7,5},{8,14},{10,8},{12,... | collective-permute-start | bytes 1572872 | tf_op jit(solution)/shard_map/ppermute | solution.py:129
  164.7 19.5 %collective-permute-start.14 = (bf16[4,32,2048]{2,1,0:T(8,128)(2,1)}, bf16[4,32,2048]{2,1,0:T(8,128)(2,1)}, u32[]{:S(2)}, u32[]{:S(2)}) collective-permute-start(bf16[4,32,2048]{2,1,0:T(8,128)(2,1)} %get-tuple-element.42), channel_id=1, source_target_pairs={{0,6},{2,0},{4,2},{6,4},{1,7},{3,1},{5,3},{7,5},{8,14},{10,8},{12,... | collective-permute-start | bytes 1572872 | tf_op jit(solution)/shard_map/ppermute | solution.py:129
  166.3 29.2 %collective-permute-start.15 = (bf16[4,32,2048]{2,1,0:T(8,128)(2,1)}, bf16[4,32,2048]{2,1,0:T(8,128)(2,1)}, u32[]{:S(2)}, u32[]{:S(2)}) collective-permute-start(bf16[4,32,2048]{2,1,0:T(8,128)(2,1)} %get-tuple-element.41), channel_id=1, source_target_pairs={{0,2},{2,4},{4,6},{6,0},{1,3},{3,5},{5,7},{7,1},{8,10},{10,12},{12... | collective-permute-start | bytes 1572872 | tf_op jit(solution)/shard_map/ppermute | solution.py:129
  166.8 39.6 %all-to-all-start.3 = ((bf16[16,3,216,128]{3,2,1,0:T(8,128)(2,1)}), bf16[16,3,216,128]{3,2,1,0:T(8,128)(2,1)S(1)}, u32[]{:S(2)}, u32[]{:S(2)}) async-start(bf16[16,3,216,128]{3,2,1,0:T(8,128)(2,1)} %attend_grad.1), calls=%async_computation.3 | async-start | bytes 5308416 | tf_op jit(solution)/shard_map/all_to_all | solution.py:210
  175.0 19.3 %collective-permute-start.13 = (bf16[4,32,2048]{2,1,0:T(8,128)(2,1)S(1)}, bf16[4,32,2048]{2,1,0:T(8,128)(2,1)S(1)}, u32[]{:S(2)}, u32[]{:S(2)}) collective-permute-start(bf16[4,32,2048]{2,1,0:T(8,128)(2,1)S(1)} %fusion.5), channel_id=1, source_target_pairs={{0,2},{2,4},{4,6},{6,0},{1,3},{3,5},{5,7},{7,1},{8,10},{10,12},{12... | collective-permute-start | bytes 1572872 | tf_op jit(solution)/shard_map/ppermute | solution.py:129
  176.4 19.0 %collective-permute-start.17 = (bf16[4,32,2048]{2,1,0:T(8,128)(2,1)S(1)}, bf16[4,32,2048]{2,1,0:T(8,128)(2,1)S(1)}, u32[]{:S(2)}, u32[]{:S(2)}) collective-permute-start(bf16[4,32,2048]{2,1,0:T(8,128)(2,1)S(1)} %fusion.3), channel_id=1, source_target_pairs={{0,6},{2,0},{4,2},{6,4},{1,7},{3,1},{5,3},{7,5},{8,14},{10,8},{12,... | collective-permute-start | bytes 1572872 | tf_op jit(solution)/shard_map/ppermute | solution.py:129
  183.0 31.6 %collective-permute-start.11 = (bf16[216,2048]{1,0:T(8,128)(2,1)S(1)}, bf16[216,2048]{1,0:T(8,128)(2,1)}, u32[]{:S(2)}, u32[]{:S(2)}) collective-permute-start(bf16[216,2048]{1,0:T(8,128)(2,1)S(1)} %dynamic-slice_convert_fusion), channel_id=1, source_target_pairs={{0,8},{8,0},{1,9},{9,1},{2,10},{10,2},{3,11},{11,3},{4,12},{12,4},... | collective-permute-start | bytes 2654216 | tf_op jit(solution)/shard_map/ppermute | solution.py:129
  206.3 27.4 %all-to-all-start.4 = ((bf16[16,16,2048]{2,1,0:T(8,128)(2,1)}), bf16[16,16,2048]{2,1,0:T(8,128)(2,1)}, u32[]{:S(2)}, u32[]{:S(2)}) async-start(bf16[16,16,2048]{2,1,0:T(8,128)(2,1)} %add_convert_fusion), calls=%async_computation.4 | async-start | bytes 2097152 | tf_op jit(solution)/shard_map/all_to_all | solution.py:174
  218.7 1.4 copy-start.3

commit v3 on v2

v3 whole, which is shorter than its diff:
```python
import math

import jax
import jax.numpy as jnp
import numpy as np
from jax import lax
from jax.experimental import pallas as pl
from jax.experimental.pallas import tpu as pltpu
from jax.sharding import Mesh, PartitionSpec as P

T=192; NT=18; NB=9; N=T*NT; KC=T*NB; HD=128
bf=jnp.bfloat16; f32=jnp.float32
SC=1.0/math.sqrt(HD); LOG2E=math.log2(math.e)
PITCH=4
KP=1792; BW=256; BLOCKS=KP//BW
U1=2; U2=2
COST=pl.CostEstimate(flops=30*10**9,bytes_accessed=20*10**6,transcendentals=0)

def permute_rows(order_ref, src, dst, width, scatter, unroll=32):
    def body(i, c):
        for u in range(unroll):
            p=i*unroll+u
            t=order_ref[p]
            a,b=(t,p) if scatter else (p,t)
            dst[pl.ds(a*width,width),:]=src[pl.ds(b*width,width),:]
        return c
    lax.fori_loop(0,N//unroll,body,0)

def load_keys(t, to, rows, neigh_ref):
    for j in range(NB):
        to[pl.ds(j*T,T),:]=rows[pl.ds(pl.multiple_of(neigh_ref[t*NB+j]*T,T),T),:]

def scores_ready(t, qp_ref, kp_ref, kc, neigh_ref):
    load_keys(t,kc,kp_ref,neigh_ref)
    kc[pl.ds(KC,KP-KC),:]=kc[pl.ds(KC-(KP-KC),KP-KC),:]
    return qp_ref[pl.ds(pl.multiple_of(t*T,T),T),:]

def k1(order_ref, neigh_ref, turn_ref, qkv_ref, att_ref, qp_ref, kp_ref, vp_ref, o_ref, rinv_ref, e_ref, tok, per, kc, vc, held, sb, mx):
    i=pl.program_id(0)
    R=U1*T
    @pl.when(i==0)
    def _():
        for j in range(3):
            for s in range(16):
                tok[pl.ds(s*216*PITCH+j,216,stride=PITCH),:]=qkv_ref[s,j].astype(f32)
        permute_rows(order_ref,tok,per,PITCH,False)
        for j,r in enumerate((qp_ref,kp_ref,vp_ref)):
            for u in range(NT):
                r[pl.ds(u*T,T),:]=per[pl.ds(u*T*PITCH+j,T,stride=PITCH),:].astype(bf)
        vc[pl.ds(KC,KP-KC),:]=jnp.zeros((KP-KC,HD),bf)
        q=scores_ready(0,qp_ref,kp_ref,kc,neigh_ref)
        s=lax.dot_general(q,kc[...],(((1,),(1,)),((),())),preferred_element_type=f32)
        sb[0]=s
        top=s[:,:HD]
        for b in range(1,KP//HD):
            top=jnp.maximum(top,s[:,b*HD:(b+1)*HD])
        mx[0]=top
    back=jnp.maximum(i-1,0)*R
    for p in range(R):
        tok[pl.ds(order_ref[back+p],1),:]=held[pl.ds(p,1),:]
    for u in range(2):
        t=2*i+u
        load_keys(t,vc,vp_ref,neigh_ref)
        nq=scores_ready(jnp.minimum(t+1,NT-1),qp_ref,kp_ref,kc,neigh_ref)
        mc=jnp.max(mx[u],axis=-1,keepdims=True)*(SC*LOG2E)
        total=jnp.zeros((T,HD),f32)
        o=jnp.zeros((T,HD),f32)
        top=None
        for b in range(BLOCKS):
            cols=pl.ds(b*BW,BW)
            s=lax.dot_general(nq,kc[cols,:],(((1,),(1,)),((),())),preferred_element_type=f32)
            sb[1-u,:,cols]=s
            part=jnp.maximum(s[:,:HD],s[:,HD:])
            top=part if top is None else jnp.maximum(top,part)
            e=jnp.exp2(sb[u,:,cols]*(SC*LOG2E)-mc)
            right=e[:,HD:]
            if b==BLOCKS-1:
                right=jnp.where(lax.broadcasted_iota(jnp.int32,(T,HD),1)<KC%HD,right,0.0)
            total=total+(e[:,:HD]+right)
            eb=e.astype(bf)
            e_ref[u,:,cols]=eb
            o=o+jnp.dot(eb,vc[cols,:],preferred_element_type=f32)
        mx[1-u]=top
        rinv=1.0/jnp.sum(total,axis=-1,keepdims=True)
        o=o*rinv
        rinv_ref[pl.ds(u*T,T),:]=jnp.broadcast_to(rinv,(T,HD))
        o_ref[pl.ds(u*T,T),:]=o
        held[pl.ds(u*T,T),:]=o
    @pl.when(i==NT//U1-1)
    def _():
        def last(c,_):
            for w in range(32):
                p=c*32+w
                tok[pl.ds(order_ref[N-R+p],1),:]=held[pl.ds(p,1),:]
            return _
        lax.fori_loop(0,R//32,last,0)
        for s in range(16):
            att_ref[s]=pltpu.roll(tok[pl.ds(s*216,216),:],lax.rem(HD-turn_ref[0],HD),1).astype(bf)

def run_k1(order, neigh, turn, qkv):
    full=lambda shape: pl.BlockSpec(shape,lambda t,*_:(0,)*len(shape))
    return pl.pallas_call(k1,
      grid_spec=pltpu.PrefetchScalarGridSpec(num_scalar_prefetch=3,grid=(NT//U1,),
        in_specs=[full((16,3,216,HD))],
        out_specs=[full((16,216,HD)),full((N,HD)),full((N,HD)),full((N,HD)),pl.BlockSpec((U1*T,HD),lambda t,*_:(t,0)),
                   pl.BlockSpec((U1*T,HD),lambda t,*_:(t,0)),pl.BlockSpec((U1,T,KP),lambda t,*_:(t,0,0))],
        scratch_shapes=[pltpu.VMEM((N*PITCH,HD),f32),pltpu.VMEM((N*PITCH,HD),f32),pltpu.VMEM((KP,HD),bf),pltpu.VMEM((KP,HD),bf),pltpu.VMEM((U1*T,HD),f32),pltpu.VMEM((2,T,KP),f32),pltpu.VMEM((2,T,HD),f32)]),
      out_shape=[jax.ShapeDtypeStruct((16,216,HD),bf)]+[jax.ShapeDtypeStruct((N,HD),bf)]*3+[jax.ShapeDtypeStruct((N,HD),f32),jax.ShapeDtypeStruct((N,HD),f32),jax.ShapeDtypeStruct((NT,T,KP),bf)],
      compiler_params=pltpu.CompilerParams(vmem_limit_bytes=60*1024*1024),
      cost_estimate=COST,name="attend")(order,neigh,turn,qkv)

def k2(order_ref, neigh_ref, turn_ref, g_ref, qp_ref, kp_ref, vp_ref, o_ref, rinv_ref, e_ref, out_ref, tok, gp, acc, kc, vc):
    i=pl.program_id(0)
    R=U2*T
    @pl.when(i==0)
    def _():
        for s in range(16):
            tok[pl.ds(s*216,216),:]=pltpu.roll(g_ref[s].astype(f32),turn_ref[0],1)
        def first(c,_):
            for w in range(32):
                p=c*32+w
                gp[pl.ds(p,1),:]=tok[pl.ds(order_ref[p],1),:]
            return _
        lax.fori_loop(0,R//32,first,0)
        for u in range(NT*PITCH):
            acc[pl.ds(u*T,T),:]=jnp.zeros((T,HD),f32)
    g=gp[...]
    ahead=jnp.minimum((i+1)*R,N-R)
    for p in range(R):
        gp[pl.ds(p,1),:]=tok[pl.ds(order_ref[ahead+p],1),:]
    gs_all=(g*rinv_ref[...]).astype(bf)
    d_all=jnp.sum(gs_all.astype(f32)*o_ref[...],axis=-1,keepdims=True)
    for u in range(U2):
        t=i*U2+u
        ns=[]
        for j in range(NB):
            n=neigh_ref[t*NB+j]
            off=pl.multiple_of(n*T,T); ns.append(n)
            kc[u,pl.ds(j*T,T),:]=kp_ref[pl.ds(off,T),:]
            vc[u,pl.ds(j*T,T),:]=vp_ref[pl.ds(off,T),:]
        q=qp_ref[pl.ds(u*T,T),:]
        gs=gs_all[u*T:(u+1)*T]
        d=d_all[u*T:(u+1)*T]
        dp=lax.dot_general(gs,vc[u],(((1,),(1,)),((),())),preferred_element_type=f32)
        eb=e_ref[u,:,:KC]
        ds=(eb.astype(f32)*(dp-d)).astype(bf)
        dq=jnp.dot(ds,kc[u],preferred_element_type=f32)
        acc[pl.ds(t*T*PITCH,T,stride=PITCH),:]=dq
        dk=lax.dot_general(ds,q,(((0,),(0,)),((),())),preferred_element_type=f32)
        dv=lax.dot_general(eb,gs,(((0,),(0,)),((),())),preferred_element_type=f32)
        for j in range(NB):
            base=ns[j]*(T*PITCH)
            i1=pl.ds(base+1,T,stride=PITCH); i2=pl.ds(base+2,T,stride=PITCH)
            acc[i1,:]=acc[i1,:]+dk[j*T:(j+1)*T]
            acc[i2,:]=acc[i2,:]+dv[j*T:(j+1)*T]
    @pl.when(i==NT//U2-1)
    def _():
        permute_rows(order_ref,acc,tok,PITCH,True)
        for s in range(16):
            for j in range(3):
                rows=tok[pl.ds(s*216*PITCH+j,216,stride=PITCH),:]
                out_ref[s,j]=(rows*SC if j<2 else rows).astype(bf)

def run_k2(order, neigh, turn, g, qp,kp,vp,o,rinv,e):
    full=lambda shape: pl.BlockSpec(shape,lambda t,*_:(0,)*len(shape))
    row=pl.BlockSpec((U2*T,HD),lambda t,*_:(t,0))
    return pl.pallas_call(k2,
      grid_spec=pltpu.PrefetchScalarGridSpec(num_scalar_prefetch=3,grid=(NT//U2,),
        in_specs=[full((16,216,HD)),row,full((N,HD)),full((N,HD)),row,
                   row,pl.BlockSpec((U2,T,KP),lambda t,*_:(t,0,0))],
        out_specs=full((16,3,216,HD)),
        scratch_shapes=[pltpu.VMEM((N*PITCH,HD),f32),pltpu.VMEM((U2*T,HD),f32),pltpu.VMEM((N*PITCH,HD),f32),pltpu.VMEM((U2,KC,HD),bf),pltpu.VMEM((U2,KC,HD),bf)]),
      out_shape=jax.ShapeDtypeStruct((16,3,216,HD),bf),
      compiler_params=pltpu.CompilerParams(vmem_limit_bytes=60*1024*1024),
      cost_estimate=COST,name="attend_grad")(order,neigh,turn,g,qp,kp,vp,o,rinv,e)


def rows_kernel(y_ref, cot_ref, near, near_after, low_half, high_half, near_before, far, far_after, far_before, grad_ref, w_ref):
    cot = cot_ref[...]
    for r in range(4):
        for zl in range(2):
            at = {0: 0, 1: 2, 3: 4}.get(r, 0) + zl
            if r == 2:
                opposite = high_half[3] if zl else low_half[3]
                parts = [far[zl], far_after[zl], opposite, far_before[zl]]
            else:
                opposite = low_half[at] if at < 3 else high_half[at - 3]
                parts = [near[at], near_after[at], opposite, near_before[at]]
            head = lax.rem(y_ref[0] + r, 4) * 2 + zl
            for d in range(4):
                w_ref[head, pl.ds(d * 32, 32), :] = parts[d]
            grad_ref[head] = lax.dot_general(
                cot, w_ref[head], (((1,), (1,)), ((), ())), preferred_element_type=f32
            ).astype(bf)


def run_rows(y, cot, near, far):
    whole = pl.BlockSpec(memory_space=pltpu.VMEM)
    return pl.pallas_call(
        rows_kernel,
        in_specs=[pl.BlockSpec(memory_space=pltpu.SMEM)] + [whole] * 9,
        out_specs=[whole, whole],
        out_shape=[
            jax.ShapeDtypeStruct((8, 432, HD), bf),
            jax.ShapeDtypeStruct((8, HD, 2048), bf),
        ],
        compiler_params=pltpu.CompilerParams(vmem_limit_bytes=40 * 1024 * 1024),
        cost_estimate=pl.CostEstimate(flops=5 * 10**9, bytes_accessed=10**7, transcendentals=0),
        name="grad_rows",
    )(y, cot, *near, *far)


CHIPS = ("y", "zl")
SEQ = ("y", "zl", "c")
VIDEOS = ("x", "zh")


def shift(value, axis, size, step):
    return lax.ppermute(value, axis, [(i, (i + step) % size) for i in range(size)])


def in_place(axis, own, other):
    low = lax.axis_index(axis) == 0
    return jnp.concatenate([jnp.where(low, own, other), jnp.where(low, other, own)], axis=0)


def around(value, axis):
    half = value.shape[0] // 2
    after, before = shift(value, axis, 4, -1), shift(value, axis, 4, 1)
    far = [shift(after[:half], axis, 4, -1), shift(before[half:], axis, 4, 1)]
    return [after, jnp.concatenate(far, axis=0), before]


def gather_weight(own, qkv):
    pairs = [[(i, i ^ flip) for i in range(4)] for flip in (1, 2, 3)]
    next_zh, next_zl, next_both = (lax.ppermute(own, ("zl", "zh"), pair) for pair in pairs)
    w = in_place("zl", in_place("zh", own, next_zh)[None], in_place("zh", next_zl, next_both)[None])
    y = lax.axis_index("y")
    ring = jnp.stack([w] + around(w, "y"))
    ring = jnp.concatenate([ring, ring], axis=0)
    w = lax.dynamic_slice_in_dim(ring, 4 - y, 4, 0).reshape(8, 32, 2048)
    w, qkv = lax.optimization_barrier((w, qkv))
    return jnp.concatenate([w] + around(w, "x"), axis=1), qkv


def low(value):
    return value.astype(bf)


def sum_last(rows, grads):
    def at(value, index):
        return lax.dynamic_index_in_dim(value, index, 0, keepdims=False)

    y, z = lax.axis_index("y"), lax.axis_index(("zl", "zh"))
    rows = rows.reshape(4, 4, 16, 2048)
    got = [shift(at(rows, (y + d) % 4), "y", 4, d) for d in (1, 2, 3)]
    *got, grads = lax.optimization_barrier((*got, grads))
    rows = low(sum((part.astype(f32) for part in got), at(rows, y).astype(f32)))
    total = at(rows, z).astype(f32)
    for flip in (1, 2, 3):
        pairs = [(i, i ^ flip) for i in range(4)]
        total = total + lax.ppermute(at(rows, z ^ flip), ("zl", "zh"), pairs).astype(f32)
    return low(total), grads


def local(queries, key_vectors, values, out_weight, cotangent, neighbours, tile_order):
    core = lax.axis_index("c")
    turn = (lax.axis_index("x") * 32).astype(jnp.int32).reshape(1)
    neigh = neighbours.reshape(-1)

    def by_head(tensor):
        return tensor.reshape(216, 16, HD).transpose(1, 0, 2)

    qkv = jnp.stack([by_head(queries[0]), by_head(key_vectors[0]), by_head(values[0])], axis=1)
    cot = cotangent[0]
    weight, qkv = gather_weight(out_weight, qkv)
    weight = weight.reshape(1024, 2048)
    qkv = lax.all_to_all(qkv, SEQ, split_axis=0, concat_axis=0, tiled=True)

    def of_chip(mine, theirs=None):
        theirs = shift(mine, "c", 2, 1) if theirs is None else theirs
        return jnp.concatenate(
            [jnp.where(core == 0, mine, theirs), jnp.where(core == 0, theirs, mine)], axis=0
        )

    cot_chip = of_chip(cot)
    grad = lax.dot_general(
        cot_chip, weight, (((1,), (1,)), ((), ())), preferred_element_type=f32
    ).astype(bf)
    grad = grad.reshape(432, 8, HD).transpose(1, 0, 2)
    grad, qkv = lax.optimization_barrier((grad, qkv))
    grad = lax.all_to_all(grad, CHIPS, split_axis=0, concat_axis=0, tiled=True)

    att, *saved = run_k1(tile_order, neigh, turn, qkv)
    att, grad, cot = lax.optimization_barrier((att, grad, cot))
    cots = [shift(cot, "x", 4, d) for d in (1, 2, 3)]
    att = lax.all_to_all(att.reshape(8, 432, HD), CHIPS, split_axis=0, concat_axis=0, tiled=True)
    att = att.transpose(1, 0, 2).reshape(432, 1024)
    grads = run_k2(tile_order, neigh, turn, grad.reshape(16, 216, HD), *saved)
    att, grads, *cots = lax.optimization_barrier((att, grads, *cots))
    grads = lax.all_to_all(grads, SEQ, split_axis=0, concat_axis=0, tiled=True)

    first_other = shift(cots[0], "c", 2, 1)
    att, first_other = lax.optimization_barrier((att, first_other))
    shares = att.reshape(432, 8, 4, 32).transpose(2, 0, 1, 3).reshape(4, 432, 256)
    shares = [shares[0]] + [shift(shares[d], "x", 4, d) for d in (1, 2, 3)]
    rows = jnp.zeros((256, 2048), f32)
    for share, rows_of in zip(shares, [cot_chip, of_chip(cots[0], first_other), of_chip(cots[1]), of_chip(cots[2])]):
        rows = rows + lax.dot_general(
            share, rows_of, (((0,), (0,)), ((), ())), preferred_element_type=f32
        )
    rows = low(rows).reshape(16, 16, 2048)
    partial = jnp.dot(att, weight, preferred_element_type=f32)
    mine = lax.dynamic_slice_in_dim(partial, core * 216, 216, 0)
    other = lax.dynamic_slice_in_dim(partial, (1 - core) * 216, 216, 0).astype(bf)
    projected = (mine + shift(other, "c", 2, 1).astype(f32)).astype(bf)
    grad_weight, grads = sum_last(rows, grads)

    def by_token(tensor):
        return tensor.transpose(1, 0, 2).reshape(1, 216, 2048)

    return (
        projected[None],
        by_token(grads[:, 0]),
        by_token(grads[:, 1]),
        by_token(grads[:, 2]),
        grad_weight,
    )


def solution(mesh):
    fine = Mesh(np.asarray(mesh.devices).reshape(4, 2, 2, 4, 2), ("y", "zl", "c", "x", "zh"))
    rows = P(VIDEOS, SEQ, None)
    weight = P(SEQ + VIDEOS, None)
    return jax.shard_map(
        local,
        mesh=fine,
        in_specs=(rows, rows, rows, weight, rows, P(), P()),
        out_specs=(rows, rows, rows, rows, weight),
        check_vma=False,
    )
```

time: 237 us -> 214 us (0.903)
  Pallas kernels: 67.8 us -> 55.8 us
  waiting for transfers between devices: 65.6 us -> 54.8 us
  other arithmetic: 17 us -> 13.6 us
  starting transfers between devices: 58.2 us -> 61.2 us
    all_to_all x1 -> x0, waiting for transfers between devices: 10.8 us -> none  [scatter_weight(): lax.all_to_all(rows, ('y', 'zl', 'zh'), split_axis=0, concat_axis=0, tile...]
    ppermute x0 -> x6, starting transfers between devices: none -> 9.76 us  [the longest x3 5.67 us: gather_weight(): lax.ppermute(own, ('zl', 'zh'), pair)]
    ppermute x18 -> x22, waiting for transfers between devices: 42.8 us -> 51.4 us  [shift(): lax.ppermute(value, axis, [(i, (i + step) % size) for i in range(size)])]
    all_to_all x1 -> x0, starting transfers between devices: 8.32 us -> none  [scatter_weight(): lax.all_to_all(rows, ('y', 'zl', 'zh'), split_axis=0, concat_axis=0, tile...]
    all_to_all x1, waiting for transfers between devices: 8.23 us -> 0.01 us  [local(): grads = lax.all_to_all(grads, SEQ, split_axis=0, concat_axis=0, tiled=True)]
    pallas_call x1, Pallas kernels: 33.5 us -> 25.9 us  [run_k1(): pl.pallas_call(k1, grid_spec=pltpu.PrefetchScalarGridSpec(num_scalar_pref...]
    select_n x1 -> x4, other arithmetic: 1.4 us -> 6.15 us  [of_chip(): jnp.where(core == 0, mine, theirs)]
    pallas_call x1, Pallas kernels: 34.4 us -> 29.9 us  [run_k2(): pl.pallas_call(k2, grid_spec=pltpu.PrefetchScalarGridSpec(num_scalar_pref...]
  transfers between devices with their start and end apart: 23 -> 32, of which waited for: 13 -> 14; matrix products, arithmetic and copies ran while one was open for 15% -> 16% of each run, Pallas kernels for 29% -> 26%
where the time goes in v3:
time: 214 us; the launch traced here: 213 us
  starting transfers between devices  61.2 us (29%)
  Pallas kernels  55.8 us (26%)
  waiting for transfers between devices  54.8 us (26%)
  local copies, waits for them, and re-layouts  16.8 us (8%)
  other arithmetic  13.6 us (6%)
  matrix products  9.44 us (4%)
    ppermute x22, waiting for transfers between devices, shift(): lax.ppermute(value, axis, [(i, (i + step) % size) for i in range(size)])  51.4 us
    pallas_call x1, Pallas kernels, run_k2(): pl.pallas_call(k2, grid_spec=pltpu.PrefetchScalarGridSpec(num_scalar_pref...  29.9 us
    ppermute x22, starting transfers between devices, shift(): lax.ppermute(value, axis, [(i, (i + step) % size) for i in range(size)])  29.6 us
    pallas_call x1, Pallas kernels, run_k1(): pl.pallas_call(k1, grid_spec=pltpu.PrefetchScalarGridSpec(num_scalar_pref...  25.9 us
    select_n x4, other arithmetic, of_chip(): jnp.where(core == 0, mine, theirs)  6.15 us
    all_to_all x1, starting transfers between devices, local(): grad = lax.all_to_all(grad, CHIPS, split_axis=0, concat_axis=0, tiled=True)  6.03 us
    all_to_all x1, starting transfers between devices, local(): lax.all_to_all(att.reshape(8, 432, HD), CHIPS, split_axis=0, concat_axis=...  5.68 us
    ppermute x3, starting transfers between devices, gather_weight(): lax.ppermute(own, ('zl', 'zh'), pair)  5.67 us
  transfers between devices with their start and end apart: 32, of which 14 were waited for; matrix products, arithmetic and copies ran while one was open for 16% of the time, Pallas kernels for 26%

profile of v3, /device:TPU:0, one launch (start us, length us, event | category | flops | bytes accessed | tf_op | source)
XLA Modules:
  0.0 212.8 jit_solution(9374155835118753074)
XLA Ops:
  0.6 2.1 collective-permute-start.2
  2.7 2.5 %collective-permute-start.3 = (bf16[16,2048]{1,0:T(8,128)(2,1)}, bf16[16,2048]{1,0:T(8,128)(2,1)S(1)}, u32[]{:S(2)}, u32[]{:S(2)}) collective-permute-start(bf16[16,2048]{1,0:T(8,128)(2,1)} %param.10), channel_id=1, source_target_pairs={{0,17},{1,16},{16,1},{17,0},{2,19},{3,18},{18,3},{19,2},{4,21},{5,... | collective-permute-start | bytes 196616 | tf_op jit(solution)/shard_map/ppermute | solution.py:236
  6.3 1.3 copy.36
  9.4 1.8 collective-permute-done.1
  11.4 3.1 %collective-permute-start.4 = (bf16[2,32,2048]{2,1,0:T(8,128)(2,1)S(1)}, bf16[2,32,2048]{2,1,0:T(8,128)(2,1)S(1)}, u32[]{:S(2)}, u32[]{:S(2)}) collective-permute-start(bf16[2,32,2048]{2,1,0:T(8,128)(2,1)S(1)} %pad_maximum_fusion.5), channel_id=1, source_target_pairs={{0,96},{32,0},{64,32},{96,64},{1,97},{33,1},{65,33},{97,65},{2,98}... | collective-permute-start | bytes 786440 | tf_op jit(solution)/shard_map/ppermute | solution.py:219
  14.5 1.8 pad_maximum_fusion.1
  16.2 2.1 collective-permute-done.4
  18.4 3.8 %collective-permute-start.5 = (bf16[1,32,2048]{2,1,0:T(8,128)(2,1)S(1)}, bf16[1,32,2048]{2,1,0:T(8,128)(2,1)S(1)}, u32[]{:S(2)}, u32[]{:S(2)}) collective-permute-start(bf16[1,32,2048]{2,1,0:T(8,128)(2,1)S(1)} %slice.48), channel_id=1, source_target_pairs={{0,96},{32,0},{64,32},{96,64},{1,97},{33,1},{65,33},{97,65},{2,98}... | collective-permute-start | bytes 393224 | tf_op jit(solution)/shard_map/ppermute | solution.py:219
  22.3 2.4 %collective-permute-done.5 = bf16[1,32,2048]{2,1,0:T(8,128)(2,1)S(1)} collective-permute-done((bf16[1,32,2048]{2,1,0:T(8,128)(2,1)S(1)}, bf16[1,32,2048]{2,1,0:T(8,128)(2,1)S(1)}, u32[]{:S(2)}, u32[]{:S(2)}) %collective-permute-start.5) | collective-permute-done | bytes 131104 | tf_op jit(solution)/shard_map/ppermute | solution.py:219
  24.7 3.7 %collective-permute-done.7 = bf16[1,32,2048]{2,1,0:T(8,128)(2,1)S(1)} collective-permute-done((bf16[1,32,2048]{2,1,0:T(8,128)(2,1)S(1)}, bf16[1,32,2048]{2,1,0:T(8,128)(2,1)S(1)}, u32[]{:S(2)}, u32[]{:S(2)}) %collective-permute-start.7) | collective-permute-done | bytes 131104 | tf_op jit(solution)/shard_map/ppermute | solution.py:219
  28.7 1.6 collective-permute-start.10
  30.3 1.7 collective-permute-start.8
  32.0 4.5 %all-to-all-start = ((bf16[16,3,216,128]{3,2,1,0:T(8,128)(2,1)}), bf16[16,3,216,128]{3,2,1,0:T(8,128)(2,1)}, u32[]{:S(2)}, u32[]{:S(2)}) async-start(bf16[16,3,216,128]{3,2,1,0:T(8,128)(2,1)} %pad_maximum_fusion.1), calls=%async_computation | async-start | bytes 5308416 | tf_op jit(solution)/shard_map/all_to_all | solution.py:278
  37.5 14.3 %collective-permute-done.10 = bf16[8,32,2048]{2,1,0:T(8,128)(2,1)S(1)} collective-permute-done((bf16[8,32,2048]{2,1,0:T(8,128)(2,1)S(1)}, bf16[8,32,2048]{2,1,0:T(8,128)(2,1)S(1)}, u32[]{:S(2)}, u32[]{:S(2)}) %collective-permute-start.10) | collective-permute-done | bytes 1048608 | tf_op jit(solution)/shard_map/ppermute | solution.py:219
  51.9 1.6 collective-permute-start.11
  54.6 1.8 collective-permute-start.9
  56.4 1.4 broadcast_select_fusion.7
  57.8 4.6 %collective-permute-done.11 = bf16[4,32,2048]{2,1,0:T(8,128)(2,1)S(1)} collective-permute-done((bf16[4,32,2048]{2,1,0:T(8,128)(2,1)S(1)}, bf16[4,32,2048]{2,1,0:T(8,128)(2,1)S(1)}, u32[]{:S(2)}, u32[]{:S(2)}) %collective-permute-start.11) | collective-permute-done | bytes 524320 | tf_op jit(solution)/shard_map/ppermute | solution.py:219
  62.4 1.4 collective-permute-done.9
  63.8 1.6 pad_maximum_fusion
  65.5 2.1 fusion.15
  68.7 1.5 all-to-all-done.qkv_ref
  70.3 6.0 %all-to-all-start.1 = ((bf16[8,432,128]{2,1,0:T(8,128)(2,1)}), bf16[8,432,128]{2,1,0:T(8,128)(2,1)S(1)}, u32[]{:S(2)}, u32[]{:S(2)}) async-start(bf16[8,432,128]{2,1,0:T(8,128)(2,1)} %bitcast.112), calls=%async_computation.1 | async-start | bytes 1769472 | tf_op jit(solution)/shard_map/all_to_all | solution.py:292
  76.3 25.9 %attend.1 = (bf16[16,216,128]{2,1,0:T(8,128)(2,1)}, bf16[3456,128]{1,0:T(8,128)(2,1)}, bf16[3456,128]{1,0:T(8,128)(2,1)}, bf16[3456,128]{1,0:T(8,128)(2,1)}, f32...) custom-call(s32[3456]{0:T(1024)} %order_ref.3, s32[162]{0:T(256)} %reshape.171.neigh_ref, ...), custom_call_target="tpu_custom_call" | custom-call | flops 30000001024 | bytes 20000000 | tf_op jit(solution)/shard_map/attend/pallas_call | solution.py:102
  102.6 2.7 %collective-permute-start.13 = (bf16[216,2048]{1,0:T(8,128)(2,1)S(1)}, bf16[216,2048]{1,0:T(8,128)(2,1)}, u32[]{:S(2)}, u32[]{:S(2)}) collective-permute-start(bf16[216,2048]{1,0:T(8,128)(2,1)S(1)} %bitcast.134), channel_id=1, source_target_pairs={{0,4},{2,6},{4,0},{6,2},{1,5},{3,7},{5,1},{7,3},{8,12},{10,14},{12... | collective-permute-start | bytes 2654216 | tf_op jit(solution)/shard_map/ppermute | solution.py:219
  105.3 1.4 collective-permute-start.14
  106.8 5.7 %all-to-all-start.2 = ((bf16[8,432,128]{2,1,0:T(8,128)(2,1)}), bf16[8,432,128]{2,1,0:T(8,128)(2,1)S(1)}, u32[]{:S(2)}, u32[]{:S(2)}) async-start(bf16[8,432,128]{2,1,0:T(8,128)(2,1)} %bitcast.131), calls=%async_computation.2 | async-start | bytes 1769472 | tf_op jit(solution)/shard_map/all_to_all | solution.py:297
  112.4 29.9 %attend_grad.1 = bf16[16,3,216,128]{3,2,1,0:T(8,128)(2,1)} custom-call(s32[3456]{0:T(1024)} %order_ref.3, s32[162]{0:T(256)} %reshape.171.neigh_ref, s32[1]{0:T(128)} %bitcast.turn_ref, bf16[16,216,128]{2,1,0:T(8,128)(2,1)} %bitcast.130, bf16[3456,128]{1,0:T(8,128)(2,1)} %get-tuple-element.37.qp_ref, bf16[3456,128]{1,0:T(8,128)(2,1)} %get-tuple-element.38.kp_ref, ...), custom_call_target="tpu_custom_call" | custom-call | flops 30000001024 | bytes 20000000 | tf_op jit(solution)/shard_map/attend_grad/pallas_call | solution.py:167
  145.3 5.6 %all-to-all-start.3 = ((bf16[16,3,216,128]{3,2,1,0:T(8,128)(2,1)}), bf16[16,3,216,128]{3,2,1,0:T(8,128)(2,1)S(1)}, u32[]{:S(2)}, u32[]{:S(2)}) async-start(bf16[16,3,216,128]{3,2,1,0:T(8,128)(2,1)} %attend_grad.1), calls=%async_computation.3 | async-start | bytes 5308416 | tf_op jit(solution)/shard_map/all_to_all | solution.py:301
  150.9 2.3 %copy.29 = bf16[432,1024]{0,1:T(8,128)(2,1)} copy(bf16[432,1024]{1,0:T(8,128)(2,1)} %copy_bitcast_fusion) | data formatting | bytes 1769472 | tf_op jit(solution)/shard_map/optimization_barrier | solution.py:304
  153.2 4.4 %fusion.31 = f32[432,2048]{1,0:T(8,128)S(1)} fusion(bf16[432,1024]{1,0:T(8,128)(2,1)} %copy_bitcast_fusion, bf16[1024,2048]{1,0:T(8,128)(2,1)} %bitcast.117), kind=kOutput, calls=%fused_computation.79 | convolution fusion | flops 1811939328 | bytes 8617984 | tf_op jit(solution)/shard_map/dot_general | solution.py:313
  157.7 1.6 broadcast_select_fusion.5
  160.7 2.9 %collective-permute-start.18 = (bf16[432,256]{0,1:T(8,128)(2,1)S(1)}, bf16[432,256]{0,1:T(8,128)(2,1)S(1)}, u32[]{:S(2)}, u32[]{:S(2)}) collective-permute-start(bf16[432,256]{0,1:T(8,128)(2,1)S(1)} %bitcast.137), channel_id=1, source_target_pairs={{0,4},{2,6},{4,0},{6,2},{1,5},{3,7},{5,1},{7,3},{8,12},{10,14},{12... | collective-permute-start | bytes 663560 | tf_op jit(solution)/shard_map/ppermute | solution.py:219
  164.5 1.6 broadcast_select_fusion.3
  166.0 1.6 broadcast_select_fusion.1
  167.6 1.8 collective-permute-done.17
  170.1 5.8 %collective-permute-done.18 = bf16[432,256]{0,1:T(8,128)(2,1)S(1)} collective-permute-done((bf16[432,256]{0,1:T(8,128)(2,1)S(1)}, bf16[432,256]{0,1:T(8,128)(2,1)S(1)}, u32[]{:S(2)}, u32[]{:S(2)}) %collective-permute-start.18) | collective-permute-done | bytes 221216 | tf_op jit(solution)/shard_map/ppermute | solution.py:219
  178.7 1.7 collective-permute-start.22
  180.4 2.7 %collective-permute-start.23 = (bf16[4,16,2048]{2,1,0:T(8,128)(2,1)S(1)}, bf16[4,16,2048]{2,1,0:T(8,128)(2,1)S(1)}, u32[]{:S(2)}, u32[]{:S(2)}) collective-permute-start(bf16[4,16,2048]{2,1,0:T(8,128)(2,1)S(1)} %get-tuple-element.67), channel_id=1, source_target_pairs={{0,64},{32,96},{64,0},{96,32},{1,65},{33,97},{65,1},{97,33},{2,66}... | collective-permute-start | bytes 786440 | tf_op jit(solution)/shard_map/ppermute | solution.py:219
  183.1 1.5 collective-permute-start.24
  185.7 8.6 %collective-permute-done.22 = bf16[4,16,2048]{2,1,0:T(8,128)(2,1)S(1)} collective-permute-done((bf16[4,16,2048]{2,1,0:T(8,128)(2,1)S(1)}, bf16[4,16,2048]{2,1,0:T(8,128)(2,1)S(1)}, u32[]{:S(2)}, u32[]{:S(2)}) %collective-permute-start.22) | collective-permute-done | bytes 262176 | tf_op jit(solution)/shard_map/ppermute | solution.py:219
  194.3 5.2 %collective-permute-done.23 = bf16[4,16,2048]{2,1,0:T(8,128)(2,1)S(1)} collective-permute-done((bf16[4,16,2048]{2,1,0:T(8,128)(2,1)S(1)}, bf16[4,16,2048]{2,1,0:T(8,128)(2,1)S(1)}, u32[]{:S(2)}, u32[]{:S(2)}) %collective-permute-start.23) | collective-permute-done | bytes 262176 | tf_op jit(solution)/shard_map/ppermute | solution.py:219
  201.4 1.5 collective-permute-start.25
  203.0 2.6 %collective-permute-start.27 = (bf16[16,2048]{1,0:T(8,128)(2,1)}, bf16[16,2048]{1,0:T(8,128)(2,1)}, u32[]{:S(2)}, u32[]{:S(2)}) collective-permute-start(bf16[16,2048]{1,0:T(8,128)(2,1)} %get-tuple-element.74), channel_id=1, source_target_pairs={{0,17},{1,16},{16,1},{17,0},{2,19},{3,18},{18,3},{19,2},{4,21},{5,... | collective-permute-start | bytes 196616 | tf_op jit(solution)/shard_map/ppermute | solution.py:262
  205.5 1.4 slice_bitcast_fusion
  207.1 1.3 reshape.180
  209.9 1.3 reshape.182
  211.2 1.6 fusion.24
  (103 shorter events, 20.3 us)
Async XLA Ops:
  0.6 7.0 %copy-start.8 = (bf16[1,216,2048]{2,1,0:T(8,128)(2,1)S(1)}, bf16[1,216,2048]{2,1,0:T(8,128)(2,1)}, u32[]{:S(2)}) copy-start(bf16[1,216,2048]{2,1,0:T(8,128)(2,1)} %param.9) | copy-start | bytes 2654212
  0.6 10.6 %collective-permute-start.2 = (bf16[16,2048]{1,0:T(8,128)(2,1)}, bf16[16,2048]{1,0:T(8,128)(2,1)S(1)}, u32[]{:S(2)}, u32[]{:S(2)}) collective-permute-start(bf16[16,2048]{1,0:T(8,128)(2,1)} %param.10), channel_id=1, source_target_pairs={{0,16},{1,17},{16,0},{17,1},{2,18},{3,19},{18,2},{19,3},{4,20},{5,... | collective-permute-start | bytes 196616 | tf_op jit(solution)/shard_map/ppermute | solution.py:236
  2.7 8.5 %collective-permute-start.3 = (bf16[16,2048]{1,0:T(8,128)(2,1)}, bf16[16,2048]{1,0:T(8,128)(2,1)S(1)}, u32[]{:S(2)}, u32[]{:S(2)}) collective-permute-start(bf16[16,2048]{1,0:T(8,128)(2,1)} %param.10), channel_id=1, source_target_pairs={{0,17},{1,16},{16,1},{17,0},{2,19},{3,18},{18,3},{19,2},{4,21},{5,... | collective-permute-start | bytes 196616 | tf_op jit(solution)/shard_map/ppermute | solution.py:236
  5.2 6.0 %collective-permute-start.1 = (bf16[16,2048]{1,0:T(8,128)(2,1)}, bf16[16,2048]{1,0:T(8,128)(2,1)S(1)}, u32[]{:S(2)}, u32[]{:S(2)}) collective-permute-start(bf16[16,2048]{1,0:T(8,128)(2,1)} %param.10), channel_id=1, source_target_pairs={{0,1},{1,0},{16,17},{17,16},{2,3},{3,2},{18,19},{19,18},{4,5},{5,4... | collective-permute-start | bytes 196616 | tf_op jit(solution)/shard_map/ppermute | solution.py:236
  7.8 1.2 copy-start.9
  8.3 2.9 %copy-start.14 = (bf16[16,2048]{1,0:T(8,128)(2,1)S(1)}, bf16[16,2048]{1,0:T(8,128)(2,1)}, u32[]{:S(2)}) copy-start(bf16[16,2048]{1,0:T(8,128)(2,1)} %param.10) | copy-start | bytes 196612
  11.4 7.0 %collective-permute-start.4 = (bf16[2,32,2048]{2,1,0:T(8,128)(2,1)S(1)}, bf16[2,32,2048]{2,1,0:T(8,128)(2,1)S(1)}, u32[]{:S(2)}, u32[]{:S(2)}) collective-permute-start(bf16[2,32,2048]{2,1,0:T(8,128)(2,1)S(1)} %pad_maximum_fusion.5), channel_id=1, source_target_pairs={{0,96},{32,0},{64,32},{96,64},{1,97},{33,1},{65,33},{97,65},{2,98}... | collective-permute-start | bytes 786440 | tf_op jit(solution)/shard_map/ppermute | solution.py:219
  14.5 7.7 %collective-permute-start.6 = (bf16[2,32,2048]{2,1,0:T(8,128)(2,1)S(1)}, bf16[2,32,2048]{2,1,0:T(8,128)(2,1)S(1)}, u32[]{:S(2)}, u32[]{:S(2)}) collective-permute-start(bf16[2,32,2048]{2,1,0:T(8,128)(2,1)S(1)} %pad_maximum_fusion.5), channel_id=1, source_target_pairs={{0,32},{32,64},{64,96},{96,0},{1,33},{33,65},{65,97},{97,1},{2,34}... | collective-permute-start | bytes 786440 | tf_op jit(solution)/shard_map/ppermute | solution.py:219
  18.4 6.3 %collective-permute-start.5 = (bf16[1,32,2048]{2,1,0:T(8,128)(2,1)S(1)}, bf16[1,32,2048]{2,1,0:T(8,128)(2,1)S(1)}, u32[]{:S(2)}, u32[]{:S(2)}) collective-permute-start(bf16[1,32,2048]{2,1,0:T(8,128)(2,1)S(1)} %slice.48), channel_id=1, source_target_pairs={{0,96},{32,0},{64,32},{96,64},{1,97},{33,1},{65,33},{97,65},{2,98}... | collective-permute-start | bytes 393224 | tf_op jit(solution)/shard_map/ppermute | solution.py:219
  22.1 6.2 %collective-permute-start.7 = (bf16[1,32,2048]{2,1,0:T(8,128)(2,1)S(1)}, bf16[1,32,2048]{2,1,0:T(8,128)(2,1)S(1)}, u32[]{:S(2)}, u32[]{:S(2)}) collective-permute-start(bf16[1,32,2048]{2,1,0:T(8,128)(2,1)S(1)} %slice.49), channel_id=1, source_target_pairs={{0,32},{32,64},{64,96},{96,0},{1,33},{33,65},{65,97},{97,1},{2,34}... | collective-permute-start | bytes 393224 | tf_op jit(solution)/shard_map/ppermute | solution.py:219
  28.7 7.8 %copy-start.11 = (bf16[1,216,2048]{2,1,0:T(8,128)(2,1)S(1)}, bf16[1,216,2048]{2,1,0:T(8,128)(2,1)}, u32[]{:S(2)}) copy-start(bf16[1,216,2048]{2,1,0:T(8,128)(2,1)} %param.11) | copy-start | bytes 2654212
  28.7 8.1 %copy-start.15 = (s32[18,9]{0,1:T(8,128)S(1)}, s32[18,9]{0,1:T(8,128)}, u32[]{:S(2)}) copy-start(s32[18,9]{0,1:T(8,128)} %param.12) | copy-start | bytes 1948
  28.7 23.2 %collective-permute-start.10 = (bf16[8,32,2048]{2,1,0:T(8,128)(2,1)S(1)}, bf16[8,32,2048]{2,1,0:T(8,128)(2,1)S(1)}, u32[]{:S(2)}, u32[]{:S(2)}) collective-permute-start(bf16[8,32,2048]{2,1,0:T(8,128)(2,1)S(1)} %bitcast.119), channel_id=1, source_target_pairs={{0,2},{2,4},{4,6},{6,0},{1,3},{3,5},{5,7},{7,1},{8,10},{10,12},{12... | collective-permute-start | bytes 3145736 | tf_op jit(solution)/shard_map/ppermute | solution.py:219
  30.3 23.2 %collective-permute-start.8 = (bf16[8,32,2048]{2,1,0:T(8,128)(2,1)S(1)}, bf16[8,32,2048]{2,1,0:T(8,128)(2,1)}, u32[]{:S(2)}, u32[]{:S(2)}) collective-permute-start(bf16[8,32,2048]{2,1,0:T(8,128)(2,1)S(1)} %bitcast.120), channel_id=1, source_target_pairs={{0,6},{2,0},{4,2},{6,4},{1,7},{3,1},{5,3},{7,5},{8,14},{10,8},{12,... | collective-permute-start | bytes 3145736 | tf_op jit(solution)/shard_map/ppermute | solution.py:219
  32.0 38.3 %all-to-all-start = ((bf16[16,3,216,128]{3,2,1,0:T(8,128)(2,1)}), bf16[16,3,216,128]{3,2,1,0:T(8,128)(2,1)}, u32[]{:S(2)}, u32[]{:S(2)}) async-start(bf16[16,3,216,128]{3,2,1,0:T(8,128)(2,1)} %pad_maximum_fusion.1), calls=%async_computation | async-start | bytes 5308416 | tf_op jit(solution)/shard_map/all_to_all | solution.py:278
  36.5 19.9 %collective-permute-start = (bf16[216,2048]{1,0:T(8,128)(2,1)S(1)}, bf16[216,2048]{1,0:T(8,128)(2,1)}, u32[]{:S(2)}, u32[]{:S(2)}) collective-permute-start(bf16[216,2048]{1,0:T(8,128)(2,1)S(1)} %bitcast.132), channel_id=1, source_target_pairs={{0,8},{8,0},{1,9},{9,1},{2,10},{10,2},{3,11},{11,3},{4,12},{12,4},... | collective-permute-start | bytes 2654216 | tf_op jit(solution)/shard_map/ppermute | solution.py:219
  37.5 18.8 %copy-start.12 = (bf16[1,216,2048]{2,1,0:T(8,128)(2,1)S(1)}, bf16[1,216,2048]{2,1,0:T(8,128)(2,1)}, u32[]{:S(2)}) copy-start(bf16[1,216,2048]{2,1,0:T(8,128)(2,1)} %param.11) | copy-start | bytes 2654212
  51.9 10.5 %collective-permute-start.11 = (bf16[4,32,2048]{2,1,0:T(8,128)(2,1)S(1)}, bf16[4,32,2048]{2,1,0:T(8,128)(2,1)S(1)}, u32[]{:S(2)}, u32[]{:S(2)}) collective-permute-start(bf16[4,32,2048]{2,1,0:T(8,128)(2,1)S(1)} %slice.51), channel_id=1, source_target_pairs={{0,2},{2,4},{4,6},{6,0},{1,3},{3,5},{5,7},{7,1},{8,10},{10,12},{12... | collective-permute-start | bytes 1572872 | tf_op jit(solution)/shard_map/ppermute | solution.py:219
  54.6 9.2 %collective-permute-start.9 = (bf16[4,32,2048]{2,1,0:T(8,128)(2,1)S(1)}, bf16[4,32,2048]{2,1,0:T(8,128)(2,1)S(1)}, u32[]{:S(2)}, u32[]{:S(2)}) collective-permute-start(bf16[4,32,2048]{2,1,0:T(8,128)(2,1)S(1)} %slice.50), channel_id=1, source_target_pairs={{0,6},{2,0},{4,2},{6,4},{1,7},{3,1},{5,3},{7,5},{8,14},{10,8},{12,... | collective-permute-start | bytes 1572872 | tf_op jit(solution)/shard_map/ppermute | solution.py:219
  57.8 7.7 %copy-start.3 = (bf16[216,2048]{1,0:T(8,128)(2,1)}, bf16[216,2048]{1,0:T(8,128)(2,1)S(1)}, u32[]{:S(2)}) copy-start(bf16[216,2048]{1,0:T(8,128)(2,1)S(1)} %get-tuple-element.65) | copy-start | bytes 2654212
  65.4 2.1 copy-start.1
  70.3 32.0 %all-to-all-start.1 = ((bf16[8,432,128]{2,1,0:T(8,128)(2,1)}), bf16[8,432,128]{2,1,0:T(8,128)(2,1)S(1)}, u32[]{:S(2)}, u32[]{:S(2)}) async-start(bf16[8,432,128]{2,1,0:T(8,128)(2,1)} %bitcast.112), calls=%async_computation.1 | async-start | bytes 1769472 | tf_op jit(solution)/shard_map/all_to_all | solution.py:292
  76.3 25.9 %copy-start.13 = (bf16[1,216,2048]{2,1,0:T(8,128)(2,1)S(1)}, bf16[1,216,2048]{2,1,0:T(8,128)(2,1)}, u32[]{:S(2)}) copy-start(bf16[1,216,2048]{2,1,0:T(8,128)(2,1)} %param.11) | copy-start | bytes 2654212
  102.2 10.2 %copy-start.10 = (bf16[8,432,128]{2,1,0:T(8,128)(2,1)}, bf16[8,432,128]{2,1,0:T(8,128)(2,1)S(1)}, u32[]{:S(2)}) copy-start(bf16[8,432,128]{2,1,0:T(8,128)(2,1)S(1)} %all-to-all-done.1) | copy-start | bytes 2654212
  102.2 41.9 %collective-permute-start.12 = (bf16[216,2048]{1,0:T(8,128)(2,1)S(1)}, bf16[216,2048]{1,0:T(8,128)(2,1)}, u32[]{:S(2)}, u32[]{:S(2)}) collective-permute-start(bf16[216,2048]{1,0:T(8,128)(2,1)S(1)} %bitcast.133), channel_id=1, source_target_pairs={{0,2},{2,4},{4,6},{6,0},{1,3},{3,5},{5,7},{7,1},{8,10},{10,12},{12... | collective-permute-start | bytes 2654216 | tf_op jit(solution)/shard_map/ppermute | solution.py:219
  102.6 41.6 %collective-permute-start.13 = (bf16[216,2048]{1,0:T(8,128)(2,1)S(1)}, bf16[216,2048]{1,0:T(8,128)(2,1)}, u32[]{:S(2)}, u32[]{:S(2)}) collective-permute-start(bf16[216,2048]{1,0:T(8,128)(2,1)S(1)} %bitcast.134), channel_id=1, source_target_pairs={{0,4},{2,6},{4,0},{6,2},{1,5},{3,7},{5,1},{7,3},{8,12},{10,14},{12... | collective-permute-start | bytes 2654216 | tf_op jit(solution)/shard_map/ppermute | solution.py:219
  105.3 39.5 %collective-permute-start.14 = (bf16[216,2048]{1,0:T(8,128)(2,1)S(1)}, bf16[216,2048]{1,0:T(8,128)(2,1)}, u32[]{:S(2)}, u32[]{:S(2)}) collective-permute-start(bf16[216,2048]{1,0:T(8,128)(2,1)S(1)} %bitcast.135), channel_id=1, source_target_pairs={{0,6},{2,0},{4,2},{6,4},{1,7},{3,1},{5,3},{7,5},{8,14},{10,8},{12,... | collective-permute-start | bytes 2654216 | tf_op jit(solution)/shard_map/ppermute | solution.py:219
  106.8 35.6 %all-to-all-start.2 = ((bf16[8,432,128]{2,1,0:T(8,128)(2,1)}), bf16[8,432,128]{2,1,0:T(8,128)(2,1)S(1)}, u32[]{:S(2)}, u32[]{:S(2)}) async-start(bf16[8,432,128]{2,1,0:T(8,128)(2,1)} %bitcast.131), calls=%async_computation.2 | async-start | bytes 1769472 | tf_op jit(solution)/shard_map/all_to_all | solution.py:297
  144.8 6.2 %collective-permute-start.15 = (bf16[216,2048]{1,0:T(8,128)(2,1)}, bf16[216,2048]{1,0:T(8,128)(2,1)}, u32[]{:S(2)}, u32[]{:S(2)}) collective-permute-start(bf16[216,2048]{1,0:T(8,128)(2,1)} %collective-permute-done.12), channel_id=1, source_target_pairs={{0,8},{8,0},{1,9},{9,1},{2,10},{10,2},{3,11},{11,3},{4,12},{12,4},... | collective-permute-start | bytes 2654216 | tf_op jit(solution)/shard_map/ppermute | solution.py:219
  144.8 19.4 %collective-permute-start.19 = (bf16[216,2048]{1,0:T(8,128)(2,1)}, bf16[216,2048]{1,0:T(8,128)(2,1)}, u32[]{:S(2)}, u32[]{:S(2)}) collective-permute-start(bf16[216,2048]{1,0:T(8,128)(2,1)} %collective-permute-done.13), channel_id=1, source_target_pairs={{0,8},{8,0},{1,9},{9,1},{2,10},{10,2},{3,11},{11,3},{4,12},{12,4},... | collective-permute-start | bytes 2654216 | tf_op jit(solution)/shard_map/ppermute | solution.py:219
  145.3 20.8 %collective-permute-start.21 = (bf16[216,2048]{1,0:T(8,128)(2,1)}, bf16[216,2048]{1,0:T(8,128)(2,1)}, u32[]{:S(2)}, u32[]{:S(2)}) collective-permute-start(bf16[216,2048]{1,0:T(8,128)(2,1)} %collective-permute-done.14), channel_id=1, source_target_pairs={{0,8},{8,0},{1,9},{9,1},{2,10},{10,2},{3,11},{11,3},{4,12},{12,4},... | collective-permute-start | bytes 2654216 | tf_op jit(solution)/shard_map/ppermute | solution.py:219
  145.3 54.2 %all-to-all-start.3 = ((bf16[16,3,216,128]{3,2,1,0:T(8,128)(2,1)}), bf16[16,3,216,128]{3,2,1,0:T(8,128)(2,1)S(1)}, u32[]{:S(2)}, u32[]{:S(2)}) async-start(bf16[16,3,216,128]{3,2,1,0:T(8,128)(2,1)} %attend_grad.1), calls=%async_computation.3 | async-start | bytes 5308416 | tf_op jit(solution)/shard_map/all_to_all | solution.py:301
  157.6 1.8 copy-start.2
  159.5 9.9 %collective-permute-start.17 = (bf16[432,256]{0,1:T(8,128)(2,1)S(1)}, bf16[432,256]{0,1:T(8,128)(2,1)S(1)}, u32[]{:S(2)}, u32[]{:S(2)}) collective-permute-start(bf16[432,256]{0,1:T(8,128)(2,1)S(1)} %bitcast.138), channel_id=1, source_target_pairs={{0,2},{2,4},{4,6},{6,0},{1,3},{3,5},{5,7},{7,1},{8,10},{10,12},{12... | collective-permute-start | bytes 663560 | tf_op jit(solution)/shard_map/ppermute | solution.py:219
  160.7 15.2 %collective-permute-start.18 = (bf16[432,256]{0,1:T(8,128)(2,1)S(1)}, bf16[432,256]{0,1:T(8,128)(2,1)S(1)}, u32[]{:S(2)}, u32[]{:S(2)}) collective-permute-start(bf16[432,256]{0,1:T(8,128)(2,1)S(1)} %bitcast.137), channel_id=1, source_target_pairs={{0,4},{2,6},{4,0},{6,2},{1,5},{3,7},{5,1},{7,3},{8,12},{10,14},{12... | collective-permute-start | bytes 663560 | tf_op jit(solution)/shard_map/ppermute | solution.py:219
  163.7 12.9 %collective-permute-start.20 = (bf16[432,256]{0,1:T(8,128)(2,1)S(1)}, bf16[432,256]{0,1:T(8,128)(2,1)S(1)}, u32[]{:S(2)}, u32[]{:S(2)}) collective-permute-start(bf16[432,256]{0,1:T(8,128)(2,1)S(1)} %bitcast.136), channel_id=1, source_target_pairs={{0,6},{2,0},{4,2},{6,4},{1,7},{3,1},{5,3},{7,5},{8,14},{10,8},{12,... | collective-permute-start | bytes 663560 | tf_op jit(solution)/shard_map/ppermute | solution.py:219
  164.2 20.4 %collective-permute-start.16 = (bf16[216,2048]{1,0:T(8,128)(2,1)S(1)}, bf16[216,2048]{1,0:T(8,128)(2,1)S(1)}, u32[]{:S(2)}, u32[]{:S(2)}) collective-permute-start(bf16[216,2048]{1,0:T(8,128)(2,1)S(1)} %dynamic-slice_convert_fusion), channel_id=1, source_target_pairs={{0,8},{8,0},{1,9},{9,1},{2,10},{10,2},{3,11},{11,3},{4,12},{12,4},... | collective-permute-start | bytes 2654216 | tf_op jit(solution)/shard_map/ppermute | solution.py:219
  176.6 1.2 copy-start.4
  178.6 7.1 %copy-start = (bf16[256,2048]{1,0:T(8,128)(2,1)}, bf16[256,2048]{1,0:T(8,128)(2,1)S(1)}, u32[]{:S(2)}) copy-start(bf16[256,2048]{1,0:T(8,128)(2,1)S(1)} %fusion.2) | copy-start | bytes 3145732
  178.7 15.6 %collective-permute-start.22 = (bf16[4,16,2048]{2,1,0:T(8,128)(2,1)S(1)}, bf16[4,16,2048]{2,1,0:T(8,128)(2,1)S(1)}, u32[]{:S(2)}, u32[]{:S(2)}) collective-permute-start(bf16[4,16,2048]{2,1,0:T(8,128)(2,1)S(1)} %get-tuple-element.68), channel_id=1, source_target_pairs={{0,32},{32,64},{64,96},{96,0},{1,33},{33,65},{65,97},{97,1},{2,34}... | collective-permute-start | bytes 786440 | tf_op jit(solution)/shard_map/ppermute | solution.py:219
  180.4 19.1 %collective-permute-start.23 = (bf16[4,16,2048]{2,1,0:T(8,128)(2,1)S(1)}, bf16[4,16,2048]{2,1,0:T(8,128)(2,1)S(1)}, u32[]{:S(2)}, u32[]{:S(2)}) collective-permute-start(bf16[4,16,2048]{2,1,0:T(8,128)(2,1)S(1)} %get-tuple-element.67), channel_id=1, source_target_pairs={{0,64},{32,96},{64,0},{96,32},{1,65},{33,97},{65,1},{97,33},{2,66}... | collective-permute-start | bytes 786440 | tf_op jit(solution)/shard_map/ppermute | solution.py:219
  183.1 16.4 %collective-permute-start.24 = (bf16[4,16,2048]{2,1,0:T(8,128)(2,1)S(1)}, bf16[4,16,2048]{2,1,0:T(8,128)(2,1)}, u32[]{:S(2)}, u32[]{:S(2)}) collective-permute-start(bf16[4,16,2048]{2,1,0:T(8,128)(2,1)S(1)} %get-tuple-element.66), channel_id=1, source_target_pairs={{0,96},{32,0},{64,32},{96,64},{1,97},{33,1},{65,33},{97,65},{2,98}... | collective-permute-start | bytes 786440 | tf_op jit(solution)/shard_map/ppermute | solution.py:219
  200.7 2.3 %copy-start.7 = (bf16[4,16,2048]{2,1,0:T(8,128)(2,1)}, bf16[4,16,2048]{2,1,0:T(8,128)(2,1)S(1)}, u32[]{:S(2)}) copy-start(bf16[4,16,2048]{2,1,0:T(8,128)(2,1)S(1)} %fusion.19) | copy-start | bytes 786436
  201.4 9.7 %collective-permute-start.25 = (bf16[16,2048]{1,0:T(8,128)(2,1)}, bf16[16,2048]{1,0:T(8,128)(2,1)}, u32[]{:S(2)}, u32[]{:S(2)}) collective-permute-start(bf16[16,2048]{1,0:T(8,128)(2,1)} %get-tuple-element.73), channel_id=1, source_target_pairs={{0,1},{1,0},{16,17},{17,16},{2,3},{3,2},{18,19},{19,18},{4,5},{5,4... | collective-permute-start | bytes 196616 | tf_op jit(solution)/shard_map/ppermute | solution.py:262
  203.0 8.2 %collective-permute-start.26 = (bf16[16,2048]{1,0:T(8,128)(2,1)}, bf16[16,2048]{1,0:T(8,128)(2,1)}, u32[]{:S(2)}, u32[]{:S(2)}) collective-permute-start(bf16[16,2048]{1,0:T(8,128)(2,1)} %get-tuple-element.75), channel_id=1, source_target_pairs={{0,16},{1,17},{16,0},{17,1},{2,18},{3,19},{18,2},{19,3},{4,20},{5,... | collective-permute-start | bytes 196616 | tf_op jit(solution)/shard_map/ppermute | solution.py:262
  203.0 8.2 %collective-permute-start.27 = (bf16[16,2048]{1,0:T(8,128)(2,1)}, bf16[16,2048]{1,0:T(8,128)(2,1)}, u32[]{:S(2)}, u32[]{:S(2)}) collective-permute-start(bf16[16,2048]{1,0:T(8,128)(2,1)} %get-tuple-element.74), channel_id=1, source_target_pairs={{0,17},{1,16},{16,1},{17,0},{2,19},{3,18},{18,3},{19,2},{4,21},{5,... | collective-permute-start | bytes 196616 | tf_op jit(solution)/shard_map/ppermute | solution.py:262
  206.9 1.4 copy-start.6
  208.3 1.4 copy-start.5

commit v4 on v3

--- a/solution.py
+++ b/solution.py
@@ -232,11 +232,18 @@
 
 
 def gather_weight(own, qkv):
-    pairs = [[(i, i ^ flip) for i in range(4)] for flip in (1, 2, 3)]
-    next_zh, next_zl, next_both = (lax.ppermute(own, ("zl", "zh"), pair) for pair in pairs)
-    w = in_place("zl", in_place("zh", own, next_zh)[None], in_place("zh", next_zl, next_both)[None])
+    def along_z(value):
+        next_zh, next_zl, next_both = (
+            lax.ppermute(value, ("zl", "zh"), [(i, i ^ flip) for i in range(4)]) for flip in (1, 2, 3)
+        )
+        return in_place(
+            "zl", in_place("zh", value, next_zh)[None], in_place("zh", next_zl, next_both)[None]
+        )
+
+    opposite = shift(own, "y", 4, 2)
+    w = along_z(own)
     y = lax.axis_index("y")
-    ring = jnp.stack([w] + around(w, "y"))
+    ring = jnp.stack([w, shift(w, "y", 4, -1), along_z(opposite), shift(w, "y", 4, 1)])
     ring = jnp.concatenate([ring, ring], axis=0)
     w = lax.dynamic_slice_in_dim(ring, 4 - y, 4, 0).reshape(8, 32, 2048)
     w, qkv = lax.optimization_barrier((w, qkv))

time: 214 us -> 211 us (0.986)
  waiting for transfers between devices: 54.8 us -> 52.4 us
    ppermute x3 -> x6, starting transfers between devices: 5.67 us -> 9.84 us  [along_z(): lax.ppermute(value, ('zl', 'zh'), [(i, i ^ flip) for i in range(4)])]
    ppermute x22 -> x21, waiting for transfers between devices: 51.4 us -> 47.6 us  [shift(): lax.ppermute(value, axis, [(i, (i + step) % size) for i in range(size)])]
    ppermute x3 -> x6, waiting for transfers between devices: 1.81 us -> 4.86 us  [along_z(): lax.ppermute(value, ('zl', 'zh'), [(i, i ^ flip) for i in range(4)])]
    ppermute x22 -> x21, starting transfers between devices: 29.6 us -> 27.3 us  [shift(): lax.ppermute(value, axis, [(i, (i + step) % size) for i in range(size)])]
  transfers between devices with their start and end apart: 32 -> 34, of which waited for: 14 -> 12; matrix products, arithmetic and copies ran while one was open for 16% -> 17% of each run, Pallas kernels for 26% -> 27%
where the time goes in v4:
time: 211 us; the launch traced here: 210 us
  starting transfers between devices  61.6 us (29%)
  Pallas kernels  55.8 us (26%)
  waiting for transfers between devices  52.4 us (25%)
  local copies, waits for them, and re-layouts  16.1 us (8%)
  other arithmetic  13.6 us (6%)
  matrix products  9.44 us (4%)
    ppermute x21, waiting for transfers between devices, shift(): lax.ppermute(value, axis, [(i, (i + step) % size) for i in range(size)])  47.6 us
    pallas_call x1, Pallas kernels, run_k2(): pl.pallas_call(k2, grid_spec=pltpu.PrefetchScalarGridSpec(num_scalar_pref...  29.9 us
    ppermute x21, starting transfers between devices, shift(): lax.ppermute(value, axis, [(i, (i + step) % size) for i in range(size)])  27.3 us
    pallas_call x1, Pallas kernels, run_k1(): pl.pallas_call(k1, grid_spec=pltpu.PrefetchScalarGridSpec(num_scalar_pref...  26 us
    ppermute x6, starting transfers between devices, along_z(): lax.ppermute(value, ('zl', 'zh'), [(i, i ^ flip) for i in range(4)])  9.84 us
    select_n x4, other arithmetic, of_chip(): jnp.where(core == 0, mine, theirs)  6.15 us
    all_to_all x1, starting transfers between devices, local(): lax.all_to_all(att.reshape(8, 432, HD), CHIPS, split_axis=0, concat_axis=...  5.68 us
    all_to_all x1, starting transfers between devices, local(): grads = lax.all_to_all(grads, SEQ, split_axis=0, concat_axis=0, tiled=True)  5.63 us
  transfers between devices with their start and end apart: 34, of which 12 were waited for; matrix products, arithmetic and copies ran while one was open for 17% of the time, Pallas kernels for 27%

profile of v4, /device:TPU:0, one launch (start us, length us, event | category | flops | bytes accessed | tf_op | source)
XLA Modules:
  0.0 210.1 jit_solution(16139529015577616414)
XLA Ops:
  0.7 2.1 collective-permute-start.2
  2.7 2.5 %collective-permute-start.3 = (bf16[16,2048]{1,0:T(8,128)(2,1)}, bf16[16,2048]{1,0:T(8,128)(2,1)S(1)}, u32[]{:S(2)}, u32[]{:S(2)}) collective-permute-start(bf16[16,2048]{1,0:T(8,128)(2,1)} %param.10), channel_id=1, source_target_pairs={{0,17},{1,16},{16,1},{17,0},{2,19},{3,18},{18,3},{19,2},{4,21},{5,... | collective-permute-start | bytes 196616 | tf_op jit(solution)/shard_map/ppermute | solution.py:237
  6.3 3.2 %collective-permute-start.5 = (bf16[16,2048]{1,0:T(8,128)(2,1)}, bf16[16,2048]{1,0:T(8,128)(2,1)S(1)}, u32[]{:S(2)}, u32[]{:S(2)}) collective-permute-start(bf16[16,2048]{1,0:T(8,128)(2,1)} %param.10), channel_id=1, source_target_pairs={{0,64},{32,96},{64,0},{96,32},{1,65},{33,97},{65,1},{97,33},{2,66}... | collective-permute-start | bytes 196616 | tf_op jit(solution)/shard_map/ppermute | solution.py:219
  9.5 1.3 copy.36
  11.9 1.7 pad_maximum_fusion.1
  13.9 2.5 %collective-permute-start.6 = (bf16[16,2048]{1,0:T(8,128)(2,1)S(1)}, bf16[16,2048]{1,0:T(8,128)(2,1)S(1)}, u32[]{:S(2)}, u32[]{:S(2)}) collective-permute-start(bf16[16,2048]{1,0:T(8,128)(2,1)S(1)} %collective-permute-done.5), channel_id=1, source_target_pairs={{0,1},{1,0},{16,17},{17,16},{2,3},{3,2},{18,19},{19,18},{4,5},{5,4... | collective-permute-start | bytes 196616 | tf_op jit(solution)/shard_map/ppermute | solution.py:237
  16.4 1.4 collective-permute-start.4
  20.3 2.5 %collective-permute-done.7 = bf16[16,2048]{1,0:T(8,128)(2,1)S(1)} collective-permute-done((bf16[16,2048]{1,0:T(8,128)(2,1)S(1)}, bf16[16,2048]{1,0:T(8,128)(2,1)S(1)}, u32[]{:S(2)}, u32[]{:S(2)}) %collective-permute-start.7) | collective-permute-done | bytes 65568 | tf_op jit(solution)/shard_map/ppermute | solution.py:237
  22.8 2.2 %collective-permute-done.8 = bf16[16,2048]{1,0:T(8,128)(2,1)S(1)} collective-permute-done((bf16[16,2048]{1,0:T(8,128)(2,1)S(1)}, bf16[16,2048]{1,0:T(8,128)(2,1)S(1)}, u32[]{:S(2)}, u32[]{:S(2)}) %collective-permute-start.8) | collective-permute-done | bytes 65568 | tf_op jit(solution)/shard_map/ppermute | solution.py:237
  25.7 2.8 %collective-permute-start.10 = (bf16[8,32,2048]{2,1,0:T(8,128)(2,1)S(1)}, bf16[8,32,2048]{2,1,0:T(8,128)(2,1)S(1)}, u32[]{:S(2)}, u32[]{:S(2)}) collective-permute-start(bf16[8,32,2048]{2,1,0:T(8,128)(2,1)S(1)} %bitcast.127), channel_id=1, source_target_pairs={{0,6},{2,0},{4,2},{6,4},{1,7},{3,1},{5,3},{7,5},{8,14},{10,8},{12,... | collective-permute-start | bytes 3145736 | tf_op jit(solution)/shard_map/ppermute | solution.py:219
  28.6 4.5 %all-to-all-start = ((bf16[16,3,216,128]{3,2,1,0:T(8,128)(2,1)}), bf16[16,3,216,128]{3,2,1,0:T(8,128)(2,1)}, u32[]{:S(2)}, u32[]{:S(2)}) async-start(bf16[16,3,216,128]{3,2,1,0:T(8,128)(2,1)} %pad_maximum_fusion.1), calls=%async_computation | async-start | bytes 5308416 | tf_op jit(solution)/shard_map/all_to_all | solution.py:285
  34.1 14.6 %collective-permute-done.10 = bf16[8,32,2048]{2,1,0:T(8,128)(2,1)S(1)} collective-permute-done((bf16[8,32,2048]{2,1,0:T(8,128)(2,1)S(1)}, bf16[8,32,2048]{2,1,0:T(8,128)(2,1)S(1)}, u32[]{:S(2)}, u32[]{:S(2)}) %collective-permute-start.10) | collective-permute-done | bytes 1048608 | tf_op jit(solution)/shard_map/ppermute | solution.py:219
  48.8 3.0 %collective-permute-start.11 = (bf16[4,32,2048]{2,1,0:T(8,128)(2,1)S(1)}, bf16[4,32,2048]{2,1,0:T(8,128)(2,1)S(1)}, u32[]{:S(2)}, u32[]{:S(2)}) collective-permute-start(bf16[4,32,2048]{2,1,0:T(8,128)(2,1)S(1)} %slice.40), channel_id=1, source_target_pairs={{0,6},{2,0},{4,2},{6,4},{1,7},{3,1},{5,3},{7,5},{8,14},{10,8},{12,... | collective-permute-start | bytes 1572872 | tf_op jit(solution)/shard_map/ppermute | solution.py:219
  51.8 1.1 slice.41
  53.0 1.4 broadcast_select_fusion.7
  54.4 4.7 %collective-permute-done.11 = bf16[4,32,2048]{2,1,0:T(8,128)(2,1)S(1)} collective-permute-done((bf16[4,32,2048]{2,1,0:T(8,128)(2,1)S(1)}, bf16[4,32,2048]{2,1,0:T(8,128)(2,1)S(1)}, u32[]{:S(2)}, u32[]{:S(2)}) %collective-permute-start.11) | collective-permute-done | bytes 524320 | tf_op jit(solution)/shard_map/ppermute | solution.py:219
  59.1 4.4 %collective-permute-done.13 = bf16[4,32,2048]{2,1,0:T(8,128)(2,1)S(1)} collective-permute-done((bf16[4,32,2048]{2,1,0:T(8,128)(2,1)S(1)}, bf16[4,32,2048]{2,1,0:T(8,128)(2,1)S(1)}, u32[]{:S(2)}, u32[]{:S(2)}) %collective-permute-start.13) | collective-permute-done | bytes 524320 | tf_op jit(solution)/shard_map/ppermute | solution.py:219
  63.4 1.6 pad_maximum_fusion
  65.0 2.1 fusion.15
  67.1 1.2 copy.43
  68.3 4.6 %all-to-all-start.1 = ((bf16[8,432,128]{2,1,0:T(8,128)(2,1)}), bf16[8,432,128]{2,1,0:T(8,128)(2,1)S(1)}, u32[]{:S(2)}, u32[]{:S(2)}) async-start(bf16[8,432,128]{2,1,0:T(8,128)(2,1)} %bitcast.120), calls=%async_computation.1 | async-start | bytes 1769472 | tf_op jit(solution)/shard_map/all_to_all | solution.py:299
  72.8 26.0 %attend.1 = (bf16[16,216,128]{2,1,0:T(8,128)(2,1)}, bf16[3456,128]{1,0:T(8,128)(2,1)}, bf16[3456,128]{1,0:T(8,128)(2,1)}, bf16[3456,128]{1,0:T(8,128)(2,1)}, f32...) custom-call(s32[3456]{0:T(1024)} %order_ref.3, s32[162]{0:T(256)} %reshape.283.neigh_ref, ...), custom_call_target="tpu_custom_call" | custom-call | flops 30000001024 | bytes 20000000 | tf_op jit(solution)/shard_map/attend/pallas_call | solution.py:102
  99.6 4.0 %collective-permute-start.15 = (bf16[216,2048]{1,0:T(8,128)(2,1)S(1)}, bf16[216,2048]{1,0:T(8,128)(2,1)}, u32[]{:S(2)}, u32[]{:S(2)}) collective-permute-start(bf16[216,2048]{1,0:T(8,128)(2,1)S(1)} %bitcast.142), channel_id=1, source_target_pairs={{0,4},{2,6},{4,0},{6,2},{1,5},{3,7},{5,1},{7,3},{8,12},{10,14},{12... | collective-permute-start | bytes 2654216 | tf_op jit(solution)/shard_map/ppermute | solution.py:219
  103.8 5.7 %all-to-all-start.2 = ((bf16[8,432,128]{2,1,0:T(8,128)(2,1)}), bf16[8,432,128]{2,1,0:T(8,128)(2,1)S(1)}, u32[]{:S(2)}, u32[]{:S(2)}) async-start(bf16[8,432,128]{2,1,0:T(8,128)(2,1)} %bitcast.139), calls=%async_computation.2 | async-start | bytes 1769472 | tf_op jit(solution)/shard_map/all_to_all | solution.py:304
  109.5 29.9 %attend_grad.1 = bf16[16,3,216,128]{3,2,1,0:T(8,128)(2,1)} custom-call(s32[3456]{0:T(1024)} %order_ref.3, s32[162]{0:T(256)} %reshape.283.neigh_ref, s32[1]{0:T(128)} %bitcast.turn_ref, bf16[16,216,128]{2,1,0:T(8,128)(2,1)} %bitcast.138, bf16[3456,128]{1,0:T(8,128)(2,1)} %get-tuple-element.37.qp_ref, bf16[3456,128]{1,0:T(8,128)(2,1)} %get-tuple-element.38.kp_ref, ...), custom_call_target="tpu_custom_call" | custom-call | flops 30000001024 | bytes 20000000 | tf_op jit(solution)/shard_map/attend_grad/pallas_call | solution.py:167
  140.4 1.8 collective-permute-done.15
  142.7 5.6 %all-to-all-start.3 = ((bf16[16,3,216,128]{3,2,1,0:T(8,128)(2,1)}), bf16[16,3,216,128]{3,2,1,0:T(8,128)(2,1)S(1)}, u32[]{:S(2)}, u32[]{:S(2)}) async-start(bf16[16,3,216,128]{3,2,1,0:T(8,128)(2,1)} %attend_grad.1), calls=%async_computation.3 | async-start | bytes 5308416 | tf_op jit(solution)/shard_map/all_to_all | solution.py:308
  148.4 2.3 %copy.29 = bf16[432,1024]{0,1:T(8,128)(2,1)} copy(bf16[432,1024]{1,0:T(8,128)(2,1)} %copy_bitcast_fusion) | data formatting | bytes 1769472 | tf_op jit(solution)/shard_map/optimization_barrier | solution.py:311
  150.6 4.4 %fusion.31 = f32[432,2048]{1,0:T(8,128)S(1)} fusion(bf16[432,1024]{1,0:T(8,128)(2,1)} %copy_bitcast_fusion, bf16[1024,2048]{1,0:T(8,128)(2,1)} %bitcast.125), kind=kOutput, calls=%fused_computation.87 | convolution fusion | flops 1811939328 | bytes 8617984 | tf_op jit(solution)/shard_map/dot_general | solution.py:320
  155.1 1.6 broadcast_select_fusion.5
  157.8 2.8 %collective-permute-start.20 = (bf16[432,256]{0,1:T(8,128)(2,1)S(1)}, bf16[432,256]{0,1:T(8,128)(2,1)S(1)}, u32[]{:S(2)}, u32[]{:S(2)}) collective-permute-start(bf16[432,256]{0,1:T(8,128)(2,1)S(1)} %bitcast.145), channel_id=1, source_target_pairs={{0,4},{2,6},{4,0},{6,2},{1,5},{3,7},{5,1},{7,3},{8,12},{10,14},{12... | collective-permute-start | bytes 663560 | tf_op jit(solution)/shard_map/ppermute | solution.py:219
  161.5 1.6 broadcast_select_fusion.3
  163.1 1.6 broadcast_select_fusion.1
  164.7 2.3 %collective-permute-done.19 = bf16[432,256]{0,1:T(8,128)(2,1)S(1)} collective-permute-done((bf16[432,256]{0,1:T(8,128)(2,1)S(1)}, bf16[432,256]{0,1:T(8,128)(2,1)S(1)}, u32[]{:S(2)}, u32[]{:S(2)}) %collective-permute-start.19) | collective-permute-done | bytes 221216 | tf_op jit(solution)/shard_map/ppermute | solution.py:219
  167.7 5.2 %collective-permute-done.20 = bf16[432,256]{0,1:T(8,128)(2,1)S(1)} collective-permute-done((bf16[432,256]{0,1:T(8,128)(2,1)S(1)}, bf16[432,256]{0,1:T(8,128)(2,1)S(1)}, u32[]{:S(2)}, u32[]{:S(2)}) %collective-permute-start.20) | collective-permute-done | bytes 221216 | tf_op jit(solution)/shard_map/ppermute | solution.py:219
  175.7 1.7 collective-permute-start.24
  177.4 2.7 %collective-permute-start.25 = (bf16[4,16,2048]{2,1,0:T(8,128)(2,1)S(1)}, bf16[4,16,2048]{2,1,0:T(8,128)(2,1)S(1)}, u32[]{:S(2)}, u32[]{:S(2)}) collective-permute-start(bf16[4,16,2048]{2,1,0:T(8,128)(2,1)S(1)} %get-tuple-element.67), channel_id=1, source_target_pairs={{0,64},{32,96},{64,0},{96,32},{1,65},{33,97},{65,1},{97,33},{2,66}... | collective-permute-start | bytes 786440 | tf_op jit(solution)/shard_map/ppermute | solution.py:219
  180.0 1.5 collective-permute-start.26
  181.5 1.1 fusion.16
  182.6 9.1 %collective-permute-done.24 = bf16[4,16,2048]{2,1,0:T(8,128)(2,1)S(1)} collective-permute-done((bf16[4,16,2048]{2,1,0:T(8,128)(2,1)S(1)}, bf16[4,16,2048]{2,1,0:T(8,128)(2,1)S(1)}, u32[]{:S(2)}, u32[]{:S(2)}) %collective-permute-start.24) | collective-permute-done | bytes 262176 | tf_op jit(solution)/shard_map/ppermute | solution.py:219
  191.7 5.2 %collective-permute-done.25 = bf16[4,16,2048]{2,1,0:T(8,128)(2,1)S(1)} collective-permute-done((bf16[4,16,2048]{2,1,0:T(8,128)(2,1)S(1)}, bf16[4,16,2048]{2,1,0:T(8,128)(2,1)S(1)}, u32[]{:S(2)}, u32[]{:S(2)}) %collective-permute-start.25) | collective-permute-done | bytes 262176 | tf_op jit(solution)/shard_map/ppermute | solution.py:219
  197.0 1.1 fusion.19
  199.9 3.0 %collective-permute-start.29 = (bf16[16,2048]{1,0:T(8,128)(2,1)}, bf16[16,2048]{1,0:T(8,128)(2,1)}, u32[]{:S(2)}, u32[]{:S(2)}) collective-permute-start(bf16[16,2048]{1,0:T(8,128)(2,1)} %get-tuple-element.74), channel_id=1, source_target_pairs={{0,17},{1,16},{16,1},{17,0},{2,19},{3,18},{18,3},{19,2},{4,21},{5,... | collective-permute-start | bytes 196616 | tf_op jit(solution)/shard_map/ppermute | solution.py:269
  202.9 1.4 slice_bitcast_fusion
  204.4 1.3 reshape.292
  205.8 1.3 reshape.293
  207.2 1.3 reshape.294
  208.5 1.6 fusion.24
  (108 shorter events, 16.6 us)
Async XLA Ops:
  0.6 10.2 %copy-start.8 = (bf16[1,216,2048]{2,1,0:T(8,128)(2,1)S(1)}, bf16[1,216,2048]{2,1,0:T(8,128)(2,1)}, u32[]{:S(2)}) copy-start(bf16[1,216,2048]{2,1,0:T(8,128)(2,1)} %param.9) | copy-start | bytes 2654212
  0.6 10.4 %copy-start.9 = (bf16[1,216,2048]{2,1,0:T(8,128)(2,1)S(1)}, bf16[1,216,2048]{2,1,0:T(8,128)(2,1)}, u32[]{:S(2)}) copy-start(bf16[1,216,2048]{2,1,0:T(8,128)(2,1)} %param.7) | copy-start | bytes 2654212
  0.7 13.1 %collective-permute-start.2 = (bf16[16,2048]{1,0:T(8,128)(2,1)}, bf16[16,2048]{1,0:T(8,128)(2,1)S(1)}, u32[]{:S(2)}, u32[]{:S(2)}) collective-permute-start(bf16[16,2048]{1,0:T(8,128)(2,1)} %param.10), channel_id=1, source_target_pairs={{0,16},{1,17},{16,0},{17,1},{2,18},{3,19},{18,2},{19,3},{4,20},{5,... | collective-permute-start | bytes 196616 | tf_op jit(solution)/shard_map/ppermute | solution.py:237
  2.7 11.0 %collective-permute-start.3 = (bf16[16,2048]{1,0:T(8,128)(2,1)}, bf16[16,2048]{1,0:T(8,128)(2,1)S(1)}, u32[]{:S(2)}, u32[]{:S(2)}) collective-permute-start(bf16[16,2048]{1,0:T(8,128)(2,1)} %param.10), channel_id=1, source_target_pairs={{0,17},{1,16},{16,1},{17,0},{2,19},{3,18},{18,3},{19,2},{4,21},{5,... | collective-permute-start | bytes 196616 | tf_op jit(solution)/shard_map/ppermute | solution.py:237
  5.3 8.4 %collective-permute-start.1 = (bf16[16,2048]{1,0:T(8,128)(2,1)}, bf16[16,2048]{1,0:T(8,128)(2,1)S(1)}, u32[]{:S(2)}, u32[]{:S(2)}) collective-permute-start(bf16[16,2048]{1,0:T(8,128)(2,1)} %param.10), channel_id=1, source_target_pairs={{0,1},{1,0},{16,17},{17,16},{2,3},{3,2},{18,19},{19,18},{4,5},{5,4... | collective-permute-start | bytes 196616 | tf_op jit(solution)/shard_map/ppermute | solution.py:237
  6.3 7.5 %collective-permute-start.5 = (bf16[16,2048]{1,0:T(8,128)(2,1)}, bf16[16,2048]{1,0:T(8,128)(2,1)S(1)}, u32[]{:S(2)}, u32[]{:S(2)}) collective-permute-start(bf16[16,2048]{1,0:T(8,128)(2,1)} %param.10), channel_id=1, source_target_pairs={{0,64},{32,96},{64,0},{96,32},{1,65},{33,97},{65,1},{97,33},{2,66}... | collective-permute-start | bytes 196616 | tf_op jit(solution)/shard_map/ppermute | solution.py:219
  11.9 1.8 copy-start.14
  13.9 6.4 %collective-permute-start.6 = (bf16[16,2048]{1,0:T(8,128)(2,1)S(1)}, bf16[16,2048]{1,0:T(8,128)(2,1)S(1)}, u32[]{:S(2)}, u32[]{:S(2)}) collective-permute-start(bf16[16,2048]{1,0:T(8,128)(2,1)S(1)} %collective-permute-done.5), channel_id=1, source_target_pairs={{0,1},{1,0},{16,17},{17,16},{2,3},{3,2},{18,19},{19,18},{4,5},{5,4... | collective-permute-start | bytes 196616 | tf_op jit(solution)/shard_map/ppermute | solution.py:237
  16.4 8.7 %collective-permute-start.4 = (bf16[2,32,2048]{2,1,0:T(8,128)(2,1)S(1)}, bf16[2,32,2048]{2,1,0:T(8,128)(2,1)S(1)}, u32[]{:S(2)}, u32[]{:S(2)}) collective-permute-start(bf16[2,32,2048]{2,1,0:T(8,128)(2,1)S(1)} %pad_maximum_fusion.5), channel_id=1, source_target_pairs={{0,96},{32,0},{64,32},{96,64},{1,97},{33,1},{65,33},{97,65},{2,98}... | collective-permute-start | bytes 786440 | tf_op jit(solution)/shard_map/ppermute | solution.py:219
  17.9 7.6 %collective-permute-start.9 = (bf16[2,32,2048]{2,1,0:T(8,128)(2,1)S(1)}, bf16[2,32,2048]{2,1,0:T(8,128)(2,1)S(1)}, u32[]{:S(2)}, u32[]{:S(2)}) collective-permute-start(bf16[2,32,2048]{2,1,0:T(8,128)(2,1)S(1)} %pad_maximum_fusion.5), channel_id=1, source_target_pairs={{0,32},{32,64},{64,96},{96,0},{1,33},{33,65},{65,97},{97,1},{2,34}... | collective-permute-start | bytes 786440 | tf_op jit(solution)/shard_map/ppermute | solution.py:219
  18.5 4.3 %collective-permute-start.7 = (bf16[16,2048]{1,0:T(8,128)(2,1)S(1)}, bf16[16,2048]{1,0:T(8,128)(2,1)S(1)}, u32[]{:S(2)}, u32[]{:S(2)}) collective-permute-start(bf16[16,2048]{1,0:T(8,128)(2,1)S(1)} %collective-permute-done.5), channel_id=1, source_target_pairs={{0,16},{1,17},{16,0},{17,1},{2,18},{3,19},{18,2},{19,3},{4,20},{5,... | collective-permute-start | bytes 196616 | tf_op jit(solution)/shard_map/ppermute | solution.py:237
  19.5 5.5 %collective-permute-start.8 = (bf16[16,2048]{1,0:T(8,128)(2,1)S(1)}, bf16[16,2048]{1,0:T(8,128)(2,1)S(1)}, u32[]{:S(2)}, u32[]{:S(2)}) collective-permute-start(bf16[16,2048]{1,0:T(8,128)(2,1)S(1)} %collective-permute-done.5), channel_id=1, source_target_pairs={{0,17},{1,16},{16,1},{17,0},{2,19},{3,18},{18,3},{19,2},{4,21},{5,... | collective-permute-start | bytes 196616 | tf_op jit(solution)/shard_map/ppermute | solution.py:237
  25.7 7.3 %copy-start.11 = (bf16[1,216,2048]{2,1,0:T(8,128)(2,1)S(1)}, bf16[1,216,2048]{2,1,0:T(8,128)(2,1)}, u32[]{:S(2)}) copy-start(bf16[1,216,2048]{2,1,0:T(8,128)(2,1)} %param.11) | copy-start | bytes 2654212
  25.7 7.6 %copy-start.15 = (s32[18,9]{0,1:T(8,128)S(1)}, s32[18,9]{0,1:T(8,128)}, u32[]{:S(2)}) copy-start(s32[18,9]{0,1:T(8,128)} %param.12) | copy-start | bytes 1948
  25.7 23.0 %collective-permute-start.10 = (bf16[8,32,2048]{2,1,0:T(8,128)(2,1)S(1)}, bf16[8,32,2048]{2,1,0:T(8,128)(2,1)S(1)}, u32[]{:S(2)}, u32[]{:S(2)}) collective-permute-start(bf16[8,32,2048]{2,1,0:T(8,128)(2,1)S(1)} %bitcast.127), channel_id=1, source_target_pairs={{0,6},{2,0},{4,2},{6,4},{1,7},{3,1},{5,3},{7,5},{8,14},{10,8},{12,... | collective-permute-start | bytes 3145736 | tf_op jit(solution)/shard_map/ppermute | solution.py:219
  28.6 23.2 %collective-permute-start.12 = (bf16[8,32,2048]{2,1,0:T(8,128)(2,1)S(1)}, bf16[8,32,2048]{2,1,0:T(8,128)(2,1)}, u32[]{:S(2)}, u32[]{:S(2)}) collective-permute-start(bf16[8,32,2048]{2,1,0:T(8,128)(2,1)S(1)} %bitcast.128), channel_id=1, source_target_pairs={{0,2},{2,4},{4,6},{6,0},{1,3},{3,5},{5,7},{7,1},{8,10},{10,12},{12... | collective-permute-start | bytes 3145736 | tf_op jit(solution)/shard_map/ppermute | solution.py:219
  28.6 39.7 %all-to-all-start = ((bf16[16,3,216,128]{3,2,1,0:T(8,128)(2,1)}), bf16[16,3,216,128]{3,2,1,0:T(8,128)(2,1)}, u32[]{:S(2)}, u32[]{:S(2)}) async-start(bf16[16,3,216,128]{3,2,1,0:T(8,128)(2,1)} %pad_maximum_fusion.1), calls=%async_computation | async-start | bytes 5308416 | tf_op jit(solution)/shard_map/all_to_all | solution.py:285
  33.0 19.9 %collective-permute-start = (bf16[216,2048]{1,0:T(8,128)(2,1)S(1)}, bf16[216,2048]{1,0:T(8,128)(2,1)}, u32[]{:S(2)}, u32[]{:S(2)}) collective-permute-start(bf16[216,2048]{1,0:T(8,128)(2,1)S(1)} %bitcast.140), channel_id=1, source_target_pairs={{0,8},{8,0},{1,9},{9,1},{2,10},{10,2},{3,11},{11,3},{4,12},{12,4},... | collective-permute-start | bytes 2654216 | tf_op jit(solution)/shard_map/ppermute | solution.py:219
  34.1 18.9 %copy-start.12 = (bf16[1,216,2048]{2,1,0:T(8,128)(2,1)S(1)}, bf16[1,216,2048]{2,1,0:T(8,128)(2,1)}, u32[]{:S(2)}) copy-start(bf16[1,216,2048]{2,1,0:T(8,128)(2,1)} %param.11) | copy-start | bytes 2654212
  48.8 10.3 %collective-permute-start.11 = (bf16[4,32,2048]{2,1,0:T(8,128)(2,1)S(1)}, bf16[4,32,2048]{2,1,0:T(8,128)(2,1)S(1)}, u32[]{:S(2)}, u32[]{:S(2)}) collective-permute-start(bf16[4,32,2048]{2,1,0:T(8,128)(2,1)S(1)} %slice.40), channel_id=1, source_target_pairs={{0,6},{2,0},{4,2},{6,4},{1,7},{3,1},{5,3},{7,5},{8,14},{10,8},{12,... | collective-permute-start | bytes 1572872 | tf_op jit(solution)/shard_map/ppermute | solution.py:219
  52.9 10.6 %collective-permute-start.13 = (bf16[4,32,2048]{2,1,0:T(8,128)(2,1)S(1)}, bf16[4,32,2048]{2,1,0:T(8,128)(2,1)S(1)}, u32[]{:S(2)}, u32[]{:S(2)}) collective-permute-start(bf16[4,32,2048]{2,1,0:T(8,128)(2,1)S(1)} %slice.41), channel_id=1, source_target_pairs={{0,2},{2,4},{4,6},{6,0},{1,3},{3,5},{5,7},{7,1},{8,10},{10,12},{12... | collective-permute-start | bytes 1572872 | tf_op jit(solution)/shard_map/ppermute | solution.py:219
  54.4 10.7 %copy-start.3 = (bf16[216,2048]{1,0:T(8,128)(2,1)}, bf16[216,2048]{1,0:T(8,128)(2,1)S(1)}, u32[]{:S(2)}) copy-start(bf16[216,2048]{1,0:T(8,128)(2,1)S(1)} %get-tuple-element.65) | copy-start | bytes 2654212
  65.0 2.1 copy-start.1
  68.3 30.5 %all-to-all-start.1 = ((bf16[8,432,128]{2,1,0:T(8,128)(2,1)}), bf16[8,432,128]{2,1,0:T(8,128)(2,1)S(1)}, u32[]{:S(2)}, u32[]{:S(2)}) async-start(bf16[8,432,128]{2,1,0:T(8,128)(2,1)} %bitcast.120), calls=%async_computation.1 | async-start | bytes 1769472 | tf_op jit(solution)/shard_map/all_to_all | solution.py:299
  72.8 26.0 %copy-start.13 = (bf16[1,216,2048]{2,1,0:T(8,128)(2,1)S(1)}, bf16[1,216,2048]{2,1,0:T(8,128)(2,1)}, u32[]{:S(2)}) copy-start(bf16[1,216,2048]{2,1,0:T(8,128)(2,1)} %param.11) | copy-start | bytes 2654212
  98.8 10.7 %copy-start.10 = (bf16[8,432,128]{2,1,0:T(8,128)(2,1)}, bf16[8,432,128]{2,1,0:T(8,128)(2,1)S(1)}, u32[]{:S(2)}) copy-start(bf16[8,432,128]{2,1,0:T(8,128)(2,1)S(1)} %all-to-all-done.1) | copy-start | bytes 2654212
  98.8 41.6 %collective-permute-start.14 = (bf16[216,2048]{1,0:T(8,128)(2,1)S(1)}, bf16[216,2048]{1,0:T(8,128)(2,1)}, u32[]{:S(2)}, u32[]{:S(2)}) collective-permute-start(bf16[216,2048]{1,0:T(8,128)(2,1)S(1)} %bitcast.141), channel_id=1, source_target_pairs={{0,2},{2,4},{4,6},{6,0},{1,3},{3,5},{5,7},{7,1},{8,10},{10,12},{12... | collective-permute-start | bytes 2654216 | tf_op jit(solution)/shard_map/ppermute | solution.py:219
  99.6 42.6 %collective-permute-start.15 = (bf16[216,2048]{1,0:T(8,128)(2,1)S(1)}, bf16[216,2048]{1,0:T(8,128)(2,1)}, u32[]{:S(2)}, u32[]{:S(2)}) collective-permute-start(bf16[216,2048]{1,0:T(8,128)(2,1)S(1)} %bitcast.142), channel_id=1, source_target_pairs={{0,4},{2,6},{4,0},{6,2},{1,5},{3,7},{5,1},{7,3},{8,12},{10,14},{12... | collective-permute-start | bytes 2654216 | tf_op jit(solution)/shard_map/ppermute | solution.py:219
  103.6 38.6 %collective-permute-start.16 = (bf16[216,2048]{1,0:T(8,128)(2,1)S(1)}, bf16[216,2048]{1,0:T(8,128)(2,1)}, u32[]{:S(2)}, u32[]{:S(2)}) collective-permute-start(bf16[216,2048]{1,0:T(8,128)(2,1)S(1)} %bitcast.143), channel_id=1, source_target_pairs={{0,6},{2,0},{4,2},{6,4},{1,7},{3,1},{5,3},{7,5},{8,14},{10,8},{12,... | collective-permute-start | bytes 2654216 | tf_op jit(solution)/shard_map/ppermute | solution.py:219
  103.8 35.6 %all-to-all-start.2 = ((bf16[8,432,128]{2,1,0:T(8,128)(2,1)}), bf16[8,432,128]{2,1,0:T(8,128)(2,1)S(1)}, u32[]{:S(2)}, u32[]{:S(2)}) async-start(bf16[8,432,128]{2,1,0:T(8,128)(2,1)} %bitcast.139), calls=%async_computation.2 | async-start | bytes 1769472 | tf_op jit(solution)/shard_map/all_to_all | solution.py:304
  142.2 6.2 %collective-permute-start.17 = (bf16[216,2048]{1,0:T(8,128)(2,1)}, bf16[216,2048]{1,0:T(8,128)(2,1)}, u32[]{:S(2)}, u32[]{:S(2)}) collective-permute-start(bf16[216,2048]{1,0:T(8,128)(2,1)} %collective-permute-done.14), channel_id=1, source_target_pairs={{0,8},{8,0},{1,9},{9,1},{2,10},{10,2},{3,11},{11,3},{4,12},{12,4},... | collective-permute-start | bytes 2654216 | tf_op jit(solution)/shard_map/ppermute | solution.py:219
  142.2 19.0 %collective-permute-start.21 = (bf16[216,2048]{1,0:T(8,128)(2,1)}, bf16[216,2048]{1,0:T(8,128)(2,1)}, u32[]{:S(2)}, u32[]{:S(2)}) collective-permute-start(bf16[216,2048]{1,0:T(8,128)(2,1)} %collective-permute-done.15), channel_id=1, source_target_pairs={{0,8},{8,0},{1,9},{9,1},{2,10},{10,2},{3,11},{11,3},{4,12},{12,4},... | collective-permute-start | bytes 2654216 | tf_op jit(solution)/shard_map/ppermute | solution.py:219
  142.7 20.4 %collective-permute-start.23 = (bf16[216,2048]{1,0:T(8,128)(2,1)}, bf16[216,2048]{1,0:T(8,128)(2,1)}, u32[]{:S(2)}, u32[]{:S(2)}) collective-permute-start(bf16[216,2048]{1,0:T(8,128)(2,1)} %collective-permute-done.16), channel_id=1, source_target_pairs={{0,8},{8,0},{1,9},{9,1},{2,10},{10,2},{3,11},{11,3},{4,12},{12,4},... | collective-permute-start | bytes 2654216 | tf_op jit(solution)/shard_map/ppermute | solution.py:219
  142.7 54.2 %all-to-all-start.3 = ((bf16[16,3,216,128]{3,2,1,0:T(8,128)(2,1)}), bf16[16,3,216,128]{3,2,1,0:T(8,128)(2,1)S(1)}, u32[]{:S(2)}, u32[]{:S(2)}) async-start(bf16[16,3,216,128]{3,2,1,0:T(8,128)(2,1)} %attend_grad.1), calls=%async_computation.3 | async-start | bytes 5308416 | tf_op jit(solution)/shard_map/all_to_all | solution.py:308
  155.1 1.8 copy-start.2
  156.9 10.0 %collective-permute-start.19 = (bf16[432,256]{0,1:T(8,128)(2,1)S(1)}, bf16[432,256]{0,1:T(8,128)(2,1)S(1)}, u32[]{:S(2)}, u32[]{:S(2)}) collective-permute-start(bf16[432,256]{0,1:T(8,128)(2,1)S(1)} %bitcast.146), channel_id=1, source_target_pairs={{0,2},{2,4},{4,6},{6,0},{1,3},{3,5},{5,7},{7,1},{8,10},{10,12},{12... | collective-permute-start | bytes 663560 | tf_op jit(solution)/shard_map/ppermute | solution.py:219
  157.8 15.1 %collective-permute-start.20 = (bf16[432,256]{0,1:T(8,128)(2,1)S(1)}, bf16[432,256]{0,1:T(8,128)(2,1)S(1)}, u32[]{:S(2)}, u32[]{:S(2)}) collective-permute-start(bf16[432,256]{0,1:T(8,128)(2,1)S(1)} %bitcast.145), channel_id=1, source_target_pairs={{0,4},{2,6},{4,0},{6,2},{1,5},{3,7},{5,1},{7,3},{8,12},{10,14},{12... | collective-permute-start | bytes 663560 | tf_op jit(solution)/shard_map/ppermute | solution.py:219
  160.6 12.9 %collective-permute-start.22 = (bf16[432,256]{0,1:T(8,128)(2,1)S(1)}, bf16[432,256]{0,1:T(8,128)(2,1)S(1)}, u32[]{:S(2)}, u32[]{:S(2)}) collective-permute-start(bf16[432,256]{0,1:T(8,128)(2,1)S(1)} %bitcast.144), channel_id=1, source_target_pairs={{0,6},{2,0},{4,2},{6,4},{1,7},{3,1},{5,3},{7,5},{8,14},{10,8},{12,... | collective-permute-start | bytes 663560 | tf_op jit(solution)/shard_map/ppermute | solution.py:219
  161.2 20.3 %collective-permute-start.18 = (bf16[216,2048]{1,0:T(8,128)(2,1)S(1)}, bf16[216,2048]{1,0:T(8,128)(2,1)S(1)}, u32[]{:S(2)}, u32[]{:S(2)}) collective-permute-start(bf16[216,2048]{1,0:T(8,128)(2,1)S(1)} %dynamic-slice_convert_fusion), channel_id=1, source_target_pairs={{0,8},{8,0},{1,9},{9,1},{2,10},{10,2},{3,11},{11,3},{4,12},{12,4},... | collective-permute-start | bytes 2654216 | tf_op jit(solution)/shard_map/ppermute | solution.py:219
  175.6 7.1 %copy-start = (bf16[256,2048]{1,0:T(8,128)(2,1)}, bf16[256,2048]{1,0:T(8,128)(2,1)S(1)}, u32[]{:S(2)}) copy-start(bf16[256,2048]{1,0:T(8,128)(2,1)S(1)} %fusion.2) | copy-start | bytes 3145732
  175.7 16.1 %collective-permute-start.24 = (bf16[4,16,2048]{2,1,0:T(8,128)(2,1)S(1)}, bf16[4,16,2048]{2,1,0:T(8,128)(2,1)S(1)}, u32[]{:S(2)}, u32[]{:S(2)}) collective-permute-start(bf16[4,16,2048]{2,1,0:T(8,128)(2,1)S(1)} %get-tuple-element.68), channel_id=1, source_target_pairs={{0,32},{32,64},{64,96},{96,0},{1,33},{33,65},{65,97},{97,1},{2,34}... | collective-permute-start | bytes 786440 | tf_op jit(solution)/shard_map/ppermute | solution.py:219
  177.4 19.6 %collective-permute-start.25 = (bf16[4,16,2048]{2,1,0:T(8,128)(2,1)S(1)}, bf16[4,16,2048]{2,1,0:T(8,128)(2,1)S(1)}, u32[]{:S(2)}, u32[]{:S(2)}) collective-permute-start(bf16[4,16,2048]{2,1,0:T(8,128)(2,1)S(1)} %get-tuple-element.67), channel_id=1, source_target_pairs={{0,64},{32,96},{64,0},{96,32},{1,65},{33,97},{65,1},{97,33},{2,66}... | collective-permute-start | bytes 786440 | tf_op jit(solution)/shard_map/ppermute | solution.py:219
  180.0 16.9 %collective-permute-start.26 = (bf16[4,16,2048]{2,1,0:T(8,128)(2,1)S(1)}, bf16[4,16,2048]{2,1,0:T(8,128)(2,1)S(1)}, u32[]{:S(2)}, u32[]{:S(2)}) collective-permute-start(bf16[4,16,2048]{2,1,0:T(8,128)(2,1)S(1)} %get-tuple-element.66), channel_id=1, source_target_pairs={{0,96},{32,0},{64,32},{96,64},{1,97},{33,1},{65,33},{97,65},{2,98}... | collective-permute-start | bytes 786440 | tf_op jit(solution)/shard_map/ppermute | solution.py:219
  198.0 1.8 copy-start.7
  198.8 9.7 %collective-permute-start.27 = (bf16[16,2048]{1,0:T(8,128)(2,1)}, bf16[16,2048]{1,0:T(8,128)(2,1)}, u32[]{:S(2)}, u32[]{:S(2)}) collective-permute-start(bf16[16,2048]{1,0:T(8,128)(2,1)} %get-tuple-element.73), channel_id=1, source_target_pairs={{0,1},{1,0},{16,17},{17,16},{2,3},{3,2},{18,19},{19,18},{4,5},{5,4... | collective-permute-start | bytes 196616 | tf_op jit(solution)/shard_map/ppermute | solution.py:269
  199.9 8.7 %collective-permute-start.28 = (bf16[16,2048]{1,0:T(8,128)(2,1)}, bf16[16,2048]{1,0:T(8,128)(2,1)}, u32[]{:S(2)}, u32[]{:S(2)}) collective-permute-start(bf16[16,2048]{1,0:T(8,128)(2,1)} %get-tuple-element.75), channel_id=1, source_target_pairs={{0,16},{1,17},{16,0},{17,1},{2,18},{3,19},{18,2},{19,3},{4,20},{5,... | collective-permute-start | bytes 196616 | tf_op jit(solution)/shard_map/ppermute | solution.py:269
  199.9 8.7 %collective-permute-start.29 = (bf16[16,2048]{1,0:T(8,128)(2,1)}, bf16[16,2048]{1,0:T(8,128)(2,1)}, u32[]{:S(2)}, u32[]{:S(2)}) collective-permute-start(bf16[16,2048]{1,0:T(8,128)(2,1)} %get-tuple-element.74), channel_id=1, source_target_pairs={{0,17},{1,16},{16,1},{17,0},{2,19},{3,18},{18,3},{19,2},{4,21},{5,... | collective-permute-start | bytes 196616 | tf_op jit(solution)/shard_map/ppermute | solution.py:269
  205.7 1.4 copy-start.5
  (2 other events, 2.6 us)

commit v5 on v4

--- a/solution.py
+++ b/solution.py
@@ -12,6 +12,8 @@
 bf=jnp.bfloat16; f32=jnp.float32
 SC=1.0/math.sqrt(HD); LOG2E=math.log2(math.e)
 PITCH=4
+PITCH1=3
+SPARE=16
 KP=1792; BW=256; BLOCKS=KP//BW
 U1=2; U2=2
 COST=pl.CostEstimate(flops=30*10**9,bytes_accessed=20*10**6,transcendentals=0)
@@ -42,11 +44,11 @@
     def _():
         for j in range(3):
             for s in range(16):
-                tok[pl.ds(s*216*PITCH+j,216,stride=PITCH),:]=qkv_ref[s,j].astype(f32)
-        permute_rows(order_ref,tok,per,PITCH,False)
+                tok[pl.ds(s*216*PITCH1+j,216,stride=PITCH1),:]=qkv_ref[s,j].astype(f32)
+        permute_rows(order_ref,tok,per,PITCH1,False)
         for j,r in enumerate((qp_ref,kp_ref,vp_ref)):
             for u in range(NT):
-                r[pl.ds(u*T,T),:]=per[pl.ds(u*T*PITCH+j,T,stride=PITCH),:].astype(bf)
+                r[pl.ds(u*T,T),:]=per[pl.ds(u*T*PITCH1+j,T,stride=PITCH1),:].astype(bf)
         vc[pl.ds(KC,KP-KC),:]=jnp.zeros((KP-KC,HD),bf)
         q=scores_ready(0,qp_ref,kp_ref,kc,neigh_ref)
         s=lax.dot_general(q,kc[...],(((1,),(1,)),((),())),preferred_element_type=f32)
@@ -104,7 +106,7 @@
         in_specs=[full((16,3,216,HD))],
         out_specs=[full((16,216,HD)),full((N,HD)),full((N,HD)),full((N,HD)),pl.BlockSpec((U1*T,HD),lambda t,*_:(t,0)),
                    pl.BlockSpec((U1*T,HD),lambda t,*_:(t,0)),pl.BlockSpec((U1,T,KP),lambda t,*_:(t,0,0))],
-        scratch_shapes=[pltpu.VMEM((N*PITCH,HD),f32),pltpu.VMEM((N*PITCH,HD),f32),pltpu.VMEM((KP,HD),bf),pltpu.VMEM((KP,HD),bf),pltpu.VMEM((U1*T,HD),f32),pltpu.VMEM((2,T,KP),f32),pltpu.VMEM((2,T,HD),f32)]),
+        scratch_shapes=[pltpu.VMEM((N*PITCH1+SPARE,HD),f32),pltpu.VMEM((N*PITCH1+SPARE,HD),f32),pltpu.VMEM((KP,HD),bf),pltpu.VMEM((KP,HD),bf),pltpu.VMEM((U1*T+SPARE,HD),f32),pltpu.VMEM((2,T,KP),f32),pltpu.VMEM((2,T,HD),f32)]),
       out_shape=[jax.ShapeDtypeStruct((16,216,HD),bf)]+[jax.ShapeDtypeStruct((N,HD),bf)]*3+[jax.ShapeDtypeStruct((N,HD),f32),jax.ShapeDtypeStruct((N,HD),f32),jax.ShapeDtypeStruct((NT,T,KP),bf)],
       compiler_params=pltpu.CompilerParams(vmem_limit_bytes=60*1024*1024),
       cost_estimate=COST,name="attend")(order,neigh,turn,qkv)
@@ -122,9 +124,10 @@
                 gp[pl.ds(p,1),:]=tok[pl.ds(order_ref[p],1),:]
             return _
         lax.fori_loop(0,R//32,first,0)
-        for u in range(NT*PITCH):
-            acc[pl.ds(u*T,T),:]=jnp.zeros((T,HD),f32)
-    g=gp[...]
+        for u in range(NT):
+            for j in (1,2):
+                acc[pl.ds(u*T*PITCH+j,T,stride=PITCH),:]=jnp.zeros((T,HD),f32)
+    g=gp[pl.ds(0,R),:]
     ahead=jnp.minimum((i+1)*R,N-R)
     for p in range(R):
         gp[pl.ds(p,1),:]=tok[pl.ds(order_ref[ahead+p],1),:]
@@ -169,7 +172,7 @@
         in_specs=[full((16,216,HD)),row,full((N,HD)),full((N,HD)),row,
                    row,pl.BlockSpec((U2,T,KP),lambda t,*_:(t,0,0))],
         out_specs=full((16,3,216,HD)),
-        scratch_shapes=[pltpu.VMEM((N*PITCH,HD),f32),pltpu.VMEM((U2*T,HD),f32),pltpu.VMEM((N*PITCH,HD),f32),pltpu.VMEM((U2,KC,HD),bf),pltpu.VMEM((U2,KC,HD),bf)]),
+        scratch_shapes=[pltpu.VMEM((N*PITCH+SPARE,HD),f32),pltpu.VMEM((U2*T+SPARE,HD),f32),pltpu.VMEM((N*PITCH+SPARE,HD),f32),pltpu.VMEM((U2,KC,HD),bf),pltpu.VMEM((U2,KC,HD),bf)]),
       out_shape=jax.ShapeDtypeStruct((16,3,216,HD),bf),
       compiler_params=pltpu.CompilerParams(vmem_limit_bytes=60*1024*1024),
       cost_estimate=COST,name="attend_grad")(order,neigh,turn,g,qp,kp,vp,o,rinv,e)

time: 211 us -> 211 us (level)
  transfers between devices with their start and end apart: 34 -> 34, of which waited for: 12 -> 12; matrix products, arithmetic and copies ran while one was open for 17% -> 17% of each run, Pallas kernels for 27% -> 26%
where the time goes in v5:
time: 211 us; the launch traced here: 210 us
  starting transfers between devices  61.6 us (29%)
  Pallas kernels  55.5 us (26%)
  waiting for transfers between devices  52.4 us (25%)
  local copies, waits for them, and re-layouts  16.1 us (8%)
  other arithmetic  13.6 us (6%)
  matrix products  9.45 us (4%)
    ppermute x21, waiting for transfers between devices, shift(): lax.ppermute(value, axis, [(i, (i + step) % size) for i in range(size)])  47.5 us
    pallas_call x1, Pallas kernels, run_k2(): pl.pallas_call(k2, grid_spec=pltpu.PrefetchScalarGridSpec(num_scalar_pref...  30 us
    ppermute x21, starting transfers between devices, shift(): lax.ppermute(value, axis, [(i, (i + step) % size) for i in range(size)])  27.3 us
    pallas_call x1, Pallas kernels, run_k1(): pl.pallas_call(k1, grid_spec=pltpu.PrefetchScalarGridSpec(num_scalar_pref...  25.5 us
    ppermute x6, starting transfers between devices, along_z(): lax.ppermute(value, ('zl', 'zh'), [(i, i ^ flip) for i in range(4)])  9.84 us
    select_n x4, other arithmetic, of_chip(): jnp.where(core == 0, mine, theirs)  6.15 us
    all_to_all x1, starting transfers between devices, local(): lax.all_to_all(att.reshape(8, 432, HD), CHIPS, split_axis=0, concat_axis=...  5.69 us
    all_to_all x1, starting transfers between devices, local(): grads = lax.all_to_all(grads, SEQ, split_axis=0, concat_axis=0, tiled=True)  5.61 us
  transfers between devices with their start and end apart: 34, of which 12 were waited for; matrix products, arithmetic and copies ran while one was open for 17% of the time, Pallas kernels for 26%

profile of v5, /device:TPU:0, one launch (start us, length us, event | category | flops | bytes accessed | tf_op | source)
XLA Modules:
  0.0 209.7 jit_solution(11897610933440119963)
XLA Ops:
  0.7 2.1 collective-permute-start.2
  2.7 2.5 %collective-permute-start.3 = (bf16[16,2048]{1,0:T(8,128)(2,1)}, bf16[16,2048]{1,0:T(8,128)(2,1)S(1)}, u32[]{:S(2)}, u32[]{:S(2)}) collective-permute-start(bf16[16,2048]{1,0:T(8,128)(2,1)} %param.10), channel_id=1, source_target_pairs={{0,17},{1,16},{16,1},{17,0},{2,19},{3,18},{18,3},{19,2},{4,21},{5,... | collective-permute-start | bytes 196616 | tf_op jit(solution)/shard_map/ppermute | solution.py:240
  6.3 3.2 %collective-permute-start.5 = (bf16[16,2048]{1,0:T(8,128)(2,1)}, bf16[16,2048]{1,0:T(8,128)(2,1)S(1)}, u32[]{:S(2)}, u32[]{:S(2)}) collective-permute-start(bf16[16,2048]{1,0:T(8,128)(2,1)} %param.10), channel_id=1, source_target_pairs={{0,64},{32,96},{64,0},{96,32},{1,65},{33,97},{65,1},{97,33},{2,66}... | collective-permute-start | bytes 196616 | tf_op jit(solution)/shard_map/ppermute | solution.py:222
  9.5 1.3 copy.36
  11.9 1.7 pad_maximum_fusion.1
  13.9 2.5 %collective-permute-start.6 = (bf16[16,2048]{1,0:T(8,128)(2,1)S(1)}, bf16[16,2048]{1,0:T(8,128)(2,1)S(1)}, u32[]{:S(2)}, u32[]{:S(2)}) collective-permute-start(bf16[16,2048]{1,0:T(8,128)(2,1)S(1)} %collective-permute-done.5), channel_id=1, source_target_pairs={{0,1},{1,0},{16,17},{17,16},{2,3},{3,2},{18,19},{19,18},{4,5},{5,4... | collective-permute-start | bytes 196616 | tf_op jit(solution)/shard_map/ppermute | solution.py:240
  16.4 1.4 collective-permute-start.4
  20.3 2.5 %collective-permute-done.7 = bf16[16,2048]{1,0:T(8,128)(2,1)S(1)} collective-permute-done((bf16[16,2048]{1,0:T(8,128)(2,1)S(1)}, bf16[16,2048]{1,0:T(8,128)(2,1)S(1)}, u32[]{:S(2)}, u32[]{:S(2)}) %collective-permute-start.7) | collective-permute-done | bytes 65568 | tf_op jit(solution)/shard_map/ppermute | solution.py:240
  22.8 2.2 %collective-permute-done.8 = bf16[16,2048]{1,0:T(8,128)(2,1)S(1)} collective-permute-done((bf16[16,2048]{1,0:T(8,128)(2,1)S(1)}, bf16[16,2048]{1,0:T(8,128)(2,1)S(1)}, u32[]{:S(2)}, u32[]{:S(2)}) %collective-permute-start.8) | collective-permute-done | bytes 65568 | tf_op jit(solution)/shard_map/ppermute | solution.py:240
  25.7 2.8 %collective-permute-start.10 = (bf16[8,32,2048]{2,1,0:T(8,128)(2,1)S(1)}, bf16[8,32,2048]{2,1,0:T(8,128)(2,1)S(1)}, u32[]{:S(2)}, u32[]{:S(2)}) collective-permute-start(bf16[8,32,2048]{2,1,0:T(8,128)(2,1)S(1)} %bitcast.127), channel_id=1, source_target_pairs={{0,6},{2,0},{4,2},{6,4},{1,7},{3,1},{5,3},{7,5},{8,14},{10,8},{12,... | collective-permute-start | bytes 3145736 | tf_op jit(solution)/shard_map/ppermute | solution.py:222
  28.6 4.5 %all-to-all-start = ((bf16[16,3,216,128]{3,2,1,0:T(8,128)(2,1)}), bf16[16,3,216,128]{3,2,1,0:T(8,128)(2,1)}, u32[]{:S(2)}, u32[]{:S(2)}) async-start(bf16[16,3,216,128]{3,2,1,0:T(8,128)(2,1)} %pad_maximum_fusion.1), calls=%async_computation | async-start | bytes 5308416 | tf_op jit(solution)/shard_map/all_to_all | solution.py:288
  34.1 14.6 %collective-permute-done.10 = bf16[8,32,2048]{2,1,0:T(8,128)(2,1)S(1)} collective-permute-done((bf16[8,32,2048]{2,1,0:T(8,128)(2,1)S(1)}, bf16[8,32,2048]{2,1,0:T(8,128)(2,1)S(1)}, u32[]{:S(2)}, u32[]{:S(2)}) %collective-permute-start.10) | collective-permute-done | bytes 1048608 | tf_op jit(solution)/shard_map/ppermute | solution.py:222
  48.8 3.0 %collective-permute-start.11 = (bf16[4,32,2048]{2,1,0:T(8,128)(2,1)S(1)}, bf16[4,32,2048]{2,1,0:T(8,128)(2,1)S(1)}, u32[]{:S(2)}, u32[]{:S(2)}) collective-permute-start(bf16[4,32,2048]{2,1,0:T(8,128)(2,1)S(1)} %slice.40), channel_id=1, source_target_pairs={{0,6},{2,0},{4,2},{6,4},{1,7},{3,1},{5,3},{7,5},{8,14},{10,8},{12,... | collective-permute-start | bytes 1572872 | tf_op jit(solution)/shard_map/ppermute | solution.py:222
  51.8 1.1 slice.41
  53.0 1.4 broadcast_select_fusion.7
  54.4 4.7 %collective-permute-done.11 = bf16[4,32,2048]{2,1,0:T(8,128)(2,1)S(1)} collective-permute-done((bf16[4,32,2048]{2,1,0:T(8,128)(2,1)S(1)}, bf16[4,32,2048]{2,1,0:T(8,128)(2,1)S(1)}, u32[]{:S(2)}, u32[]{:S(2)}) %collective-permute-start.11) | collective-permute-done | bytes 524320 | tf_op jit(solution)/shard_map/ppermute | solution.py:222
  59.1 4.4 %collective-permute-done.13 = bf16[4,32,2048]{2,1,0:T(8,128)(2,1)S(1)} collective-permute-done((bf16[4,32,2048]{2,1,0:T(8,128)(2,1)S(1)}, bf16[4,32,2048]{2,1,0:T(8,128)(2,1)S(1)}, u32[]{:S(2)}, u32[]{:S(2)}) %collective-permute-start.13) | collective-permute-done | bytes 524320 | tf_op jit(solution)/shard_map/ppermute | solution.py:222
  63.4 1.6 pad_maximum_fusion
  65.0 2.1 fusion.15
  67.1 1.2 copy.43
  68.3 4.6 %all-to-all-start.1 = ((bf16[8,432,128]{2,1,0:T(8,128)(2,1)}), bf16[8,432,128]{2,1,0:T(8,128)(2,1)S(1)}, u32[]{:S(2)}, u32[]{:S(2)}) async-start(bf16[8,432,128]{2,1,0:T(8,128)(2,1)} %bitcast.120), calls=%async_computation.1 | async-start | bytes 1769472 | tf_op jit(solution)/shard_map/all_to_all | solution.py:302
  72.8 25.5 %attend.1 = (bf16[16,216,128]{2,1,0:T(8,128)(2,1)}, bf16[3456,128]{1,0:T(8,128)(2,1)}, bf16[3456,128]{1,0:T(8,128)(2,1)}, bf16[3456,128]{1,0:T(8,128)(2,1)}, f32...) custom-call(s32[3456]{0:T(1024)} %order_ref.3, s32[162]{0:T(256)} %reshape.283.neigh_ref, ...), custom_call_target="tpu_custom_call" | custom-call | flops 30000001024 | bytes 20000000 | tf_op jit(solution)/shard_map/attend/pallas_call | solution.py:104
  99.2 3.9 %collective-permute-start.15 = (bf16[216,2048]{1,0:T(8,128)(2,1)S(1)}, bf16[216,2048]{1,0:T(8,128)(2,1)}, u32[]{:S(2)}, u32[]{:S(2)}) collective-permute-start(bf16[216,2048]{1,0:T(8,128)(2,1)S(1)} %bitcast.142), channel_id=1, source_target_pairs={{0,4},{2,6},{4,0},{6,2},{1,5},{3,7},{5,1},{7,3},{8,12},{10,14},{12... | collective-permute-start | bytes 2654216 | tf_op jit(solution)/shard_map/ppermute | solution.py:222
  103.4 5.7 %all-to-all-start.2 = ((bf16[8,432,128]{2,1,0:T(8,128)(2,1)}), bf16[8,432,128]{2,1,0:T(8,128)(2,1)S(1)}, u32[]{:S(2)}, u32[]{:S(2)}) async-start(bf16[8,432,128]{2,1,0:T(8,128)(2,1)} %bitcast.139), calls=%async_computation.2 | async-start | bytes 1769472 | tf_op jit(solution)/shard_map/all_to_all | solution.py:307
  109.0 30.0 %attend_grad.1 = bf16[16,3,216,128]{3,2,1,0:T(8,128)(2,1)} custom-call(s32[3456]{0:T(1024)} %order_ref.3, s32[162]{0:T(256)} %reshape.283.neigh_ref, s32[1]{0:T(128)} %bitcast.turn_ref, bf16[16,216,128]{2,1,0:T(8,128)(2,1)} %bitcast.138, bf16[3456,128]{1,0:T(8,128)(2,1)} %get-tuple-element.37.qp_ref, bf16[3456,128]{1,0:T(8,128)(2,1)} %get-tuple-element.38.kp_ref, ...), custom_call_target="tpu_custom_call" | custom-call | flops 30000001024 | bytes 20000000 | tf_op jit(solution)/shard_map/attend_grad/pallas_call | solution.py:170
  140.0 1.7 collective-permute-done.15
  142.3 5.6 %all-to-all-start.3 = ((bf16[16,3,216,128]{3,2,1,0:T(8,128)(2,1)}), bf16[16,3,216,128]{3,2,1,0:T(8,128)(2,1)S(1)}, u32[]{:S(2)}, u32[]{:S(2)}) async-start(bf16[16,3,216,128]{3,2,1,0:T(8,128)(2,1)} %attend_grad.1), calls=%async_computation.3 | async-start | bytes 5308416 | tf_op jit(solution)/shard_map/all_to_all | solution.py:311
  147.9 2.3 %copy.29 = bf16[432,1024]{0,1:T(8,128)(2,1)} copy(bf16[432,1024]{1,0:T(8,128)(2,1)} %copy_bitcast_fusion) | data formatting | bytes 1769472 | tf_op jit(solution)/shard_map/optimization_barrier | solution.py:314
  150.1 4.4 %fusion.31 = f32[432,2048]{1,0:T(8,128)S(1)} fusion(bf16[432,1024]{1,0:T(8,128)(2,1)} %copy_bitcast_fusion, bf16[1024,2048]{1,0:T(8,128)(2,1)} %bitcast.125), kind=kOutput, calls=%fused_computation.87 | convolution fusion | flops 1811939328 | bytes 8617984 | tf_op jit(solution)/shard_map/dot_general | solution.py:323
  154.6 1.6 broadcast_select_fusion.5
  157.3 2.8 %collective-permute-start.20 = (bf16[432,256]{0,1:T(8,128)(2,1)S(1)}, bf16[432,256]{0,1:T(8,128)(2,1)S(1)}, u32[]{:S(2)}, u32[]{:S(2)}) collective-permute-start(bf16[432,256]{0,1:T(8,128)(2,1)S(1)} %bitcast.145), channel_id=1, source_target_pairs={{0,4},{2,6},{4,0},{6,2},{1,5},{3,7},{5,1},{7,3},{8,12},{10,14},{12... | collective-permute-start | bytes 663560 | tf_op jit(solution)/shard_map/ppermute | solution.py:222
  161.1 1.6 broadcast_select_fusion.3
  162.6 1.6 broadcast_select_fusion.1
  164.2 2.3 %collective-permute-done.19 = bf16[432,256]{0,1:T(8,128)(2,1)S(1)} collective-permute-done((bf16[432,256]{0,1:T(8,128)(2,1)S(1)}, bf16[432,256]{0,1:T(8,128)(2,1)S(1)}, u32[]{:S(2)}, u32[]{:S(2)}) %collective-permute-start.19) | collective-permute-done | bytes 221216 | tf_op jit(solution)/shard_map/ppermute | solution.py:222
  167.2 5.2 %collective-permute-done.20 = bf16[432,256]{0,1:T(8,128)(2,1)S(1)} collective-permute-done((bf16[432,256]{0,1:T(8,128)(2,1)S(1)}, bf16[432,256]{0,1:T(8,128)(2,1)S(1)}, u32[]{:S(2)}, u32[]{:S(2)}) %collective-permute-start.20) | collective-permute-done | bytes 221216 | tf_op jit(solution)/shard_map/ppermute | solution.py:222
  175.2 1.7 collective-permute-start.24
  176.9 2.7 %collective-permute-start.25 = (bf16[4,16,2048]{2,1,0:T(8,128)(2,1)S(1)}, bf16[4,16,2048]{2,1,0:T(8,128)(2,1)S(1)}, u32[]{:S(2)}, u32[]{:S(2)}) collective-permute-start(bf16[4,16,2048]{2,1,0:T(8,128)(2,1)S(1)} %get-tuple-element.67), channel_id=1, source_target_pairs={{0,64},{32,96},{64,0},{96,32},{1,65},{33,97},{65,1},{97,33},{2,66}... | collective-permute-start | bytes 786440 | tf_op jit(solution)/shard_map/ppermute | solution.py:222
  179.6 1.5 collective-permute-start.26
  181.0 1.1 fusion.16
  182.2 9.1 %collective-permute-done.24 = bf16[4,16,2048]{2,1,0:T(8,128)(2,1)S(1)} collective-permute-done((bf16[4,16,2048]{2,1,0:T(8,128)(2,1)S(1)}, bf16[4,16,2048]{2,1,0:T(8,128)(2,1)S(1)}, u32[]{:S(2)}, u32[]{:S(2)}) %collective-permute-start.24) | collective-permute-done | bytes 262176 | tf_op jit(solution)/shard_map/ppermute | solution.py:222
  191.2 5.2 %collective-permute-done.25 = bf16[4,16,2048]{2,1,0:T(8,128)(2,1)S(1)} collective-permute-done((bf16[4,16,2048]{2,1,0:T(8,128)(2,1)S(1)}, bf16[4,16,2048]{2,1,0:T(8,128)(2,1)S(1)}, u32[]{:S(2)}, u32[]{:S(2)}) %collective-permute-start.25) | collective-permute-done | bytes 262176 | tf_op jit(solution)/shard_map/ppermute | solution.py:222
  196.5 1.1 fusion.19
  199.4 3.0 %collective-permute-start.29 = (bf16[16,2048]{1,0:T(8,128)(2,1)}, bf16[16,2048]{1,0:T(8,128)(2,1)}, u32[]{:S(2)}, u32[]{:S(2)}) collective-permute-start(bf16[16,2048]{1,0:T(8,128)(2,1)} %get-tuple-element.74), channel_id=1, source_target_pairs={{0,17},{1,16},{16,1},{17,0},{2,19},{3,18},{18,3},{19,2},{4,21},{5,... | collective-permute-start | bytes 196616 | tf_op jit(solution)/shard_map/ppermute | solution.py:272
  202.4 1.4 slice_bitcast_fusion
  203.9 1.3 reshape.292
  205.3 1.3 reshape.293
  206.8 1.3 reshape.294
  208.1 1.6 fusion.24
  (108 shorter events, 16.7 us)
Async XLA Ops:
  0.6 10.2 %copy-start.8 = (bf16[1,216,2048]{2,1,0:T(8,128)(2,1)S(1)}, bf16[1,216,2048]{2,1,0:T(8,128)(2,1)}, u32[]{:S(2)}) copy-start(bf16[1,216,2048]{2,1,0:T(8,128)(2,1)} %param.9) | copy-start | bytes 2654212
  0.6 10.4 %copy-start.9 = (bf16[1,216,2048]{2,1,0:T(8,128)(2,1)S(1)}, bf16[1,216,2048]{2,1,0:T(8,128)(2,1)}, u32[]{:S(2)}) copy-start(bf16[1,216,2048]{2,1,0:T(8,128)(2,1)} %param.7) | copy-start | bytes 2654212
  0.7 13.1 %collective-permute-start.2 = (bf16[16,2048]{1,0:T(8,128)(2,1)}, bf16[16,2048]{1,0:T(8,128)(2,1)S(1)}, u32[]{:S(2)}, u32[]{:S(2)}) collective-permute-start(bf16[16,2048]{1,0:T(8,128)(2,1)} %param.10), channel_id=1, source_target_pairs={{0,16},{1,17},{16,0},{17,1},{2,18},{3,19},{18,2},{19,3},{4,20},{5,... | collective-permute-start | bytes 196616 | tf_op jit(solution)/shard_map/ppermute | solution.py:240
  2.7 11.0 %collective-permute-start.3 = (bf16[16,2048]{1,0:T(8,128)(2,1)}, bf16[16,2048]{1,0:T(8,128)(2,1)S(1)}, u32[]{:S(2)}, u32[]{:S(2)}) collective-permute-start(bf16[16,2048]{1,0:T(8,128)(2,1)} %param.10), channel_id=1, source_target_pairs={{0,17},{1,16},{16,1},{17,0},{2,19},{3,18},{18,3},{19,2},{4,21},{5,... | collective-permute-start | bytes 196616 | tf_op jit(solution)/shard_map/ppermute | solution.py:240
  5.3 8.4 %collective-permute-start.1 = (bf16[16,2048]{1,0:T(8,128)(2,1)}, bf16[16,2048]{1,0:T(8,128)(2,1)S(1)}, u32[]{:S(2)}, u32[]{:S(2)}) collective-permute-start(bf16[16,2048]{1,0:T(8,128)(2,1)} %param.10), channel_id=1, source_target_pairs={{0,1},{1,0},{16,17},{17,16},{2,3},{3,2},{18,19},{19,18},{4,5},{5,4... | collective-permute-start | bytes 196616 | tf_op jit(solution)/shard_map/ppermute | solution.py:240
  6.3 7.5 %collective-permute-start.5 = (bf16[16,2048]{1,0:T(8,128)(2,1)}, bf16[16,2048]{1,0:T(8,128)(2,1)S(1)}, u32[]{:S(2)}, u32[]{:S(2)}) collective-permute-start(bf16[16,2048]{1,0:T(8,128)(2,1)} %param.10), channel_id=1, source_target_pairs={{0,64},{32,96},{64,0},{96,32},{1,65},{33,97},{65,1},{97,33},{2,66}... | collective-permute-start | bytes 196616 | tf_op jit(solution)/shard_map/ppermute | solution.py:222
  11.9 1.8 copy-start.14
  13.9 6.4 %collective-permute-start.6 = (bf16[16,2048]{1,0:T(8,128)(2,1)S(1)}, bf16[16,2048]{1,0:T(8,128)(2,1)S(1)}, u32[]{:S(2)}, u32[]{:S(2)}) collective-permute-start(bf16[16,2048]{1,0:T(8,128)(2,1)S(1)} %collective-permute-done.5), channel_id=1, source_target_pairs={{0,1},{1,0},{16,17},{17,16},{2,3},{3,2},{18,19},{19,18},{4,5},{5,4... | collective-permute-start | bytes 196616 | tf_op jit(solution)/shard_map/ppermute | solution.py:240
  16.4 8.7 %collective-permute-start.4 = (bf16[2,32,2048]{2,1,0:T(8,128)(2,1)S(1)}, bf16[2,32,2048]{2,1,0:T(8,128)(2,1)S(1)}, u32[]{:S(2)}, u32[]{:S(2)}) collective-permute-start(bf16[2,32,2048]{2,1,0:T(8,128)(2,1)S(1)} %pad_maximum_fusion.5), channel_id=1, source_target_pairs={{0,96},{32,0},{64,32},{96,64},{1,97},{33,1},{65,33},{97,65},{2,98}... | collective-permute-start | bytes 786440 | tf_op jit(solution)/shard_map/ppermute | solution.py:222
  17.9 7.6 %collective-permute-start.9 = (bf16[2,32,2048]{2,1,0:T(8,128)(2,1)S(1)}, bf16[2,32,2048]{2,1,0:T(8,128)(2,1)S(1)}, u32[]{:S(2)}, u32[]{:S(2)}) collective-permute-start(bf16[2,32,2048]{2,1,0:T(8,128)(2,1)S(1)} %pad_maximum_fusion.5), channel_id=1, source_target_pairs={{0,32},{32,64},{64,96},{96,0},{1,33},{33,65},{65,97},{97,1},{2,34}... | collective-permute-start | bytes 786440 | tf_op jit(solution)/shard_map/ppermute | solution.py:222
  18.5 4.3 %collective-permute-start.7 = (bf16[16,2048]{1,0:T(8,128)(2,1)S(1)}, bf16[16,2048]{1,0:T(8,128)(2,1)S(1)}, u32[]{:S(2)}, u32[]{:S(2)}) collective-permute-start(bf16[16,2048]{1,0:T(8,128)(2,1)S(1)} %collective-permute-done.5), channel_id=1, source_target_pairs={{0,16},{1,17},{16,0},{17,1},{2,18},{3,19},{18,2},{19,3},{4,20},{5,... | collective-permute-start | bytes 196616 | tf_op jit(solution)/shard_map/ppermute | solution.py:240
  19.5 5.5 %collective-permute-start.8 = (bf16[16,2048]{1,0:T(8,128)(2,1)S(1)}, bf16[16,2048]{1,0:T(8,128)(2,1)S(1)}, u32[]{:S(2)}, u32[]{:S(2)}) collective-permute-start(bf16[16,2048]{1,0:T(8,128)(2,1)S(1)} %collective-permute-done.5), channel_id=1, source_target_pairs={{0,17},{1,16},{16,1},{17,0},{2,19},{3,18},{18,3},{19,2},{4,21},{5,... | collective-permute-start | bytes 196616 | tf_op jit(solution)/shard_map/ppermute | solution.py:240
  25.7 7.3 %copy-start.11 = (bf16[1,216,2048]{2,1,0:T(8,128)(2,1)S(1)}, bf16[1,216,2048]{2,1,0:T(8,128)(2,1)}, u32[]{:S(2)}) copy-start(bf16[1,216,2048]{2,1,0:T(8,128)(2,1)} %param.11) | copy-start | bytes 2654212
  25.7 7.6 %copy-start.15 = (s32[18,9]{0,1:T(8,128)S(1)}, s32[18,9]{0,1:T(8,128)}, u32[]{:S(2)}) copy-start(s32[18,9]{0,1:T(8,128)} %param.12) | copy-start | bytes 1948
  25.7 23.0 %collective-permute-start.10 = (bf16[8,32,2048]{2,1,0:T(8,128)(2,1)S(1)}, bf16[8,32,2048]{2,1,0:T(8,128)(2,1)S(1)}, u32[]{:S(2)}, u32[]{:S(2)}) collective-permute-start(bf16[8,32,2048]{2,1,0:T(8,128)(2,1)S(1)} %bitcast.127), channel_id=1, source_target_pairs={{0,6},{2,0},{4,2},{6,4},{1,7},{3,1},{5,3},{7,5},{8,14},{10,8},{12,... | collective-permute-start | bytes 3145736 | tf_op jit(solution)/shard_map/ppermute | solution.py:222
  28.6 23.2 %collective-permute-start.12 = (bf16[8,32,2048]{2,1,0:T(8,128)(2,1)S(1)}, bf16[8,32,2048]{2,1,0:T(8,128)(2,1)}, u32[]{:S(2)}, u32[]{:S(2)}) collective-permute-start(bf16[8,32,2048]{2,1,0:T(8,128)(2,1)S(1)} %bitcast.128), channel_id=1, source_target_pairs={{0,2},{2,4},{4,6},{6,0},{1,3},{3,5},{5,7},{7,1},{8,10},{10,12},{12... | collective-permute-start | bytes 3145736 | tf_op jit(solution)/shard_map/ppermute | solution.py:222
  28.6 39.7 %all-to-all-start = ((bf16[16,3,216,128]{3,2,1,0:T(8,128)(2,1)}), bf16[16,3,216,128]{3,2,1,0:T(8,128)(2,1)}, u32[]{:S(2)}, u32[]{:S(2)}) async-start(bf16[16,3,216,128]{3,2,1,0:T(8,128)(2,1)} %pad_maximum_fusion.1), calls=%async_computation | async-start | bytes 5308416 | tf_op jit(solution)/shard_map/all_to_all | solution.py:288
  33.0 19.9 %collective-permute-start = (bf16[216,2048]{1,0:T(8,128)(2,1)S(1)}, bf16[216,2048]{1,0:T(8,128)(2,1)}, u32[]{:S(2)}, u32[]{:S(2)}) collective-permute-start(bf16[216,2048]{1,0:T(8,128)(2,1)S(1)} %bitcast.140), channel_id=1, source_target_pairs={{0,8},{8,0},{1,9},{9,1},{2,10},{10,2},{3,11},{11,3},{4,12},{12,4},... | collective-permute-start | bytes 2654216 | tf_op jit(solution)/shard_map/ppermute | solution.py:222
  34.1 18.9 %copy-start.12 = (bf16[1,216,2048]{2,1,0:T(8,128)(2,1)S(1)}, bf16[1,216,2048]{2,1,0:T(8,128)(2,1)}, u32[]{:S(2)}) copy-start(bf16[1,216,2048]{2,1,0:T(8,128)(2,1)} %param.11) | copy-start | bytes 2654212
  48.8 10.3 %collective-permute-start.11 = (bf16[4,32,2048]{2,1,0:T(8,128)(2,1)S(1)}, bf16[4,32,2048]{2,1,0:T(8,128)(2,1)S(1)}, u32[]{:S(2)}, u32[]{:S(2)}) collective-permute-start(bf16[4,32,2048]{2,1,0:T(8,128)(2,1)S(1)} %slice.40), channel_id=1, source_target_pairs={{0,6},{2,0},{4,2},{6,4},{1,7},{3,1},{5,3},{7,5},{8,14},{10,8},{12,... | collective-permute-start | bytes 1572872 | tf_op jit(solution)/shard_map/ppermute | solution.py:222
  52.9 10.6 %collective-permute-start.13 = (bf16[4,32,2048]{2,1,0:T(8,128)(2,1)S(1)}, bf16[4,32,2048]{2,1,0:T(8,128)(2,1)S(1)}, u32[]{:S(2)}, u32[]{:S(2)}) collective-permute-start(bf16[4,32,2048]{2,1,0:T(8,128)(2,1)S(1)} %slice.41), channel_id=1, source_target_pairs={{0,2},{2,4},{4,6},{6,0},{1,3},{3,5},{5,7},{7,1},{8,10},{10,12},{12... | collective-permute-start | bytes 1572872 | tf_op jit(solution)/shard_map/ppermute | solution.py:222
  54.4 10.7 %copy-start.3 = (bf16[216,2048]{1,0:T(8,128)(2,1)}, bf16[216,2048]{1,0:T(8,128)(2,1)S(1)}, u32[]{:S(2)}) copy-start(bf16[216,2048]{1,0:T(8,128)(2,1)S(1)} %get-tuple-element.65) | copy-start | bytes 2654212
  65.0 2.1 %copy-start.1 = (bf16[8,128,2048]{2,1,0:T(8,128)(2,1)}, bf16[8,128,2048]{2,1,0:T(8,128)(2,1)S(1)}, u32[]{:S(2)}) copy-start(bf16[8,128,2048]{2,1,0:T(8,128)(2,1)S(1)} %pad_maximum_fusion) | copy-start | bytes 12582916
  68.3 30.1 %all-to-all-start.1 = ((bf16[8,432,128]{2,1,0:T(8,128)(2,1)}), bf16[8,432,128]{2,1,0:T(8,128)(2,1)S(1)}, u32[]{:S(2)}, u32[]{:S(2)}) async-start(bf16[8,432,128]{2,1,0:T(8,128)(2,1)} %bitcast.120), calls=%async_computation.1 | async-start | bytes 1769472 | tf_op jit(solution)/shard_map/all_to_all | solution.py:302
  72.8 25.5 %copy-start.13 = (bf16[1,216,2048]{2,1,0:T(8,128)(2,1)S(1)}, bf16[1,216,2048]{2,1,0:T(8,128)(2,1)}, u32[]{:S(2)}) copy-start(bf16[1,216,2048]{2,1,0:T(8,128)(2,1)} %param.11) | copy-start | bytes 2654212
  98.4 10.7 %copy-start.10 = (bf16[8,432,128]{2,1,0:T(8,128)(2,1)}, bf16[8,432,128]{2,1,0:T(8,128)(2,1)S(1)}, u32[]{:S(2)}) copy-start(bf16[8,432,128]{2,1,0:T(8,128)(2,1)S(1)} %all-to-all-done.1) | copy-start | bytes 2654212
  98.4 41.7 %collective-permute-start.14 = (bf16[216,2048]{1,0:T(8,128)(2,1)S(1)}, bf16[216,2048]{1,0:T(8,128)(2,1)}, u32[]{:S(2)}, u32[]{:S(2)}) collective-permute-start(bf16[216,2048]{1,0:T(8,128)(2,1)S(1)} %bitcast.141), channel_id=1, source_target_pairs={{0,2},{2,4},{4,6},{6,0},{1,3},{3,5},{5,7},{7,1},{8,10},{10,12},{12... | collective-permute-start | bytes 2654216 | tf_op jit(solution)/shard_map/ppermute | solution.py:222
  99.2 42.6 %collective-permute-start.15 = (bf16[216,2048]{1,0:T(8,128)(2,1)S(1)}, bf16[216,2048]{1,0:T(8,128)(2,1)}, u32[]{:S(2)}, u32[]{:S(2)}) collective-permute-start(bf16[216,2048]{1,0:T(8,128)(2,1)S(1)} %bitcast.142), channel_id=1, source_target_pairs={{0,4},{2,6},{4,0},{6,2},{1,5},{3,7},{5,1},{7,3},{8,12},{10,14},{12... | collective-permute-start | bytes 2654216 | tf_op jit(solution)/shard_map/ppermute | solution.py:222
  103.1 38.6 %collective-permute-start.16 = (bf16[216,2048]{1,0:T(8,128)(2,1)S(1)}, bf16[216,2048]{1,0:T(8,128)(2,1)}, u32[]{:S(2)}, u32[]{:S(2)}) collective-permute-start(bf16[216,2048]{1,0:T(8,128)(2,1)S(1)} %bitcast.143), channel_id=1, source_target_pairs={{0,6},{2,0},{4,2},{6,4},{1,7},{3,1},{5,3},{7,5},{8,14},{10,8},{12,... | collective-permute-start | bytes 2654216 | tf_op jit(solution)/shard_map/ppermute | solution.py:222
  103.4 35.7 %all-to-all-start.2 = ((bf16[8,432,128]{2,1,0:T(8,128)(2,1)}), bf16[8,432,128]{2,1,0:T(8,128)(2,1)S(1)}, u32[]{:S(2)}, u32[]{:S(2)}) async-start(bf16[8,432,128]{2,1,0:T(8,128)(2,1)} %bitcast.139), calls=%async_computation.2 | async-start | bytes 1769472 | tf_op jit(solution)/shard_map/all_to_all | solution.py:307
  141.7 6.1 %collective-permute-start.17 = (bf16[216,2048]{1,0:T(8,128)(2,1)}, bf16[216,2048]{1,0:T(8,128)(2,1)}, u32[]{:S(2)}, u32[]{:S(2)}) collective-permute-start(bf16[216,2048]{1,0:T(8,128)(2,1)} %collective-permute-done.14), channel_id=1, source_target_pairs={{0,8},{8,0},{1,9},{9,1},{2,10},{10,2},{3,11},{11,3},{4,12},{12,4},... | collective-permute-start | bytes 2654216 | tf_op jit(solution)/shard_map/ppermute | solution.py:222
  141.8 19.0 %collective-permute-start.21 = (bf16[216,2048]{1,0:T(8,128)(2,1)}, bf16[216,2048]{1,0:T(8,128)(2,1)}, u32[]{:S(2)}, u32[]{:S(2)}) collective-permute-start(bf16[216,2048]{1,0:T(8,128)(2,1)} %collective-permute-done.15), channel_id=1, source_target_pairs={{0,8},{8,0},{1,9},{9,1},{2,10},{10,2},{3,11},{11,3},{4,12},{12,4},... | collective-permute-start | bytes 2654216 | tf_op jit(solution)/shard_map/ppermute | solution.py:222
  142.3 20.4 %collective-permute-start.23 = (bf16[216,2048]{1,0:T(8,128)(2,1)}, bf16[216,2048]{1,0:T(8,128)(2,1)}, u32[]{:S(2)}, u32[]{:S(2)}) collective-permute-start(bf16[216,2048]{1,0:T(8,128)(2,1)} %collective-permute-done.16), channel_id=1, source_target_pairs={{0,8},{8,0},{1,9},{9,1},{2,10},{10,2},{3,11},{11,3},{4,12},{12,4},... | collective-permute-start | bytes 2654216 | tf_op jit(solution)/shard_map/ppermute | solution.py:222
  142.3 54.2 %all-to-all-start.3 = ((bf16[16,3,216,128]{3,2,1,0:T(8,128)(2,1)}), bf16[16,3,216,128]{3,2,1,0:T(8,128)(2,1)S(1)}, u32[]{:S(2)}, u32[]{:S(2)}) async-start(bf16[16,3,216,128]{3,2,1,0:T(8,128)(2,1)} %attend_grad.1), calls=%async_computation.3 | async-start | bytes 5308416 | tf_op jit(solution)/shard_map/all_to_all | solution.py:311
  154.6 1.8 copy-start.2
  156.5 10.0 %collective-permute-start.19 = (bf16[432,256]{0,1:T(8,128)(2,1)S(1)}, bf16[432,256]{0,1:T(8,128)(2,1)S(1)}, u32[]{:S(2)}, u32[]{:S(2)}) collective-permute-start(bf16[432,256]{0,1:T(8,128)(2,1)S(1)} %bitcast.146), channel_id=1, source_target_pairs={{0,2},{2,4},{4,6},{6,0},{1,3},{3,5},{5,7},{7,1},{8,10},{10,12},{12... | collective-permute-start | bytes 663560 | tf_op jit(solution)/shard_map/ppermute | solution.py:222
  157.3 15.0 %collective-permute-start.20 = (bf16[432,256]{0,1:T(8,128)(2,1)S(1)}, bf16[432,256]{0,1:T(8,128)(2,1)S(1)}, u32[]{:S(2)}, u32[]{:S(2)}) collective-permute-start(bf16[432,256]{0,1:T(8,128)(2,1)S(1)} %bitcast.145), channel_id=1, source_target_pairs={{0,4},{2,6},{4,0},{6,2},{1,5},{3,7},{5,1},{7,3},{8,12},{10,14},{12... | collective-permute-start | bytes 663560 | tf_op jit(solution)/shard_map/ppermute | solution.py:222
  160.2 12.9 %collective-permute-start.22 = (bf16[432,256]{0,1:T(8,128)(2,1)S(1)}, bf16[432,256]{0,1:T(8,128)(2,1)S(1)}, u32[]{:S(2)}, u32[]{:S(2)}) collective-permute-start(bf16[432,256]{0,1:T(8,128)(2,1)S(1)} %bitcast.144), channel_id=1, source_target_pairs={{0,6},{2,0},{4,2},{6,4},{1,7},{3,1},{5,3},{7,5},{8,14},{10,8},{12,... | collective-permute-start | bytes 663560 | tf_op jit(solution)/shard_map/ppermute | solution.py:222
  160.8 20.3 %collective-permute-start.18 = (bf16[216,2048]{1,0:T(8,128)(2,1)S(1)}, bf16[216,2048]{1,0:T(8,128)(2,1)S(1)}, u32[]{:S(2)}, u32[]{:S(2)}) collective-permute-start(bf16[216,2048]{1,0:T(8,128)(2,1)S(1)} %dynamic-slice_convert_fusion), channel_id=1, source_target_pairs={{0,8},{8,0},{1,9},{9,1},{2,10},{10,2},{3,11},{11,3},{4,12},{12,4},... | collective-permute-start | bytes 2654216 | tf_op jit(solution)/shard_map/ppermute | solution.py:222
  175.1 7.1 %copy-start = (bf16[256,2048]{1,0:T(8,128)(2,1)}, bf16[256,2048]{1,0:T(8,128)(2,1)S(1)}, u32[]{:S(2)}) copy-start(bf16[256,2048]{1,0:T(8,128)(2,1)S(1)} %fusion.2) | copy-start | bytes 3145732
  175.2 16.1 %collective-permute-start.24 = (bf16[4,16,2048]{2,1,0:T(8,128)(2,1)S(1)}, bf16[4,16,2048]{2,1,0:T(8,128)(2,1)S(1)}, u32[]{:S(2)}, u32[]{:S(2)}) collective-permute-start(bf16[4,16,2048]{2,1,0:T(8,128)(2,1)S(1)} %get-tuple-element.68), channel_id=1, source_target_pairs={{0,32},{32,64},{64,96},{96,0},{1,33},{33,65},{65,97},{97,1},{2,34}... | collective-permute-start | bytes 786440 | tf_op jit(solution)/shard_map/ppermute | solution.py:222
  176.9 19.6 %collective-permute-start.25 = (bf16[4,16,2048]{2,1,0:T(8,128)(2,1)S(1)}, bf16[4,16,2048]{2,1,0:T(8,128)(2,1)S(1)}, u32[]{:S(2)}, u32[]{:S(2)}) collective-permute-start(bf16[4,16,2048]{2,1,0:T(8,128)(2,1)S(1)} %get-tuple-element.67), channel_id=1, source_target_pairs={{0,64},{32,96},{64,0},{96,32},{1,65},{33,97},{65,1},{97,33},{2,66}... | collective-permute-start | bytes 786440 | tf_op jit(solution)/shard_map/ppermute | solution.py:222
  179.6 16.9 %collective-permute-start.26 = (bf16[4,16,2048]{2,1,0:T(8,128)(2,1)S(1)}, bf16[4,16,2048]{2,1,0:T(8,128)(2,1)S(1)}, u32[]{:S(2)}, u32[]{:S(2)}) collective-permute-start(bf16[4,16,2048]{2,1,0:T(8,128)(2,1)S(1)} %get-tuple-element.66), channel_id=1, source_target_pairs={{0,96},{32,0},{64,32},{96,64},{1,97},{33,1},{65,33},{97,65},{2,98}... | collective-permute-start | bytes 786440 | tf_op jit(solution)/shard_map/ppermute | solution.py:222
  197.6 1.8 copy-start.7
  198.3 9.7 %collective-permute-start.27 = (bf16[16,2048]{1,0:T(8,128)(2,1)}, bf16[16,2048]{1,0:T(8,128)(2,1)}, u32[]{:S(2)}, u32[]{:S(2)}) collective-permute-start(bf16[16,2048]{1,0:T(8,128)(2,1)} %get-tuple-element.73), channel_id=1, source_target_pairs={{0,1},{1,0},{16,17},{17,16},{2,3},{3,2},{18,19},{19,18},{4,5},{5,4... | collective-permute-start | bytes 196616 | tf_op jit(solution)/shard_map/ppermute | solution.py:272
  199.4 8.6 %collective-permute-start.28 = (bf16[16,2048]{1,0:T(8,128)(2,1)}, bf16[16,2048]{1,0:T(8,128)(2,1)}, u32[]{:S(2)}, u32[]{:S(2)}) collective-permute-start(bf16[16,2048]{1,0:T(8,128)(2,1)} %get-tuple-element.75), channel_id=1, source_target_pairs={{0,16},{1,17},{16,0},{17,1},{2,18},{3,19},{18,2},{19,3},{4,20},{5,... | collective-permute-start | bytes 196616 | tf_op jit(solution)/shard_map/ppermute | solution.py:272
  199.4 8.6 %collective-permute-start.29 = (bf16[16,2048]{1,0:T(8,128)(2,1)}, bf16[16,2048]{1,0:T(8,128)(2,1)}, u32[]{:S(2)}, u32[]{:S(2)}) collective-permute-start(bf16[16,2048]{1,0:T(8,128)(2,1)} %get-tuple-element.74), channel_id=1, source_target_pairs={{0,17},{1,16},{16,1},{17,0},{2,19},{3,18},{18,3},{19,2},{4,21},{5,... | collective-permute-start | bytes 196616 | tf_op jit(solution)/shard_map/ppermute | solution.py:272
  205.2 1.4 copy-start.5
  (2 other events, 2.6 us)
